TPU v7x, 32 devices: a whole 2x2x4 slice. The times are simulated.
32 devices in a mesh: groups: 2 (over x), gx: 16 (over z, y, core).
Axes of the slice: x: 2, y: 2, z: 4, core: 2. Of those that a mesh axis runs over, the one named last changes fastest.
Arguments:
- velocity: float32 [3, 32, 4, 32, 128], P(None, ('groups', 'gx')), parts along dimension 1, may hold values from -6 to 6
- stress: float32 [6, 32, 4, 32, 128], P(None, ('groups', 'gx')), parts along dimension 1, may hold values from -6 to 6
- memory: float32 [6, 32, 4, 32, 128], P(None, ('groups', 'gx')), parts along dimension 1, may hold values from -4 to 4
- lame_lambda: float32 [32, 4, 32, 128], P(('groups', 'gx')), parts along dimension 0, may hold values from 1.5 to 2.5
- lame_mu: float32 [32, 4, 32, 128], P(('groups', 'gx')), parts along dimension 0, may hold values from 0.1 to 0.5
- buoyancy: float32 [32, 4, 32, 128], P(('groups', 'gx')), parts along dimension 0, may hold values from 0.7 to 1
- decay: float32 [32, 4, 32, 128], P(('groups', 'gx')), parts along dimension 0, may hold values from 0.3 to 0.95
- loss: float32 [32, 4, 32, 128], P(('groups', 'gx')), parts along dimension 0, may hold values from 0.1 to 1
- tile_lambda: bfloat16 [256, 256], P(('groups', 'gx')), parts along dimension 0, may hold values from 3 to 4.5
- tile_mu: bfloat16 [256, 256], P(('groups', 'gx')), parts along dimension 0, may hold values from 1 to 2
- tile_buoy: bfloat16 [256, 256], P(('groups', 'gx')), parts along dimension 0, may hold values from 0.3984375 to 0.59765625
- tile_dest: int32 [256], P(('groups', 'gx')), parts along dimension 0, may hold values from -1 to 15, as said below
- brick_tiles: int32 [32, 64], P(('groups', 'gx')), parts along dimension 0, may hold values from -1 to 127, as said below
- src_index: int32 [512], P(('groups', 'gx')), parts along dimension 0, may hold values from 0 to 16383
- src_wave: float32 [512, 2], P(('groups', 'gx')), parts along dimension 0, may hold values from -6 to 6
Outputs:
- new_velocity: float32 [3, 32, 4, 32, 128], P(None, ('groups', 'gx')), parts along dimension 1
- new_stress: float32 [6, 32, 4, 32, 128], P(None, ('groups', 'gx')), parts along dimension 1
- new_memory: float32 [6, 32, 4, 32, 128], P(None, ('groups', 'gx')), parts along dimension 1
There are 2 independent parts, one for each index of `groups`. A program takes and returns all parts, laid end to end along the dimension named above; each array names one. Nothing has to cross between parts.
Inputs may be any that keep to these rules, and one draw needn't show every extreme that they name: `tile_dest`: the 8 tiles stored on one device name distinct bricks; a brick receives at most 8 tiles, and some brick exactly 8 in every draw. `brick_tiles`: row b holds, at distinct positions, exactly the tiles whose tile_dest is b, each once.
All inputs are finite; a program needn't handle non-finite values.
Results may differ from a plain program's by a relative error of at most 0.00075.
Values may be sent and summed in bfloat16 or wider, within the bound.
No kernel may reach another device: no remote copies, remote signals or barrier semaphores. Data moves between devices by JAX's collectives and lax.ppermute only.
A program may use at most 64 MiB of HBM per device.

v0:
```python
import jax
import jax.numpy as jnp
from jax import lax
from jax.sharding import PartitionSpec as P

PY = 8
TY = 8
TZ = 8


courant = 0.25


def passed_along(block, axis, distance):
    devices = range(lax.axis_size(axis))
    route = [(i - distance, i) for i in devices if i - distance in devices]
    return lax.ppermute(block, axis, route)


def shifted(array, axis, by):
    count = lax.axis_size(axis)
    return lax.ppermute(array, axis, [(i, (i + by) % count) for i in range(count)])


def forward_diff(values, along):
    rest = lax.slice_in_dim(values, 1, values.shape[along], axis=along)
    padding = jnp.zeros_like(lax.slice_in_dim(values, 0, 1, axis=along))
    return jnp.concatenate([rest, padding], axis=along) - values


def backward_diff(values, along):
    padding = jnp.zeros_like(lax.slice_in_dim(values, 0, 1, axis=along))
    rest = lax.slice_in_dim(values, 0, values.shape[along] - 1, axis=along)
    return values - jnp.concatenate([padding, rest], axis=along)


def forward_with(values, after, along):
    rest = lax.slice_in_dim(values, 1, values.shape[along], axis=along)
    return jnp.concatenate([rest, after], axis=along) - values


def backward_with(values, before, along):
    rest = lax.slice_in_dim(values, 0, values.shape[along] - 1, axis=along)
    return values - jnp.concatenate([before, rest], axis=along)


def neighbours(ahead_x, behind_x, ahead_y, behind_y):
    got_ahead_x = passed_along(ahead_x.astype(jnp.bfloat16), "gx", -PY).astype(ahead_x.dtype)
    got_behind_x = passed_along(behind_x, "gx", PY)
    got_ahead_y = shifted(ahead_y, "gx", -1)
    got_behind_y = shifted(behind_y, "gx", 1)
    return (got_ahead_x, got_behind_x, got_ahead_y, got_behind_y)


def stress_faces(stress):
    return neighbours(stress[0:1, :1], stress[3:5, -1:], stress[1:2, :, :1], stress[3::2, :, -1:])


def velocity_faces(velocity):
    return neighbours(
        velocity[1:3, :1], velocity[0:1, -1:], velocity[0::2, :, :1], velocity[1:2, :, -1:]
    )


def body(
    velocity,
    stress,
    memory,
    lame_lambda,
    lame_mu,
    buoyancy,
    decay,
    loss,
    tile_lambda,
    tile_mu,
    tile_buoy,
    tile_dest,
    brick_tiles,
    src_index,
    src_wave,
):
    bricks = lax.axis_size("gx")
    per_device = tile_lambda.shape[0]
    width_x, width_y, width_z = lame_lambda.shape[1:]
    rows_y = width_y // TY
    rows_z = width_z // TZ
    brick_ids = jnp.arange(bricks, dtype=jnp.int32)
    route = (tile_dest[None, :] == brick_ids[:, None]).astype(jnp.bfloat16)

    def pack(tiles):
        return jnp.dot(route, tiles, preferred_element_type=jnp.float32).astype(jnp.bfloat16)

    arrived = (
        lax.all_to_all(pack(tile_lambda), "gx", split_axis=0, concat_axis=0, tiled=True),
        lax.all_to_all(pack(tile_mu), "gx", split_axis=0, concat_axis=0, tiled=True),
        lax.all_to_all(pack(tile_buoy), "gx", split_axis=0, concat_axis=0, tiled=True),
    )
    wanted = brick_tiles[0]
    owner = jnp.where(wanted >= 0, wanted // per_device, -1)
    select = (owner[:, None] == brick_ids[None, :]).astype(jnp.bfloat16)
    live = (wanted >= 0).reshape(rows_y, rows_z)
    inside = jnp.broadcast_to(
        live[None, :, None, :, None], (width_x, rows_y, TY, rows_z, TZ)
    ).reshape(width_x, width_y, width_z)

    def place(background, received):
        picked = jnp.dot(select, received, preferred_element_type=jnp.float32)
        picked = (
            picked.reshape(rows_y, rows_z, width_x, TY, TZ)
            .transpose(2, 0, 3, 1, 4)
            .reshape(width_x, width_y, width_z)
        )
        return jnp.where(inside, picked, background)

    lame = place(lame_lambda[0], arrived[0])
    shear = place(lame_mu[0], arrived[1])
    buoy_field = place(buoyancy[0], arrived[2])
    decay_here = decay[0]
    loss_here = loss[0]
    fields_v = velocity[:, 0]
    fields_s = stress[:, 0]
    fields_m = memory[:, 0]
    for step_index in range(src_wave.shape[1]):
        ahead_xs, behind_xs, ahead_ys, behind_ys = stress_faces(fields_s)
        grad_x = (
            forward_with(fields_s[0], ahead_xs[0], 0)
            + backward_with(fields_s[3], behind_ys[0], 1)
            + backward_diff(fields_s[4], 2)
        )
        grad_y = (
            backward_with(fields_s[3], behind_xs[0], 0)
            + forward_with(fields_s[1], ahead_ys[0], 1)
            + backward_diff(fields_s[5], 2)
        )
        grad_z = (
            backward_with(fields_s[4], behind_xs[1], 0)
            + backward_with(fields_s[5], behind_ys[1], 1)
            + forward_diff(fields_s[2], 2)
        )
        fields_v = fields_v + courant * buoy_field * jnp.stack([grad_x, grad_y, grad_z])
        ahead_xv, behind_xv, ahead_yv, behind_yv = velocity_faces(fields_v)
        strain_x = backward_with(fields_v[0], behind_xv[0], 0)
        strain_y = backward_with(fields_v[1], behind_yv[0], 1)
        strain_z = backward_diff(fields_v[2], 2)
        dilation = strain_x + strain_y + strain_z
        rates = jnp.stack(
            [
                lame * dilation + 2.0 * shear * strain_x,
                lame * dilation + 2.0 * shear * strain_y,
                lame * dilation + 2.0 * shear * strain_z,
                shear
                * (
                    forward_with(fields_v[0], ahead_yv[0], 1)
                    + forward_with(fields_v[1], ahead_xv[0], 0)
                ),
                shear * (forward_diff(fields_v[0], 2) + forward_with(fields_v[2], ahead_xv[1], 0)),
                shear * (forward_diff(fields_v[1], 2) + forward_with(fields_v[2], ahead_yv[1], 1)),
            ]
        )
        fields_m = decay_here * fields_m - (1.0 - decay_here) * loss_here * rates
        fields_s = fields_s + courant * (rates + fields_m)
        source = (
            jnp.zeros((width_x * width_y * width_z,), jnp.float32)
            .at[src_index]
            .add(src_wave[:, step_index])
            .reshape(width_x, width_y, width_z)
        )
        fields_s = fields_s.at[:3].add(source[None])
    return (fields_v[:, None], fields_s[:, None], fields_m[:, None])


def solution(mesh):
    return jax.shard_map(
        body,
        mesh=mesh,
        in_specs=(
            P(None, ("groups", "gx"), None, None, None),
            P(None, ("groups", "gx"), None, None, None),
            P(None, ("groups", "gx"), None, None, None),
            P(("groups", "gx"), None, None, None),
            P(("groups", "gx"), None, None, None),
            P(("groups", "gx"), None, None, None),
            P(("groups", "gx"), None, None, None),
            P(("groups", "gx"), None, None, None),
            P(("groups", "gx"), None),
            P(("groups", "gx"), None),
            P(("groups", "gx"), None),
            P(("groups", "gx")),
            P(("groups", "gx"), None),
            P(("groups", "gx")),
            P(("groups", "gx"), None),
        ),
        out_specs=(
            P(None, ("groups", "gx"), None, None, None),
            P(None, ("groups", "gx"), None, None, None),
            P(None, ("groups", "gx"), None, None, None),
        ),
        check_vma=False,
    )
```

profile of v0, /device:TPU:0, one launch (start us, length us, event | category | flops | bytes accessed | tf_op | source)
XLA Modules:
  0.0 102.7 jit_solution(5612992693066059963)
XLA Ops:
  0.7 0.8 slice.652
  1.4 1.3 %collective-permute-start = (bf16[1,1,32,128]{3,2,1,0:T(8,128)(2,1)S(1)}, bf16[1,1,32,128]{3,2,1,0:T(8,128)(2,1)S(1)}, u32[]{:S(2)}, u32[]{:S(2)}) collective-permute-start(bf16[1,1,32,128]{3,2,1,0:T(8,128)(2,1)S(1)} %slice.652), channel_id=1, source_target_pairs={{8,0},{9,1},{10,2},{11,3},{12,4},{13,5},{14,6},{15,7},{24,16},{25,... | collective-permute-start | bytes 24584 | tf_op jit(solution)/shard_map/ppermute | solution.py:17
  2.7 0.8 slice.405
  4.0 1.4 %slice.504 = f32[2,1,32,128]{3,2,1,0:T(8,128)} slice(f32[6,4,32,128]{3,2,1,0:T(8,128)} %bitcast.340), slice={[3:5], [3:4], [0:32], [0:128]} | slice | bytes 65536 | tf_op jit(solution)/shard_map/slice | solution.py:56
  5.3 6.1 %collective-permute-start.2 = (f32[2,1,32,128]{3,2,1,0:T(8,128)}, f32[2,1,32,128]{3,2,1,0:T(8,128)}, u32[]{:S(2)}, u32[]{:S(2)}) collective-permute-start(f32[2,1,32,128]{3,2,1,0:T(8,128)} %slice.504), channel_id=1, source_target_pairs={{0,8},{1,9},{2,10},{3,11},{4,12},{5,13},{6,14},{7,15},{16,24},{17,... | collective-permute-start | bytes 98312 | tf_op jit(solution)/shard_map/ppermute | solution.py:17
  11.4 1.3 %slice.507 = f32[1,4,1,128]{3,2,1,0:T(1,128)} slice(f32[6,4,32,128]{3,2,1,0:T(8,128)} %bitcast.341), slice={[1:2], [0:4], [0:1], [0:128]} | slice | bytes 4096 | tf_op jit(solution)/shard_map/slice | solution.py:56
  12.7 0.9 collective-permute-start.3
  13.6 0.8 fusion.2
  14.3 0.5 broadcast.264
  14.9 0.6 reduce.8
  15.4 0.6 reshape.547
  16.1 5.5 %all-to-all-start.2 = ((bf16[16,2,128]{2,1,0:T(2,128)(2,1)}), bf16[16,2,128]{2,1,0:T(2,128)(2,1)S(1)}, u32[]{:S(2)}, u32[]{:S(2)}) async-start(bf16[16,2,128]{2,1,0:T(2,128)(2,1)} %reshape.547), calls=%async_computation.2 | async-start | bytes 16384 | tf_op jit(solution)/shard_map/all_to_all | solution.py:95
  21.5 0.9 fusion.54
  22.4 0.5 broadcast.263
  23.1 0.7 reduce.7
  23.9 0.6 copy-done.21
  24.6 0.5 copy-done.25
  25.2 0.7 copy-done.23
  25.9 0.7 copy_bitcast_fusion.5
  26.8 0.7 copy-done.22
  27.7 0.6 slice.502
  28.3 0.7 slice.512
  29.1 0.6 slice.511
  29.7 0.7 copy.390
  30.4 0.6 slice.506
  31.3 0.6 reduce.9
  31.9 0.6 reshape.543
  32.5 0.6 reduce.10
  33.1 0.6 reshape.545
  33.7 0.7 scatter_custom_fusion
  34.4 0.7 copy.218
  35.1 0.7 scatter_custom_fusion.1
  35.8 0.6 fusion.60
  36.4 6.0 %all-to-all-start = ((bf16[16,2,128]{2,1,0:T(2,128)(2,1)}), bf16[16,2,128]{2,1,0:T(2,128)(2,1)S(1)}, u32[]{:S(2)}, u32[]{:S(2)}) async-start(bf16[16,2,128]{2,1,0:T(2,128)(2,1)} %reshape.543), calls=%async_computation | async-start | bytes 16384 | tf_op jit(solution)/shard_map/all_to_all | solution.py:96
  42.4 0.6 bitcast_convert_fusion
  43.1 5.6 %all-to-all-done = bf16[16,2,128]{2,1,0:T(2,128)(2,1)S(1)} async-done(((bf16[16,2,128]{2,1,0:T(2,128)(2,1)}), bf16[16,2,128]{2,1,0:T(2,128)(2,1)S(1)}, u32[]{:S(2)}, u32[]{:S(2)}) %all-to-all-start) | async-done | bytes 8224 | tf_op jit(solution)/shard_map/all_to_all | solution.py:96
  48.8 3.4 %all-to-all-start.1 = ((bf16[16,2,128]{2,1,0:T(2,128)(2,1)}), bf16[16,2,128]{2,1,0:T(2,128)(2,1)S(1)}, u32[]{:S(2)}, u32[]{:S(2)}) async-start(bf16[16,2,128]{2,1,0:T(2,128)(2,1)} %reshape.545), calls=%async_computation.1 | async-start | bytes 16384 | tf_op jit(solution)/shard_map/all_to_all | solution.py:94
  53.4 0.5 reshape.503
  54.2 0.5 reshape.500
  54.7 3.8 %all-to-all-done.1 = bf16[16,2,128]{2,1,0:T(2,128)(2,1)S(1)} async-done(((bf16[16,2,128]{2,1,0:T(2,128)(2,1)}), bf16[16,2,128]{2,1,0:T(2,128)(2,1)S(1)}, u32[]{:S(2)}, u32[]{:S(2)}) %all-to-all-start.1) | async-done | bytes 8224 | tf_op jit(solution)/shard_map/all_to_all | solution.py:94
  59.1 0.5 copy-done.6
  59.6 0.6 broadcast_select_fusion
  61.1 0.5 reshape.529
  62.0 0.5 reshape.528
  62.5 0.8 fusion.57
  63.3 0.9 fusion.16
  64.3 0.7 copy-done.16
  65.2 0.6 copy-done.3
  66.1 0.6 collective-permute-start.6
  66.8 1.3 %collective-permute-start.7 = (bf16[2,1,32,128]{3,2,1,0:T(8,128)(2,1)S(1)}, bf16[2,1,32,128]{3,2,1,0:T(8,128)(2,1)S(1)}, u32[]{:S(2)}, u32[]{:S(2)}) collective-permute-start(bf16[2,1,32,128]{3,2,1,0:T(8,128)(2,1)S(1)} %copy.373), channel_id=1, source_target_pairs={{8,0},{9,1},{10,2},{11,3},{12,4},{13,5},{14,6},{15,7},{24,16},{25,... | collective-permute-start | bytes 49160 | tf_op jit(solution)/shard_map/ppermute | solution.py:17
  68.2 5.4 %collective-permute-start.4 = (f32[1,1,32,128]{3,1,2,0:T(1,128)S(1)}, f32[1,1,32,128]{3,1,2,0:T(1,128)S(1)}, u32[]{:S(2)}, u32[]{:S(2)}) collective-permute-start(f32[1,1,32,128]{3,1,2,0:T(1,128)S(1)} %slice.514), channel_id=1, source_target_pairs={{0,8},{1,9},{2,10},{3,11},{4,12},{5,13},{6,14},{7,15},{16,24},{17,... | collective-permute-start | bytes 49160 | tf_op jit(solution)/shard_map/ppermute | solution.py:17
  74.1 1.0 collective-permute-done.4
  75.5 0.9 copy-done.1
  76.5 0.8 copy-done.7
  77.7 1.3 %collective-permute-start.8 = (bf16[1,1,32,128]{3,2,1,0:T(8,128)(2,1)S(1)}, bf16[1,1,32,128]{3,2,1,0:T(8,128)(2,1)S(1)}, u32[]{:S(2)}, u32[]{:S(2)}) collective-permute-start(bf16[1,1,32,128]{3,2,1,0:T(8,128)(2,1)S(1)} %copy.396), channel_id=1, source_target_pairs={{8,0},{9,1},{10,2},{11,3},{12,4},{13,5},{14,6},{15,7},{24,16},{25,... | collective-permute-start | bytes 24584 | tf_op jit(solution)/shard_map/ppermute | solution.py:17
  79.0 0.6 collective-permute-start.9
  79.5 5.2 %collective-permute-start.10 = (f32[2,1,32,128]{3,2,1,0:T(8,128)S(1)}, f32[2,1,32,128]{3,2,1,0:T(8,128)S(1)}, u32[]{:S(2)}, u32[]{:S(2)}) collective-permute-start(f32[2,1,32,128]{3,2,1,0:T(8,128)S(1)} %slice.541), channel_id=1, source_target_pairs={{0,8},{1,9},{2,10},{3,11},{4,12},{5,13},{6,14},{7,15},{16,24},{17,... | collective-permute-start | bytes 98312 | tf_op jit(solution)/shard_map/ppermute | solution.py:17
  85.3 1.0 collective-permute-done.10
  87.2 4.5 %collective-permute-start.14 = (f32[2,4,1,128]{3,1,2,0:T(4,128)S(1)}, f32[2,4,1,128]{3,1,2,0:T(4,128)S(1)}, u32[]{:S(2)}, u32[]{:S(2)}) collective-permute-start(f32[2,4,1,128]{3,1,2,0:T(4,128)S(1)} %slice.486), channel_id=1, source_target_pairs={{0,15},{1,0},{2,1},{3,2},{4,3},{5,4},{6,5},{7,6},{8,7},{9,8},{10,9... | collective-permute-start | bytes 12296 | tf_op jit(solution)/shard_map/ppermute | solution.py:22
  92.0 0.7 copy.250
  92.8 1.3 %collective-permute-start.15 = (bf16[2,1,32,128]{3,1,2,0:T(2,128)(2,1)S(1)}, bf16[2,1,32,128]{3,1,2,0:T(2,128)(2,1)S(1)}, u32[]{:S(2)}, u32[]{:S(2)}) collective-permute-start(bf16[2,1,32,128]{3,1,2,0:T(2,128)(2,1)S(1)} %slice.650), channel_id=1, source_target_pairs={{8,0},{9,1},{10,2},{11,3},{12,4},{13,5},{14,6},{15,7},{24,16},{25,... | collective-permute-start | bytes 49160 | tf_op jit(solution)/shard_map/ppermute | solution.py:17
  94.1 5.4 %collective-permute-start.12 = (f32[1,1,32,128]{3,2,1,0:T(8,128)S(1)}, f32[1,1,32,128]{3,2,1,0:T(8,128)S(1)}, u32[]{:S(2)}, u32[]{:S(2)}) collective-permute-start(f32[1,1,32,128]{3,2,1,0:T(8,128)S(1)} %bitcast.411), channel_id=1, source_target_pairs={{0,8},{1,9},{2,10},{3,11},{4,12},{5,13},{6,14},{7,15},{16,24},{17,... | collective-permute-start | bytes 49160 | tf_op jit(solution)/shard_map/ppermute | solution.py:17
  99.9 1.0 %collective-permute-done.12 = f32[1,1,32,128]{3,2,1,0:T(8,128)S(1)} collective-permute-done((f32[1,1,32,128]{3,2,1,0:T(8,128)S(1)}, f32[1,1,32,128]{3,2,1,0:T(8,128)S(1)}, u32[]{:S(2)}, u32[]{:S(2)}) %collective-permute-start.12) | collective-permute-done | bytes 16416 | tf_op jit(solution)/shard_map/ppermute | solution.py:17
  101.8 0.9 multiply_subtract_fusion
  (185 shorter events, 9.6 us)
Async XLA Ops:
  0.6 12.9 %copy-start = (bf16[8,256]{1,0:T(8,128)(2,1)S(1)}, bf16[8,256]{1,0:T(8,128)(2,1)}, u32[]{:S(2)}) copy-start(bf16[8,256]{1,0:T(8,128)(2,1)} %param.28) | copy-start | bytes 12292
  0.6 21.7 %copy-start.2 = (f32[6,1,4,32,128]{4,3,2,1,0:T(8,128)S(1)}, f32[6,1,4,32,128]{4,3,2,1,0:T(8,128)}, u32[]{:S(2)}) copy-start(f32[6,1,4,32,128]{4,3,2,1,0:T(8,128)} %param.20) | copy-start | bytes 1179652
  1.4 40.9 %collective-permute-start = (bf16[1,1,32,128]{3,2,1,0:T(8,128)(2,1)S(1)}, bf16[1,1,32,128]{3,2,1,0:T(8,128)(2,1)S(1)}, u32[]{:S(2)}, u32[]{:S(2)}) collective-permute-start(bf16[1,1,32,128]{3,2,1,0:T(8,128)(2,1)S(1)} %slice.652), channel_id=1, source_target_pairs={{8,0},{9,1},{10,2},{11,3},{12,4},{13,5},{14,6},{15,7},{24,16},{25,... | collective-permute-start | bytes 24584 | tf_op jit(solution)/shard_map/ppermute | solution.py:17
  3.5 32.3 %collective-permute-start.1 = (f32[2,4,1,128]{3,2,1,0:T(1,128)S(1)}, f32[2,4,1,128]{3,2,1,0:T(1,128)S(1)}, u32[]{:S(2)}, u32[]{:S(2)}) collective-permute-start(f32[2,4,1,128]{3,2,1,0:T(1,128)S(1)} %slice.405), channel_id=1, source_target_pairs={{0,1},{1,2},{2,3},{3,4},{4,5},{5,6},{6,7},{7,8},{8,9},{9,10},{10,1... | collective-permute-start | bytes 12296 | tf_op jit(solution)/shard_map/ppermute | solution.py:22
  5.3 57.2 %collective-permute-start.2 = (f32[2,1,32,128]{3,2,1,0:T(8,128)}, f32[2,1,32,128]{3,2,1,0:T(8,128)}, u32[]{:S(2)}, u32[]{:S(2)}) collective-permute-start(f32[2,1,32,128]{3,2,1,0:T(8,128)} %slice.504), channel_id=1, source_target_pairs={{0,8},{1,9},{2,10},{3,11},{4,12},{5,13},{6,14},{7,15},{16,24},{17,... | collective-permute-start | bytes 98312 | tf_op jit(solution)/shard_map/ppermute | solution.py:17
  12.7 50.6 %collective-permute-start.3 = (f32[1,4,1,128]{3,2,1,0:T(1,128)}, f32[1,4,1,128]{3,2,1,0:T(1,128)}, u32[]{:S(2)}, u32[]{:S(2)}) collective-permute-start(f32[1,4,1,128]{3,2,1,0:T(1,128)} %slice.507), channel_id=1, source_target_pairs={{0,15},{1,0},{2,1},{3,2},{4,3},{5,4},{6,5},{7,6},{8,7},{9,8},{10,9... | collective-permute-start | bytes 6152 | tf_op jit(solution)/shard_map/ppermute | solution.py:22
  16.1 20.3 %all-to-all-start.2 = ((bf16[16,2,128]{2,1,0:T(2,128)(2,1)}), bf16[16,2,128]{2,1,0:T(2,128)(2,1)S(1)}, u32[]{:S(2)}, u32[]{:S(2)}) async-start(bf16[16,2,128]{2,1,0:T(2,128)(2,1)} %reshape.547), calls=%async_computation.2 | async-start | bytes 16384 | tf_op jit(solution)/shard_map/all_to_all | solution.py:95
  22.4 0.7 copy-start.24
  23.8 0.7 copy-start.21
  23.9 0.7 copy-start.20
  24.5 0.7 copy-start.25
  25.2 0.7 copy-start.23
  25.9 0.8 copy-start.4
  25.9 0.9 copy-start.17
  26.8 0.7 copy-start.22
  36.4 12.4 %all-to-all-start = ((bf16[16,2,128]{2,1,0:T(2,128)(2,1)}), bf16[16,2,128]{2,1,0:T(2,128)(2,1)S(1)}, u32[]{:S(2)}, u32[]{:S(2)}) async-start(bf16[16,2,128]{2,1,0:T(2,128)(2,1)} %reshape.543), calls=%async_computation | async-start | bytes 16384 | tf_op jit(solution)/shard_map/all_to_all | solution.py:96
  48.8 9.8 %all-to-all-start.1 = ((bf16[16,2,128]{2,1,0:T(2,128)(2,1)}), bf16[16,2,128]{2,1,0:T(2,128)(2,1)S(1)}, u32[]{:S(2)}, u32[]{:S(2)}) async-start(bf16[16,2,128]{2,1,0:T(2,128)(2,1)} %reshape.545), calls=%async_computation.1 | async-start | bytes 16384 | tf_op jit(solution)/shard_map/all_to_all | solution.py:94
  58.7 0.8 copy-start.6
  58.7 0.9 copy-start.18
  60.2 0.8 copy-start.9
  62.0 1.3 %copy-start.15 = (f32[4,31,128]{2,0,1:T(4,128)S(1)}, f32[4,31,128]{2,0,1:T(4,128)}, u32[]{:S(2)}) copy-start(f32[4,31,128]{2,0,1:T(4,128)} %slice.506) | copy-start | bytes 190468
  62.5 0.8 copy-start.11
  63.3 0.9 copy-start.8
  63.3 0.9 copy-start.10
  63.3 0.9 copy-start.13
  63.3 0.9 copy-start.14
  64.2 0.7 copy-start.16
  64.2 0.7 copy-start.19
  64.9 0.9 copy-start.3
  66.1 7.6 %collective-permute-start.6 = (f32[2,4,1,128]{3,1,2,0:T(4,128)S(1)}, f32[2,4,1,128]{3,1,2,0:T(4,128)S(1)}, u32[]{:S(2)}, u32[]{:S(2)}) collective-permute-start(f32[2,4,1,128]{3,1,2,0:T(4,128)S(1)} %slice.436), channel_id=1, source_target_pairs={{0,15},{1,0},{2,1},{3,2},{4,3},{5,4},{6,5},{7,6},{8,7},{9,8},{10,9... | collective-permute-start | bytes 12296 | tf_op jit(solution)/shard_map/ppermute | solution.py:22
  66.8 6.8 %collective-permute-start.7 = (bf16[2,1,32,128]{3,2,1,0:T(8,128)(2,1)S(1)}, bf16[2,1,32,128]{3,2,1,0:T(8,128)(2,1)S(1)}, u32[]{:S(2)}, u32[]{:S(2)}) collective-permute-start(bf16[2,1,32,128]{3,2,1,0:T(8,128)(2,1)S(1)} %copy.373), channel_id=1, source_target_pairs={{8,0},{9,1},{10,2},{11,3},{12,4},{13,5},{14,6},{15,7},{24,16},{25,... | collective-permute-start | bytes 49160 | tf_op jit(solution)/shard_map/ppermute | solution.py:17
  68.1 5.9 %collective-permute-start.5 = (f32[1,4,1,128]{3,1,2,0:T(4,128)S(1)}, f32[1,4,1,128]{3,1,2,0:T(4,128)S(1)}, u32[]{:S(2)}, u32[]{:S(2)}) collective-permute-start(f32[1,4,1,128]{3,1,2,0:T(4,128)S(1)} %slice.517), channel_id=1, source_target_pairs={{0,1},{1,2},{2,3},{3,4},{4,5},{5,6},{6,7},{7,8},{8,9},{9,10},{10,1... | collective-permute-start | bytes 6152 | tf_op jit(solution)/shard_map/ppermute | solution.py:22
  68.2 6.9 %collective-permute-start.4 = (f32[1,1,32,128]{3,1,2,0:T(1,128)S(1)}, f32[1,1,32,128]{3,1,2,0:T(1,128)S(1)}, u32[]{:S(2)}, u32[]{:S(2)}) collective-permute-start(f32[1,1,32,128]{3,1,2,0:T(1,128)S(1)} %slice.514), channel_id=1, source_target_pairs={{0,8},{1,9},{2,10},{3,11},{4,12},{5,13},{6,14},{7,15},{16,24},{17,... | collective-permute-start | bytes 49160 | tf_op jit(solution)/shard_map/ppermute | solution.py:17
  74.0 1.0 %copy-start.12 = (f32[1,4,32,128]{3,2,1,0:T(8,128)S(1)}, f32[1,4,32,128]{3,2,1,0:T(8,128)}, u32[]{:S(2)}) copy-start(f32[1,4,32,128]{3,2,1,0:T(8,128)} %param.22) | copy-start | bytes 196612
  75.4 1.0 copy-start.1
  76.5 0.8 copy-start.7
  77.7 7.6 %collective-permute-start.8 = (bf16[1,1,32,128]{3,2,1,0:T(8,128)(2,1)S(1)}, bf16[1,1,32,128]{3,2,1,0:T(8,128)(2,1)S(1)}, u32[]{:S(2)}, u32[]{:S(2)}) collective-permute-start(bf16[1,1,32,128]{3,2,1,0:T(8,128)(2,1)S(1)} %copy.396), channel_id=1, source_target_pairs={{8,0},{9,1},{10,2},{11,3},{12,4},{13,5},{14,6},{15,7},{24,16},{25,... | collective-permute-start | bytes 24584 | tf_op jit(solution)/shard_map/ppermute | solution.py:17
  79.0 6.3 %collective-permute-start.9 = (f32[2,4,1,128]{3,1,2,0:T(4,128)S(1)}, f32[2,4,1,128]{3,1,2,0:T(4,128)S(1)}, u32[]{:S(2)}, u32[]{:S(2)}) collective-permute-start(f32[2,4,1,128]{3,1,2,0:T(4,128)S(1)} %bitcast.419), channel_id=1, source_target_pairs={{0,1},{1,2},{2,3},{3,4},{4,5},{5,6},{6,7},{7,8},{8,9},{9,10},{10,1... | collective-permute-start | bytes 12296 | tf_op jit(solution)/shard_map/ppermute | solution.py:22
  79.5 6.7 %collective-permute-start.10 = (f32[2,1,32,128]{3,2,1,0:T(8,128)S(1)}, f32[2,1,32,128]{3,2,1,0:T(8,128)S(1)}, u32[]{:S(2)}, u32[]{:S(2)}) collective-permute-start(f32[2,1,32,128]{3,2,1,0:T(8,128)S(1)} %slice.541), channel_id=1, source_target_pairs={{0,8},{1,9},{2,10},{3,11},{4,12},{5,13},{6,14},{7,15},{16,24},{17,... | collective-permute-start | bytes 98312 | tf_op jit(solution)/shard_map/ppermute | solution.py:17
  85.2 1.4 %collective-permute-start.11 = (f32[1,4,1,128]{3,1,2,0:T(4,128)S(1)}, f32[1,4,1,128]{3,1,2,0:T(4,128)S(1)}, u32[]{:S(2)}, u32[]{:S(2)}) collective-permute-start(f32[1,4,1,128]{3,1,2,0:T(4,128)S(1)} %slice.546), channel_id=1, source_target_pairs={{0,15},{1,0},{2,1},{3,2},{4,3},{5,4},{6,5},{7,6},{8,7},{9,8},{10,9... | collective-permute-start | bytes 6152 | tf_op jit(solution)/shard_map/ppermute | solution.py:22
  87.2 12.3 %collective-permute-start.14 = (f32[2,4,1,128]{3,1,2,0:T(4,128)S(1)}, f32[2,4,1,128]{3,1,2,0:T(4,128)S(1)}, u32[]{:S(2)}, u32[]{:S(2)}) collective-permute-start(f32[2,4,1,128]{3,1,2,0:T(4,128)S(1)} %slice.486), channel_id=1, source_target_pairs={{0,15},{1,0},{2,1},{3,2},{4,3},{5,4},{6,5},{7,6},{8,7},{9,8},{10,9... | collective-permute-start | bytes 12296 | tf_op jit(solution)/shard_map/ppermute | solution.py:22
  92.8 6.8 %collective-permute-start.15 = (bf16[2,1,32,128]{3,1,2,0:T(2,128)(2,1)S(1)}, bf16[2,1,32,128]{3,1,2,0:T(2,128)(2,1)S(1)}, u32[]{:S(2)}, u32[]{:S(2)}) collective-permute-start(bf16[2,1,32,128]{3,1,2,0:T(2,128)(2,1)S(1)} %slice.650), channel_id=1, source_target_pairs={{8,0},{9,1},{10,2},{11,3},{12,4},{13,5},{14,6},{15,7},{24,16},{25,... | collective-permute-start | bytes 49160 | tf_op jit(solution)/shard_map/ppermute | solution.py:17
  94.0 5.9 %collective-permute-start.13 = (f32[1,4,1,128]{3,1,2,0:T(4,128)S(1)}, f32[1,4,1,128]{3,1,2,0:T(4,128)S(1)}, u32[]{:S(2)}, u32[]{:S(2)}) collective-permute-start(f32[1,4,1,128]{3,1,2,0:T(4,128)S(1)} %slice.559), channel_id=1, source_target_pairs={{0,1},{1,2},{2,3},{3,4},{4,5},{5,6},{6,7},{7,8},{8,9},{9,10},{10,1... | collective-permute-start | bytes 6152 | tf_op jit(solution)/shard_map/ppermute | solution.py:22
  94.1 6.9 %collective-permute-start.12 = (f32[1,1,32,128]{3,2,1,0:T(8,128)S(1)}, f32[1,1,32,128]{3,2,1,0:T(8,128)S(1)}, u32[]{:S(2)}, u32[]{:S(2)}) collective-permute-start(f32[1,1,32,128]{3,2,1,0:T(8,128)S(1)} %bitcast.411), channel_id=1, source_target_pairs={{0,8},{1,9},{2,10},{3,11},{4,12},{5,13},{6,14},{7,15},{16,24},{17,... | collective-permute-start | bytes 49160 | tf_op jit(solution)/shard_map/ppermute | solution.py:17
  101.8 0.9 copy-start.5
where the time goes:
time: 104 us; the launch traced here: 103 us
  starting transfers between devices  49.3 us (47%)
  local copies, waits for them, and re-layouts  27.4 us (26%)
  waiting for transfers between devices  12.8 us (12%)
  other arithmetic  9.46 us (9%)
  matrix products  1.93 us (2%)
  between operations  1.81 us (2%)
    ppermute x8, starting transfers between devices, passed_along(): return lax.ppermute(block, axis, route)  27.3 us
    unnamed x91, local copies, waits for them, and re-layouts  11.2 us
    ppermute x8, starting transfers between devices, shifted(): lax.ppermute(array, axis, [(i, (i + by) % count) for i in range(count)])  7.12 us
    all_to_all x1, starting transfers between devices, body(): lax.all_to_all(pack(tile_buoy), 'gx', split_axis=0, concat_axis=0, tiled=...  6.01 us
    all_to_all x1, waiting for transfers between devices, body(): lax.all_to_all(pack(tile_buoy), 'gx', split_axis=0, concat_axis=0, tiled=...  5.65 us
    all_to_all x1, starting transfers between devices, body(): lax.all_to_all(pack(tile_mu), 'gx', split_axis=0, concat_axis=0, tiled=True)  5.46 us
    all_to_all x1, waiting for transfers between devices, body(): lax.all_to_all(pack(tile_lambda), 'gx', split_axis=0, concat_axis=0, tile...  3.85 us
    all_to_all x1, starting transfers between devices, body(): lax.all_to_all(pack(tile_lambda), 'gx', split_axis=0, concat_axis=0, tile...  3.42 us
  transfers between devices with their start and end apart: 19, of which 6 were waited for; matrix products, arithmetic and copies ran while one was open for 26% of the time, Pallas kernels for 0%

commit v1 on v0

v1 whole, which is shorter than its diff:
```python
import functools

import jax
import jax.numpy as jnp
from jax import lax
from jax.experimental import pallas as pl
from jax.experimental.pallas import tpu as pltpu
from jax.sharding import PartitionSpec as P

PY = 8
TY = 8
TZ = 8
courant = 0.25

F32 = jnp.float32
BF16 = jnp.bfloat16
XX, YY, ZZ, XY, XZ, YZ = range(6)
STRESS, VEL, HELD, GAIN, LAME, MU, BUOY = 0, 6, 9, 15, 16, 17, 18
FIELDS = 19
LAST = [(STRESS + c, i) for c in (XX, XY, XZ) for i in (2, 3)] + [(STRESS + c, 3) for c in (YY, ZZ, YZ)]
LAST += [(VEL, 2), (VEL, 3), (VEL + 1, 3), (VEL + 2, 3), (BUOY, 2), (BUOY, 3)]
LAST += [(HELD + c, 3) for c in (XX, XY, XZ)] + [(GAIN, 3), (LAME, 3), (MU, 3)]
FIRST = [(STRESS + c, i) for c in range(6) for i in (0, 1)]
FIRST += [(VEL, 0), (VEL + 1, 0), (VEL + 1, 1), (VEL + 2, 0), (VEL + 2, 1), (BUOY, 0), (BUOY, 1)]
FIRST += [(HELD + c, 0) for c in range(6)] + [(GAIN, 0), (LAME, 0), (MU, 0)]
LONGEST = max(len(LAST), len(FIRST))
ROWS = 32
EXT = ROWS + 8
LANES = 128
BLOCK = FIELDS * 8 + 8


def pair_near(i):
    return i ^ 1


def pair_far(i, n):
    return (i - 1) % n if i % 2 == 0 else (i + 1) % n


def is_merged(n):
    return n == 2 * PY


def tile_offsets(n):
    if is_merged(n):
        return [0, -1, 1, PY, PY - 1, PY + 1]
    return [0, -1, 1, -PY, -PY - 1, -PY + 1, PY, PY - 1, PY + 1]


def slot_count(n):
    return 8 if is_merged(n) else 16


def roll(x, by, axis):
    size = x.shape[axis]
    by = by % size
    return x if by == 0 else pltpu.roll(x, by, axis)


def sublane(shape):
    return lax.broadcasted_iota(jnp.int32, shape, 0)


def lane(shape):
    return lax.broadcasted_iota(jnp.int32, shape, 1)


def place_sources(into, index, wave, step, count):
    into[...] = jnp.zeros_like(into)
    lanes = lane((1, LANES))
    for e in range(count):
        cell = index[e]
        row = lax.shift_right_logical(cell, 7)
        here = jnp.where(lanes == (cell & (LANES - 1)), wave[e, step], 0.0)
        into[pl.ds(row, 1), :] = into[pl.ds(row, 1), :] + here


def pack_kernel(n, *refs):
    merged = is_merged(n)
    (vel, st, mem, lam, mu, bu, dec, los, t_lam, t_mu, t_bu, dest, tiles, index, wave) = refs[:15]
    outs = refs[15:]
    out_a, out_b, out_d, out_e, out_t, out_map = outs[:6]
    out_c = outs[6 : 7 if merged else 8]
    held, gain, source = outs[7 if merged else 8 :]
    b = lax.axis_index("gx")
    even = lax.rem(b, 2) == 0
    place_sources(source, index, wave, 0, index.shape[0])
    for i in range(4):
        d = dec[0, i]
        gain[i] = courant * (1.0 - (1.0 - d) * los[0, i])
        kept = courant * d
        for c in range(6):
            value = st[c, 0, i] + kept * mem[c, 0, i]
            if c < 3:
                value = value + source[i * ROWS : (i + 1) * ROWS, :]
            held[c, i] = value

    def get(f, i, rows=slice(None)):
        if f < VEL:
            return st[f, 0, i, rows]
        if f < HELD:
            return vel[f - VEL, 0, i, rows]
        if f < GAIN:
            return held[f - HELD, i, rows]
        if f == GAIN:
            return gain[i, rows]
        return (lam, mu, bu)[f - LAME][0, i, rows]

    sub = sublane((8, LANES))
    top, bottom = slice(0, 8), slice(ROWS - 8, ROWS)

    per = t_lam.shape[0]
    rows_z = LANES // TZ
    table = tiles[...]
    spots = table.shape[1]
    owner = jnp.where(table >= 0, jnp.floor((table.astype(F32) + 0.5) * (1.0 / per)) + 1.0, 0.0)
    spot = lane((8, spots))
    wide = jnp.where(spot // rows_z == sublane((8, spots)), jnp.broadcast_to(owner, (8, spots)), 0.0)
    spread = (lax.rem(sublane((spots, LANES)), rows_z) == lane((spots, LANES)) // TZ).astype(BF16)
    owners = jnp.dot(wide.astype(BF16), spread, preferred_element_type=F32) - 1.0
    out_map[...] = owners

    def edge_rows(f):
        if f == FIELDS:
            lo = jnp.broadcast_to(owners[0:1], (8, LANES))
            hi = jnp.broadcast_to(owners[ROWS // TY - 1 : ROWS // TY], (8, LANES))
            return lo, hi
        lo, hi = get(f, 0, top), roll(get(f, 0, bottom), 2, 0)
        for i in range(1, 4):
            mine = sub // 2 == i
            lo = jnp.where(mine, roll(get(f, i, top), 2 * i, 0), lo)
            hi = jnp.where(mine, roll(get(f, i, bottom), 2 * i + 2, 0), hi)
        return lo, hi

    for f in range(0, FIELDS + 1, 2):
        near, far = [], []
        for g in (f, f + 1):
            lo, hi = edge_rows(g)
            near.append(jnp.where(even, hi, lo))
            far.append(jnp.where(even, lo, hi))
        near, far = jnp.concatenate(near, 0), jnp.concatenate(far, 0)
        out_a[f * 8 : f * 8 + 16, :] = near
        out_b[f * 8 : f * 8 + 16, :] = far
        out_e[f * 8 : f * 8 + 16, :] = near.astype(BF16)
        out_d[f * 8 : f * 8 + 16, :] = far.astype(BF16)

    def write_layers(out, which):
        for k, (f, i) in enumerate(which):
            out[k * ROWS : (k + 1) * ROWS, :] = get(f, i).astype(BF16)

    if merged:
        out = out_c[0]
        first_x = b < PY

        @pl.when(first_x)
        def _():
            write_layers(out, LAST)
            rest = (LONGEST - len(LAST)) * ROWS
            if rest:
                out[len(LAST) * ROWS : LONGEST * ROWS, :] = jnp.zeros((rest, LANES), BF16)

        @pl.when(jnp.logical_not(first_x))
        def _():
            write_layers(out, FIRST)
            rest = (LONGEST - len(FIRST)) * ROWS
            if rest:
                out[len(FIRST) * ROWS : LONGEST * ROWS, :] = jnp.zeros((rest, LANES), BF16)

        def other_edge(f):
            if f == FIELDS:
                return owners
            parts = []
            for a in (0, 1):
                lo = jnp.where(first_x, get(f, a, top), get(f, a + 2, top))
                hi = jnp.where(first_x, get(f, a, bottom), get(f, a + 2, bottom))
                parts.append(jnp.where(lax.rem(sub, 4) < 2, roll(lo, 4 * a, 0), roll(hi, 4 * a + 4, 0)))
            return jnp.where(sub < 4, parts[0], parts[1])

        for f in range(0, FIELDS + 1, 2):
            both = jnp.concatenate([other_edge(f), other_edge(f + 1)], 0)
            out[LONGEST * ROWS + f * 8 : LONGEST * ROWS + f * 8 + 16, :] = both.astype(BF16)
    else:
        for out, which in zip(out_c, (LAST, FIRST)):
            write_layers(out, which)
            twice = jnp.concatenate([owners, owners], 0).astype(BF16)
            out[len(which) * ROWS : len(which) * ROWS + 16, :] = twice

    slots = slot_count(n)
    offsets = tile_offsets(n)
    total = n * slots
    at = lane((1, per))
    stored = jnp.full((1, per), -1, jnp.int32)
    for t in range(per):
        stored = jnp.where(at == t, dest[t], stored)
    row = sublane((total, per))
    slot = lax.rem(row, slots)
    shift = jnp.full((total, per), -4 * n, jnp.int32)
    for k, off in enumerate(offsets):
        shift = jnp.where(slot == k, off % n, shift)
    brick = row // slots + shift
    brick = jnp.where(brick >= n, brick - n, brick)
    route = (brick == stored).astype(BF16)
    for p, source_tiles in enumerate((t_lam, t_mu, t_bu)):
        picked = jnp.dot(route, source_tiles[...], preferred_element_type=F32)
        for d in range(n):
            here = picked[d * slots : (d + 1) * slots]
            both = jnp.concatenate([here[:, :LANES], here[:, LANES:]], 0).astype(BF16)
            base = (d * 6 + 2 * p) * slots
            out_t[base : base + 2 * slots, :] = both


def wave_kernel(n, *refs):
    merged = is_merged(n)
    (vel, st, mem, lam, mu, bu, dec, los, index, wave, maps, got_a, got_b, got_t) = refs[:14]
    refs = refs[14:]
    sides = 1 if merged else 2
    got_c, got_d, got_e = refs[:sides], refs[sides : 2 * sides], refs[2 * sides : 3 * sides]
    new_v, new_s, new_m, source, rows_t, spread_rows, tile_rows = refs[3 * sides :]
    b = lax.axis_index("gx")
    even = lax.rem(b, 2) == 0
    first_x = b < PY
    slots = slot_count(n)
    sub = sublane((8, LANES))

    def halo_blocks(near, far, f):
        x = near[f * 8 : f * 8 + 8, :]
        y = far[f * 8 : f * 8 + 8, :]
        return jnp.where(even, x, y), jnp.where(even, y, x)

    def halo_rows(blocks, i):
        after, before = blocks
        return jnp.where(sub < 2, roll(after, -2 * i, 0), roll(before, 6 - 2 * i, 0))

    def widen(ref):
        rows = ref.shape[0]
        return jnp.concatenate([ref[r : r + 16, :].astype(F32) for r in range(0, rows, 16)], 0)

    rows_t[...] = got_t[...].astype(F32)
    chunk = 6 * slots
    col = lane((16, LANES))
    line = sublane((16, LANES))
    on_line = col // TZ == line
    spread = (lax.rem(sublane((LANES, LANES)), TZ) == lax.rem(lane((LANES, LANES)), TZ)).astype(BF16)

    def tile_block(first, prop, pick):
        for s in range(16):
            for half in (0, 1):

                def row_of(k):
                    at = (first + s) * chunk + (2 * prop + half) * slots + k
                    return jnp.broadcast_to(rows_t[pl.ds(at, 1), :], (16, LANES))

                if len(pick) == 1:
                    value = row_of(pick[0])
                else:
                    value = jnp.where(lax.rem(line, TY) < 2, row_of(pick[1]), row_of(pick[0]))
                at = s * 32 + half * 16
                spread_rows[at : at + 16, :] = jnp.where(on_line, value, 0.0).astype(BF16)
        tile_rows[...] = jnp.dot(spread_rows[...], spread, preferred_element_type=F32)

    def overlay(prop, pick, wanted):
        def take(first, values):
            tile_block(first, prop, pick)
            done = []
            for value, (_, owner, i) in zip(values, wanted):
                for s in range(16):
                    here = tile_rows[s * 32 + i * 8 : s * 32 + i * 8 + 8, :]
                    value = jnp.where(owner == (first + s) * 1.0, here, value)
                done.append(value)
            return done

        values = [w[0] for w in wanted]
        if n == 16:
            return take(0, values)
        return lax.fori_loop(0, n // 16, lambda g, v: take(g * 16, v), values)

    column = {}
    rows_y = ROWS // TY

    def own(f, i):
        if f < VEL:
            return st[f, 0, i]
        if f < HELD:
            return vel[f - VEL, 0, i]
        if f < GAIN:
            value = st[f - HELD, 0, i] + courant * dec[0, i] * mem[f - HELD, 0, i]
            if f < HELD + 3:
                value = value + source[i * ROWS : (i + 1) * ROWS, :]
            return value
        if f == GAIN:
            return courant * (1.0 - (1.0 - dec[0, i]) * los[0, i])
        return (lam, mu, bu)[f - LAME][0, i]

    def finish(mains, halos, main_map, halo_map, pick_main, pick_halo, name):
        for f in range(FIELDS):
            layers = sorted(i for g, i in mains if g == f)
            if not layers:
                continue
            main = [mains[f, i] for i in layers]
            halo = [halos[f, i] for i in layers]
            if f >= LAME:
                wanted = []
                for i, m in zip(layers, main):
                    for p in range(rows_y):
                        owner = jnp.broadcast_to(main_map[p : p + 1], (8, LANES))
                        wanted.append((m[p * 8 : (p + 1) * 8], owner, i))
                laid = overlay(f - LAME, (pick_main,), wanted)
                main = [jnp.concatenate(laid[k * rows_y : (k + 1) * rows_y], 0) for k in range(len(layers))]
                halo = overlay(f - LAME, pick_halo, [(h, halo_map, i) for i, h in zip(layers, halo)])
            for i, m, h in zip(layers, main, halo):
                column[name, f, i] = jnp.concatenate([m, h], 0)

    place_sources(source, index, wave, 0, index.shape[0])
    mains, halos = {}, {}
    for f in range(FIELDS):
        blocks = halo_blocks(got_a, got_b, f)
        for i in range(4):
            mains[f, i] = own(f, i)
            halos[f, i] = halo_rows(blocks, i)
    after, before = halo_blocks(got_a, got_b, FIELDS)
    finish(mains, halos, maps[...], jnp.where(sub < 4, after, before), 0, (1, 2), "own")

    for side, (name, which) in enumerate((("before", LAST), ("after", FIRST))):
        mains, halos = {}, {}
        if merged:
            message = got_c[0]
            near, far = widen(got_e[0]), widen(got_d[0])
            base = LONGEST * ROWS
            edges = widen(message.at[base : base + BLOCK])
            whole = first_x if name == "after" else jnp.logical_not(first_x)
            main_map = edges[FIELDS * 8 : FIELDS * 8 + 8]
            picks = 3, (4, 5)
        else:
            message = got_c[side]
            near, far = widen(got_e[side]), widen(got_d[side])
            base = len(which) * ROWS
            main_map = message[base : base + 16, :].astype(F32)[0:8]
            picks = 3 + 3 * side, (4 + 3 * side, 5 + 3 * side)
        for k, (f, i) in enumerate(which):
            main = message[k * ROWS : (k + 1) * ROWS, :].astype(F32)
            if merged:
                edge = edges[f * 8 : f * 8 + 8]
                a = i % 2
                head = jnp.where(sub < 2, roll(edge, -4 * a, 0), 0.0)
                tail = jnp.where(sub >= 6, roll(edge, 4 - 4 * a, 0), 0.0)
                only = jnp.concatenate([head, jnp.zeros((ROWS - 16, LANES), F32), tail], 0)
                main = jnp.where(whole, main, only)
            mains[f, i] = main
            halos[f, i] = halo_rows(halo_blocks(near, far, f), i)
        after, before = halo_blocks(near, far, FIELDS)
        finish(mains, halos, main_map, jnp.where(sub < 4, after, before), picks[0], picks[1], name)

    def layers_of(f):
        names = [("before", 2), ("before", 3)] + [("own", i) for i in range(4)] + [("after", 0), ("after", 1)]
        return [column.get((name, f, i)) for name, i in names]

    s0 = [layers_of(STRESS + c) for c in range(6)]
    v0 = [layers_of(VEL + c) for c in range(3)]
    held = [layers_of(HELD + c) for c in range(6)]
    gain, lame, shear, buoy = (layers_of(f) for f in (GAIN, LAME, MU, BUOY))

    tall = sublane((EXT, LANES))
    wide = lane((EXT, LANES))

    def linked(test):
        def of(step):
            q = lax.rem(b + step + n, n)
            return jnp.where(test(q), 1, 0)

        flags = jnp.where(tall < ROWS, of(0), jnp.where(tall < ROWS + 4, of(1), of(-1)))
        return flags == 1

    link_before = linked(lambda q: q >= PY)
    link_after = linked(lambda q: q < n - PY)

    def x_next(a, l):
        if l == 1:
            return jnp.where(link_before, a[2], 0.0)
        if l == 5:
            return jnp.where(link_after, a[6], 0.0)
        return a[l + 1]

    def x_prev(a, l):
        if l == 2:
            return jnp.where(link_before, a[1], 0.0)
        if l == 6:
            return jnp.where(link_after, a[5], 0.0)
        return a[l - 1]

    def y_next(a):
        return roll(a, -1, 0)

    def y_prev(a):
        return roll(a, 1, 0)

    def z_next(a):
        return jnp.where(wide == LANES - 1, 0.0, roll(a, -1, 1))

    def z_prev(a):
        return jnp.where(wide == 0, 0.0, roll(a, 1, 1))

    def move(v, s, spans):
        new = [[None] * 8 for _ in range(3)]
        for l in spans[0]:
            grad = (x_next(s[XX], l) - s[XX][l]) + (s[XY][l] - y_prev(s[XY][l])) + (s[XZ][l] - z_prev(s[XZ][l]))
            new[0][l] = v[0][l] + courant * buoy[l] * grad
        for l in spans[1]:
            grad = (s[XY][l] - x_prev(s[XY], l)) + (y_next(s[YY][l]) - s[YY][l]) + (s[YZ][l] - z_prev(s[YZ][l]))
            new[1][l] = v[1][l] + courant * buoy[l] * grad
            grad = (s[XZ][l] - x_prev(s[XZ], l)) + (s[YZ][l] - y_prev(s[YZ][l])) + (z_next(s[ZZ][l]) - s[ZZ][l])
            new[2][l] = v[2][l] + courant * buoy[l] * grad
        return new

    def rates_at(v, l, wanted):
        out = [None] * 6
        ex = v[0][l] - x_prev(v[0], l)
        ey = v[1][l] - y_prev(v[1][l])
        ez = v[2][l] - z_prev(v[2][l])
        spread_part = lame[l] * (ex + ey + ez)
        twice = 2.0 * shear[l]
        for c, e in ((XX, ex), (YY, ey), (ZZ, ez)):
            if c in wanted:
                out[c] = spread_part + twice * e
        if XY in wanted:
            out[XY] = shear[l] * ((y_next(v[0][l]) - v[0][l]) + (x_next(v[1], l) - v[1][l]))
        if XZ in wanted:
            out[XZ] = shear[l] * ((z_next(v[0][l]) - v[0][l]) + (x_next(v[2], l) - v[2][l]))
        if YZ in wanted:
            out[YZ] = shear[l] * ((z_next(v[1][l]) - v[1][l]) + (y_next(v[2][l]) - v[2][l]))
        return out

    v1 = move(v0, s0, (range(0, 7), range(1, 8)))
    s1 = [[None] * 8 for _ in range(6)]
    m1 = {}
    for l in range(1, 7):
        wanted = (XX, XY, XZ) if l == 1 else range(6)
        rates = rates_at(v1, l, wanted)
        for c in wanted:
            s1[c][l] = held[c][l] + gain[l] * rates[c]
            if 2 <= l < 6:
                d = dec[0, l - 2]
                m1[c, l] = d * mem[c, 0, l - 2] - (1.0 - d) * los[0, l - 2] * rates[c][:ROWS]
    v2 = move(v1, s1, (range(1, 6), range(2, 7)))
    place_sources(source, index, wave, 1, index.shape[0])
    for l in range(2, 6):
        i = l - 2
        rates = rates_at(v2, l, range(6))
        d = dec[0, i]
        lost = (1.0 - d) * los[0, i]
        for c in range(3):
            new_v[c, 0, i] = v2[c][l][:ROWS]
        for c in range(6):
            rate = rates[c][:ROWS]
            m2 = d * m1[c, l] - lost * rate
            new_m[c, 0, i] = m2
            value = s1[c][l][:ROWS] + courant * (rate + m2)
            if c < 3:
                value = value + source[i * ROWS : (i + 1) * ROWS, :]
            new_s[c, 0, i] = value


def body(
    velocity,
    stress,
    memory,
    lame_lambda,
    lame_mu,
    buoyancy,
    decay,
    loss,
    tile_lambda,
    tile_mu,
    tile_buoy,
    tile_dest,
    brick_tiles,
    src_index,
    src_wave,
):
    n = lax.axis_size("gx")
    merged = is_merged(n)
    slots = slot_count(n)
    on_core = pl.BlockSpec(memory_space=pltpu.VMEM)
    scalars = pl.BlockSpec(memory_space=pltpu.SMEM)
    fields = (velocity, stress, memory, lame_lambda, lame_mu, buoyancy, decay, loss)
    if merged:
        c_rows = [LONGEST * ROWS + BLOCK]
    else:
        c_rows = [len(LAST) * ROWS + 16, len(FIRST) * ROWS + 16]
    packed = pl.pallas_call(
        functools.partial(pack_kernel, n),
        out_shape=[
            jax.ShapeDtypeStruct((BLOCK, LANES), F32),
            jax.ShapeDtypeStruct((BLOCK, LANES), F32),
            jax.ShapeDtypeStruct((BLOCK, LANES), BF16),
            jax.ShapeDtypeStruct((BLOCK, LANES), BF16),
            jax.ShapeDtypeStruct((n * 6 * slots, LANES), BF16),
            jax.ShapeDtypeStruct((8, LANES), F32),
        ]
        + [jax.ShapeDtypeStruct((r, LANES), BF16) for r in c_rows],
        in_specs=[on_core] * 11 + [scalars, on_core, scalars, scalars],
        out_specs=[on_core] * (6 + len(c_rows)),
        scratch_shapes=[
            pltpu.VMEM((6, 4, ROWS, LANES), F32),
            pltpu.VMEM((4, ROWS, LANES), F32),
            pltpu.VMEM((4 * ROWS, LANES), F32),
        ],
        compiler_params=pltpu.CompilerParams(vmem_limit_bytes=40 * 1024 * 1024),
        name="pack",
    )(*fields, tile_lambda, tile_mu, tile_buoy, tile_dest, brick_tiles, src_index, src_wave)
    out_a, out_b, out_d, out_e, out_t, own_map = packed[:6]
    out_c = packed[6:]

    def permute(array, source_of):
        return lax.ppermute(array, "gx", [(source_of(i), i) for i in range(n)])

    starts = [PY] if merged else [-PY, PY]
    got_c = [permute(c, lambda i, o=o: (i + o) % n) for c, o in zip(out_c, starts)]
    got_d = [permute(out_d, lambda i, o=o: pair_far((i + o) % n, n)) for o in starts]
    got_e = [permute(out_e, lambda i, o=o: pair_near((i + o) % n)) for o in starts]
    got_b = permute(out_b, lambda i: pair_far(i, n))
    got_a = permute(out_a, pair_near)
    got_t = lax.all_to_all(out_t, "gx", split_axis=0, concat_axis=0, tiled=True)

    return pl.pallas_call(
        functools.partial(wave_kernel, n),
        out_shape=[
            jax.ShapeDtypeStruct(velocity.shape, F32),
            jax.ShapeDtypeStruct(stress.shape, F32),
            jax.ShapeDtypeStruct(memory.shape, F32),
        ],
        in_specs=[on_core] * 8 + [scalars, scalars] + [on_core] * (4 + 3 * len(starts)),
        out_specs=[on_core] * 3,
        scratch_shapes=[
            pltpu.VMEM((4 * ROWS, LANES), F32),
            pltpu.VMEM((n * 6 * slots, LANES), F32),
            pltpu.VMEM((16 * 32, LANES), BF16),
            pltpu.VMEM((16 * 32, LANES), F32),
        ],
        compiler_params=pltpu.CompilerParams(vmem_limit_bytes=48 * 1024 * 1024),
        name="wave",
    )(*fields, src_index, src_wave, own_map, got_a, got_b, got_t, *got_c, *got_d, *got_e)


def solution(mesh):
    split = ("groups", "gx")
    whole = P(None, split, None, None, None)
    field = P(split, None, None, None)
    return jax.shard_map(
        body,
        mesh=mesh,
        in_specs=(whole,) * 3
        + (field,) * 5
        + (P(split, None),) * 3
        + (P(split), P(split, None), P(split), P(split, None)),
        out_specs=(whole,) * 3,
        check_vma=False,
    )
```

time: 104 us -> 47.2 us (0.45)
  the two profiles are of different devices: /device:TPU:0 before, /device:TPU:1 now
where the time goes in v1:
time: 47.2 us; the launch traced here: 46.6 us
  waiting for transfers between devices  16.1 us (34%)
  starting transfers between devices  15 us (32%)
  local copies, waits for them, and re-layouts  9.28 us (20%)
  Pallas kernels  5.36 us (11%)
  between operations  0.81 us (2%)
    ppermute x5, waiting for transfers between devices, permute(): return lax.ppermute(array, 'gx', [(source_of(i), i) for i in range(n)])  16.1 us
    unnamed x45, local copies, waits for them, and re-layouts  9.28 us
    ppermute x5, starting transfers between devices, permute(): return lax.ppermute(array, 'gx', [(source_of(i), i) for i in range(n)])  7.54 us
    all_to_all x1, starting transfers between devices, body(): got_t = lax.all_to_all(out_t, 'gx', split_axis=0, concat_axis=0, tiled=True)  7.49 us
    pallas_call x1, Pallas kernels, body(): pl.pallas_call(functools.partial(wave_kernel, n), out_shape=[jax.ShapeDty...  3.6 us
    pallas_call x1, Pallas kernels, body(): pl.pallas_call(functools.partial(pack_kernel, n), out_shape=[jax.ShapeDty...  1.76 us
  transfers between devices with their start and end apart: 6, of which 1 were waited for; matrix products, arithmetic and copies ran while one was open for 0% of the time, Pallas kernels for 0%

profile of v1, /device:TPU:1, one launch (start us, length us, event | category | flops | bytes accessed | tf_op | source)
XLA Modules:
  0.0 46.6 jit_solution(8966490620000375535)
XLA Ops:
  0.6 0.0 copy-start.19
  0.6 0.0 copy-start.20
  0.7 0.0 copy-start.17
  0.7 0.0 copy-start.16
  0.7 0.8 %copy.19.refs_14_.refs_9_ = f32[16,2]{1,0:T(8,128)S(1)} copy(f32[16,2]{0,1:T(2,128)} %param.29) | data formatting | bytes 256 | tf_op args[14]
  1.5 0.0 copy-done.19
  1.5 0.0 copy-done.20
  1.5 0.0 copy-done.17
  1.5 0.0 copy-done.16
  1.5 0.0 copy-start
  1.5 1.0 %copy-done = f32[6,1,4,32,128]{4,3,2,1,0:T(8,128)S(1)} copy-done((f32[6,1,4,32,128]{4,3,2,1,0:T(8,128)S(1)}, f32[6,1,4,32,128]{4,3,2,1,0:T(8,128)}, u32[]{:S(2)}) %copy-start) | copy-done | bytes 393240
  2.5 0.0 copy-start.2
  2.5 1.0 %copy-done.2 = f32[6,1,4,32,128]{4,3,2,1,0:T(8,128)S(1)} copy-done((f32[6,1,4,32,128]{4,3,2,1,0:T(8,128)S(1)}, f32[6,1,4,32,128]{4,3,2,1,0:T(8,128)}, u32[]{:S(2)}) %copy-start.2) | copy-done | bytes 393240
  3.5 0.0 copy-start.4
  3.5 0.9 %copy-done.4 = f32[3,1,4,32,128]{4,3,2,1,0:T(8,128)S(1)} copy-done((f32[3,1,4,32,128]{4,3,2,1,0:T(8,128)S(1)}, f32[3,1,4,32,128]{4,3,2,1,0:T(8,128)}, u32[]{:S(2)}) %copy-start.4) | copy-done | bytes 196632
  4.4 0.0 copy-start.6
  4.4 0.8 %copy-done.6 = f32[1,4,32,128]{3,2,1,0:T(8,128)S(1)} copy-done((f32[1,4,32,128]{3,2,1,0:T(8,128)S(1)}, f32[1,4,32,128]{3,2,1,0:T(8,128)}, u32[]{:S(2)}) %copy-start.6) | copy-done | bytes 65560
  5.2 0.0 copy-start.8
  5.2 0.8 %copy-done.8 = f32[1,4,32,128]{3,2,1,0:T(8,128)S(1)} copy-done((f32[1,4,32,128]{3,2,1,0:T(8,128)S(1)}, f32[1,4,32,128]{3,2,1,0:T(8,128)}, u32[]{:S(2)}) %copy-start.8) | copy-done | bytes 65560
  6.1 0.0 copy-start.10
  6.1 0.8 %copy-done.10 = f32[1,4,32,128]{3,2,1,0:T(8,128)S(1)} copy-done((f32[1,4,32,128]{3,2,1,0:T(8,128)S(1)}, f32[1,4,32,128]{3,2,1,0:T(8,128)}, u32[]{:S(2)}) %copy-start.10) | copy-done | bytes 65560
  6.9 0.0 copy-start.12
  6.9 0.8 %copy-done.12 = f32[1,4,32,128]{3,2,1,0:T(8,128)S(1)} copy-done((f32[1,4,32,128]{3,2,1,0:T(8,128)S(1)}, f32[1,4,32,128]{3,2,1,0:T(8,128)}, u32[]{:S(2)}) %copy-start.12) | copy-done | bytes 65560
  7.8 0.0 copy-start.14
  7.8 0.8 %copy-done.14 = f32[1,4,32,128]{3,2,1,0:T(8,128)S(1)} copy-done((f32[1,4,32,128]{3,2,1,0:T(8,128)S(1)}, f32[1,4,32,128]{3,2,1,0:T(8,128)}, u32[]{:S(2)}) %copy-start.14) | copy-done | bytes 65560
  8.6 0.0 copy-start.18
  8.6 0.7 %copy-done.18 = bf16[8,256]{1,0:T(8,128)(2,1)S(1)} copy-done((bf16[8,256]{1,0:T(8,128)(2,1)S(1)}, bf16[8,256]{1,0:T(8,128)(2,1)}, u32[]{:S(2)}) %copy-start.18) | copy-done | bytes 4120
  9.3 0.0 copy-start.21
  9.3 0.7 %copy-done.21 = s32[1,64]{1,0:T(1,128)S(1)} copy-done((s32[1,64]{1,0:T(1,128)S(1)}, s32[1,64]{1,0:T(1,128)}, u32[]{:S(2)}) %copy-start.21) | copy-done | bytes 280
  9.9 0.0 copy-start.3
  9.9 0.0 copy-start.5
  9.9 0.0 copy-start.7
  9.9 0.0 copy-start.9
  9.9 0.0 copy-start.11
  10.0 0.0 copy-start.13
  10.0 0.0 copy-start.15
  10.0 1.8 %pack.1 = (f32[160,128]{1,0:T(8,128)S(1)}, f32[160,128]{1,0:T(8,128)S(1)}, bf16[160,128]{1,0:T(8,128)(2,1)S(1)}, bf16[160,128]{1,0:T(8,128)(2,1)S(1)}, bf16[768,...) custom-call(f32[3,1,4,32,128]{4,3,2,1,0:T(8,128)S(1)} %copy-done.4, ...), custom_call_target="tpu_custom_call" | custom-call | tf_op jit(solution)/shard_map/pack/pallas_call | solution.py:490
  11.7 0.0 copy-start.1
  11.7 7.5 %all-to-all-start = ((bf16[16,48,128]{2,1,0:T(8,128)(2,1)}), bf16[16,48,128]{2,1,0:T(8,128)(2,1)S(1)}, u32[]{:S(2)}, u32[]{:S(2)}) async-start(bf16[16,48,128]{2,1,0:T(8,128)(2,1)} %bitcast), calls=%async_computation | async-start | bytes 393216 | tf_op jit(solution)/shard_map/all_to_all | solution.py:523
  19.2 2.3 %collective-permute-start.2 = (bf16[1056,128]{1,0:T(8,128)(2,1)S(1)}, bf16[1056,128]{1,0:T(8,128)(2,1)S(1)}, u32[]{:S(2)}, u32[]{:S(2)}) collective-permute-start(bf16[1056,128]{1,0:T(8,128)(2,1)S(1)} %get-tuple-element.14), channel_id=1, source_target_pairs={{8,0},{9,1},{10,2},{11,3},{12,4},{13,5},{14,6},{15,7},{0,8},{1,9},... | collective-permute-start | bytes 811016 | tf_op jit(solution)/shard_map/ppermute | solution.py:515
  21.5 0.6 %collective-permute-start = (f32[160,128]{1,0:T(8,128)S(1)}, f32[160,128]{1,0:T(8,128)S(1)}, u32[]{:S(2)}, u32[]{:S(2)}) collective-permute-start(f32[160,128]{1,0:T(8,128)S(1)} %get-tuple-element.11), channel_id=1, source_target_pairs={{1,0},{0,1},{3,2},{2,3},{5,4},{4,5},{7,6},{6,7},{9,8},{8,9},{11,10... | collective-permute-start | bytes 245768 | tf_op jit(solution)/shard_map/ppermute | solution.py:515
  22.2 1.1 %collective-permute-start.1 = (f32[160,128]{1,0:T(8,128)S(1)}, f32[160,128]{1,0:T(8,128)S(1)}, u32[]{:S(2)}, u32[]{:S(2)}) collective-permute-start(f32[160,128]{1,0:T(8,128)S(1)} %get-tuple-element.12), channel_id=1, source_target_pairs={{15,0},{2,1},{1,2},{4,3},{3,4},{6,5},{5,6},{8,7},{7,8},{10,9},{9,1... | collective-permute-start | bytes 245768 | tf_op jit(solution)/shard_map/ppermute | solution.py:515
  23.2 0.3 collective-permute-start.3
  23.5 3.3 %collective-permute-start.4 = (bf16[160,128]{1,0:T(8,128)(2,1)S(1)}, bf16[160,128]{1,0:T(8,128)(2,1)S(1)}, u32[]{:S(2)}, u32[]{:S(2)}) collective-permute-start(bf16[160,128]{1,0:T(8,128)(2,1)S(1)} %get-tuple-element.16), channel_id=1, source_target_pairs={{9,0},{8,1},{11,2},{10,3},{13,4},{12,5},{15,6},{14,7},{1,8},{0,9},... | collective-permute-start | bytes 122888 | tf_op jit(solution)/shard_map/ppermute | solution.py:515
  26.8 16.1 %collective-permute-done.3.refs_15_ = bf16[160,128]{1,0:T(8,128)(2,1)S(1)} collective-permute-done((bf16[160,128]{1,0:T(8,128)(2,1)S(1)}, bf16[160,128]{1,0:T(8,128)(2,1)S(1)}, u32[]{:S(2)}, u32[]{:S(2)}) %collective-permute-start.3) | collective-permute-done | bytes 40992 | tf_op jit(solution)/shard_map/ppermute | solution.py:515
  42.9 0.0 collective-permute-done.4.refs_16_
  42.9 0.0 collective-permute-done.refs_11_
  42.9 0.0 collective-permute-done.1.refs_12_
  42.9 0.0 collective-permute-done.2.refs_14_
  42.9 0.0 all-to-all-done
  42.9 0.0 copy-done.3
  42.9 0.0 copy-done.5
  42.9 0.0 copy-done.7
  42.9 0.0 copy-done.9
  43.0 0.0 copy-done.11
  43.0 0.0 copy-done.13
  43.0 0.0 copy-done.15
  43.0 0.0 copy-done.1
  43.0 3.6 %wave.1 = (f32[3,1,4,32,128]{4,3,2,1,0:T(8,128)}, f32[6,1,4,32,128]{4,3,2,1,0:T(8,128)}, f32[6,1,4,32,128]{4,3,2,1,0:T(8,128)}) custom-call(f32[3,1,4,32,128]{4,3,2,1,0:T(8,128)S(1)} %copy-done.5, f32[6,1,4,32,128]{4,3,2,1,0:T(8,128)S(1)} %copy-done.1, f32[6,1,4,32,128]{4,3,2,1,0:T(8,128)S(1)} %copy-done.3, f32[1,4,32,128]{3,2,1,0:T(8,128)S(1)} %copy-done.7, ...), custom_call_target="tpu_custom_call" | custom-call | tf_op jit(solution)/shard_map/wave/pallas_call | solution.py:525
Async XLA Ops:
  0.6 0.8 %copy-start.19 = (s32[16]{0:T(128)S(1)}, s32[16]{0:T(128)}, u32[]{:S(2)}) copy-start(s32[16]{0:T(128)} %refs_8_.3) | copy-start | bytes 196
  0.6 0.8 %copy-start.20 = (s32[8]{0:T(128)S(1)}, s32[8]{0:T(128)}, u32[]{:S(2)}) copy-start(s32[8]{0:T(128)} %refs_11_.1) | copy-start | bytes 100
  0.7 0.8 %copy-start.17 = (bf16[8,256]{1,0:T(8,128)(2,1)S(1)}, bf16[8,256]{1,0:T(8,128)(2,1)}, u32[]{:S(2)}) copy-start(bf16[8,256]{1,0:T(8,128)(2,1)} %refs_9_.2) | copy-start | bytes 12292
  0.7 0.8 %copy-start.16 = (bf16[8,256]{1,0:T(8,128)(2,1)S(1)}, bf16[8,256]{1,0:T(8,128)(2,1)}, u32[]{:S(2)}) copy-start(bf16[8,256]{1,0:T(8,128)(2,1)} %refs_8_.2) | copy-start | bytes 12292
  1.5 1.0 %copy-start = (f32[6,1,4,32,128]{4,3,2,1,0:T(8,128)S(1)}, f32[6,1,4,32,128]{4,3,2,1,0:T(8,128)}, u32[]{:S(2)}) copy-start(f32[6,1,4,32,128]{4,3,2,1,0:T(8,128)} %refs_1_.3) | copy-start | bytes 1179652
  2.5 1.0 %copy-start.2 = (f32[6,1,4,32,128]{4,3,2,1,0:T(8,128)S(1)}, f32[6,1,4,32,128]{4,3,2,1,0:T(8,128)}, u32[]{:S(2)}) copy-start(f32[6,1,4,32,128]{4,3,2,1,0:T(8,128)} %refs_2_.3) | copy-start | bytes 1179652
  3.5 0.9 %copy-start.4 = (f32[3,1,4,32,128]{4,3,2,1,0:T(8,128)S(1)}, f32[3,1,4,32,128]{4,3,2,1,0:T(8,128)}, u32[]{:S(2)}) copy-start(f32[3,1,4,32,128]{4,3,2,1,0:T(8,128)} %refs_0_.3) | copy-start | bytes 589828
  4.4 0.8 %copy-start.6 = (f32[1,4,32,128]{3,2,1,0:T(8,128)S(1)}, f32[1,4,32,128]{3,2,1,0:T(8,128)}, u32[]{:S(2)}) copy-start(f32[1,4,32,128]{3,2,1,0:T(8,128)} %refs_3_.3) | copy-start | bytes 196612
  5.2 0.8 %copy-start.8 = (f32[1,4,32,128]{3,2,1,0:T(8,128)S(1)}, f32[1,4,32,128]{3,2,1,0:T(8,128)}, u32[]{:S(2)}) copy-start(f32[1,4,32,128]{3,2,1,0:T(8,128)} %refs_4_.3) | copy-start | bytes 196612
  6.1 0.8 %copy-start.10 = (f32[1,4,32,128]{3,2,1,0:T(8,128)S(1)}, f32[1,4,32,128]{3,2,1,0:T(8,128)}, u32[]{:S(2)}) copy-start(f32[1,4,32,128]{3,2,1,0:T(8,128)} %refs_5_.3) | copy-start | bytes 196612
  6.9 0.8 %copy-start.12 = (f32[1,4,32,128]{3,2,1,0:T(8,128)S(1)}, f32[1,4,32,128]{3,2,1,0:T(8,128)}, u32[]{:S(2)}) copy-start(f32[1,4,32,128]{3,2,1,0:T(8,128)} %refs_6_.3) | copy-start | bytes 196612
  7.8 0.8 %copy-start.14 = (f32[1,4,32,128]{3,2,1,0:T(8,128)S(1)}, f32[1,4,32,128]{3,2,1,0:T(8,128)}, u32[]{:S(2)}) copy-start(f32[1,4,32,128]{3,2,1,0:T(8,128)} %refs_7_.3) | copy-start | bytes 196612
  8.6 0.7 %copy-start.18 = (bf16[8,256]{1,0:T(8,128)(2,1)S(1)}, bf16[8,256]{1,0:T(8,128)(2,1)}, u32[]{:S(2)}) copy-start(bf16[8,256]{1,0:T(8,128)(2,1)} %refs_10_.1) | copy-start | bytes 12292
  9.3 0.7 %copy-start.21 = (s32[1,64]{1,0:T(1,128)S(1)}, s32[1,64]{1,0:T(1,128)}, u32[]{:S(2)}) copy-start(s32[1,64]{1,0:T(1,128)} %refs_12_.1) | copy-start | bytes 772
  9.9 33.0 %copy-start.3 = (f32[6,1,4,32,128]{4,3,2,1,0:T(8,128)S(1)}, f32[6,1,4,32,128]{4,3,2,1,0:T(8,128)}, u32[]{:S(2)}) copy-start(f32[6,1,4,32,128]{4,3,2,1,0:T(8,128)} %refs_2_.3) | copy-start | bytes 1179652
  9.9 33.0 %copy-start.5 = (f32[3,1,4,32,128]{4,3,2,1,0:T(8,128)S(1)}, f32[3,1,4,32,128]{4,3,2,1,0:T(8,128)}, u32[]{:S(2)}) copy-start(f32[3,1,4,32,128]{4,3,2,1,0:T(8,128)} %refs_0_.3) | copy-start | bytes 589828
  9.9 33.0 %copy-start.7 = (f32[1,4,32,128]{3,2,1,0:T(8,128)S(1)}, f32[1,4,32,128]{3,2,1,0:T(8,128)}, u32[]{:S(2)}) copy-start(f32[1,4,32,128]{3,2,1,0:T(8,128)} %refs_3_.3) | copy-start | bytes 196612
  9.9 33.0 %copy-start.9 = (f32[1,4,32,128]{3,2,1,0:T(8,128)S(1)}, f32[1,4,32,128]{3,2,1,0:T(8,128)}, u32[]{:S(2)}) copy-start(f32[1,4,32,128]{3,2,1,0:T(8,128)} %refs_4_.3) | copy-start | bytes 196612
  9.9 33.0 %copy-start.11 = (f32[1,4,32,128]{3,2,1,0:T(8,128)S(1)}, f32[1,4,32,128]{3,2,1,0:T(8,128)}, u32[]{:S(2)}) copy-start(f32[1,4,32,128]{3,2,1,0:T(8,128)} %refs_5_.3) | copy-start | bytes 196612
  10.0 33.0 %copy-start.13 = (f32[1,4,32,128]{3,2,1,0:T(8,128)S(1)}, f32[1,4,32,128]{3,2,1,0:T(8,128)}, u32[]{:S(2)}) copy-start(f32[1,4,32,128]{3,2,1,0:T(8,128)} %refs_6_.3) | copy-start | bytes 196612
  10.0 33.0 %copy-start.15 = (f32[1,4,32,128]{3,2,1,0:T(8,128)S(1)}, f32[1,4,32,128]{3,2,1,0:T(8,128)}, u32[]{:S(2)}) copy-start(f32[1,4,32,128]{3,2,1,0:T(8,128)} %refs_7_.3) | copy-start | bytes 196612
  11.7 31.2 %copy-start.1 = (f32[6,1,4,32,128]{4,3,2,1,0:T(8,128)S(1)}, f32[6,1,4,32,128]{4,3,2,1,0:T(8,128)}, u32[]{:S(2)}) copy-start(f32[6,1,4,32,128]{4,3,2,1,0:T(8,128)} %refs_1_.3) | copy-start | bytes 1179652
  11.7 31.2 %all-to-all-start = ((bf16[16,48,128]{2,1,0:T(8,128)(2,1)}), bf16[16,48,128]{2,1,0:T(8,128)(2,1)S(1)}, u32[]{:S(2)}, u32[]{:S(2)}) async-start(bf16[16,48,128]{2,1,0:T(8,128)(2,1)} %bitcast), calls=%async_computation | async-start | bytes 393216 | tf_op jit(solution)/shard_map/all_to_all | solution.py:523
  19.2 23.7 %collective-permute-start.2 = (bf16[1056,128]{1,0:T(8,128)(2,1)S(1)}, bf16[1056,128]{1,0:T(8,128)(2,1)S(1)}, u32[]{:S(2)}, u32[]{:S(2)}) collective-permute-start(bf16[1056,128]{1,0:T(8,128)(2,1)S(1)} %get-tuple-element.14), channel_id=1, source_target_pairs={{8,0},{9,1},{10,2},{11,3},{12,4},{13,5},{14,6},{15,7},{0,8},{1,9},... | collective-permute-start | bytes 811016 | tf_op jit(solution)/shard_map/ppermute | solution.py:515
  21.5 21.4 %collective-permute-start = (f32[160,128]{1,0:T(8,128)S(1)}, f32[160,128]{1,0:T(8,128)S(1)}, u32[]{:S(2)}, u32[]{:S(2)}) collective-permute-start(f32[160,128]{1,0:T(8,128)S(1)} %get-tuple-element.11), channel_id=1, source_target_pairs={{1,0},{0,1},{3,2},{2,3},{5,4},{4,5},{7,6},{6,7},{9,8},{8,9},{11,10... | collective-permute-start | bytes 245768 | tf_op jit(solution)/shard_map/ppermute | solution.py:515
  22.2 20.7 %collective-permute-start.1 = (f32[160,128]{1,0:T(8,128)S(1)}, f32[160,128]{1,0:T(8,128)S(1)}, u32[]{:S(2)}, u32[]{:S(2)}) collective-permute-start(f32[160,128]{1,0:T(8,128)S(1)} %get-tuple-element.12), channel_id=1, source_target_pairs={{15,0},{2,1},{1,2},{4,3},{3,4},{6,5},{5,6},{8,7},{7,8},{10,9},{9,1... | collective-permute-start | bytes 245768 | tf_op jit(solution)/shard_map/ppermute | solution.py:515
  23.2 19.6 %collective-permute-start.3 = (bf16[160,128]{1,0:T(8,128)(2,1)S(1)}, bf16[160,128]{1,0:T(8,128)(2,1)S(1)}, u32[]{:S(2)}, u32[]{:S(2)}) collective-permute-start(bf16[160,128]{1,0:T(8,128)(2,1)S(1)} %get-tuple-element.15), channel_id=1, source_target_pairs={{7,0},{10,1},{9,2},{12,3},{11,4},{14,5},{13,6},{0,7},{15,8},{2,9},... | collective-permute-start | bytes 122888 | tf_op jit(solution)/shard_map/ppermute | solution.py:515
  23.5 19.4 %collective-permute-start.4 = (bf16[160,128]{1,0:T(8,128)(2,1)S(1)}, bf16[160,128]{1,0:T(8,128)(2,1)S(1)}, u32[]{:S(2)}, u32[]{:S(2)}) collective-permute-start(bf16[160,128]{1,0:T(8,128)(2,1)S(1)} %get-tuple-element.16), channel_id=1, source_target_pairs={{9,0},{8,1},{11,2},{10,3},{13,4},{12,5},{15,6},{14,7},{1,8},{0,9},... | collective-permute-start | bytes 122888 | tf_op jit(solution)/shard_map/ppermute | solution.py:515

commit v2 on v1

v2 whole, which is shorter than its diff:
```python
import functools

import jax
import jax.numpy as jnp
from jax import lax
from jax.experimental import pallas as pl
from jax.experimental.pallas import tpu as pltpu
from jax.sharding import PartitionSpec as P

PY = 8
TY = 8
TZ = 8
courant = 0.25

F32 = jnp.float32
BF16 = jnp.bfloat16
XX, YY, ZZ, XY, XZ, YZ = range(6)
STRESS, VEL, HELD, GAIN, LAME, MU, BUOY = 0, 6, 9, 15, 16, 17, 18
FIELDS = 19
LAST = [(STRESS + c, i) for c in (XX, XY, XZ) for i in (2, 3)] + [(STRESS + c, 3) for c in (YY, ZZ, YZ)]
LAST += [(VEL, 2), (VEL, 3), (VEL + 1, 3), (VEL + 2, 3), (BUOY, 2), (BUOY, 3)]
LAST += [(HELD + c, 3) for c in (XX, XY, XZ)] + [(GAIN, 3), (LAME, 3), (MU, 3)]
FIRST = [(STRESS + c, i) for c in range(6) for i in (0, 1)]
FIRST += [(VEL, 0), (VEL + 1, 0), (VEL + 1, 1), (VEL + 2, 0), (VEL + 2, 1), (BUOY, 0), (BUOY, 1)]
FIRST += [(HELD + c, 0) for c in range(6)] + [(GAIN, 0), (LAME, 0), (MU, 0)]
BELOW_LAST = [(STRESS + c, 3) for c in range(6) if c != ZZ] + [(VEL, 3), (VEL + 1, 3), (HELD + XY, 3), (GAIN, 3)]
BELOW_LAST = [(f, i, -1) for f, i in BELOW_LAST + [(MU, 3), (BUOY, 3), (STRESS + XY, 2)]] + [(STRESS + XY, 3, -2)]
ABOVE_LAST = [(STRESS + c, 3) for c in range(6)] + [(VEL, 3), (VEL + 2, 3), (HELD + XZ, 3), (GAIN, 3)]
ABOVE_LAST = [(f, i, 0) for f, i in ABOVE_LAST + [(MU, 3), (BUOY, 3), (STRESS + XZ, 2)]] + [(STRESS + XZ, 3, 1)]
BELOW_FIRST = [(STRESS + c, 0) for c in range(6)] + [(VEL + 1, 0), (VEL + 2, 0), (HELD + YZ, 0), (GAIN, 0)]
BELOW_FIRST = [(f, i, -1) for f, i in BELOW_FIRST + [(MU, 0), (BUOY, 0), (STRESS + YZ, 1)]] + [(STRESS + YZ, 0, -2)]
ABOVE_FIRST = [(STRESS + c, 0) for c in range(6)] + [(VEL + c, 0) for c in range(3)] + [(HELD + XX, 0), (HELD + YY, 0)]
ABOVE_FIRST += [(GAIN, 0), (LAME, 0), (MU, 0), (BUOY, 0), (STRESS + XX, 1), (STRESS + YY, 1)]
ABOVE_FIRST = [(f, i, 0) for f, i in ABOVE_FIRST] + [(STRESS + XX, 0, 1), (STRESS + YY, 0, 1)]
BELOW = BELOW_LAST + BELOW_FIRST
ABOVE = ABOVE_LAST + ABOVE_FIRST
ENDS_FIRST = [(STRESS + YY, 0, 0)] + [(f, 0, -1) for f in (STRESS + XY, STRESS + YY, STRESS + YZ, VEL + 1, BUOY)]
ENDS_LAST = [(f, 3, 0) for f in (STRESS + XX, STRESS + XY, STRESS + XZ, STRESS + YY, VEL, BUOY)]
ENDS_LAST += [(STRESS + XY, 3, -1), (STRESS + YZ, 3, -1)]
ENDS_MAP = 8
LONGEST = max(len(LAST), len(FIRST))
ROWS = 32
EXT = ROWS + 8
LANES = 128
BLOCK = FIELDS * 8 + 8
CORNER = -(-(max(len(BELOW), len(ABOVE)) + 1) // 16) * 16


def pair_near(i):
    return i ^ 1


def pair_far(i, n):
    return (i - 1) % n if i % 2 == 0 else (i + 1) % n


def is_merged(n):
    return n == 2 * PY


def sides_of(n):
    return [PY] if is_merged(n) else [-PY, PY]


def tile_offsets(n):
    return [k for o in [0] + sides_of(n) for k in (o, o + 1, o - 1)]


def tile_chunk(n):
    return -(-(9 + 7 * len(sides_of(n))) // 16) * 16


def roll(x, by, axis):
    size = x.shape[axis]
    by = by % size
    return x if by == 0 else pltpu.roll(x, by, axis)


def sublane(shape):
    return lax.broadcasted_iota(jnp.int32, shape, 0)


def lane(shape):
    return lax.broadcasted_iota(jnp.int32, shape, 1)


def place_sources(into, index, wave, step, count):
    into[...] = jnp.zeros_like(into)
    lanes = lane((1, LANES))
    for e in range(count):
        cell = index[e]
        row = lax.shift_right_logical(cell, 7)
        strength = jnp.broadcast_to(wave[step : step + 1, e : e + 1], (1, LANES))
        here = jnp.where(lanes == (cell & (LANES - 1)), strength, 0.0)
        into[pl.ds(row, 1), :] = into[pl.ds(row, 1), :] + here


def pack_kernel(n, per, *refs):
    merged = is_merged(n)
    count = 7 if merged else 8
    far_refs, outs = refs[:11], refs[11 : 11 + 5 + count - 6]
    refs = refs[11 + 5 + count - 6 :]
    out_a, out_b, out_d, out_e, out_map = outs[:5]
    out_c = outs[5:]
    near_refs, sems = refs[:11], refs[11]
    held, gain, source, corner = refs[12:]
    copies = [pltpu.make_async_copy(x, y, sems.at[k]) for k, (x, y) in enumerate(zip(far_refs, near_refs))]
    for copy in copies:
        copy.start()
    dec, los, index, wave, st, mem, vel, lam, mu, bu, tiles = near_refs
    b = lax.axis_index("gx")
    even = lax.rem(b, 2) == 0
    for copy in copies[:4]:
        copy.wait()
    place_sources(source, index, wave, 0, index.shape[0])
    for copy in copies[4:6]:
        copy.wait()
    for i in range(4):
        d = dec[0, i]
        gain[i] = courant * (1.0 - (1.0 - d) * los[0, i])
        kept = courant * d
        for c in range(6):
            value = st[c, 0, i] + kept * mem[c, 0, i]
            if c < 3:
                value = value + source[i * ROWS : (i + 1) * ROWS, :]
            held[c, i] = value
    for copy in copies[6:]:
        copy.wait()

    def get(f, i, rows=slice(None)):
        if f < VEL:
            return st[f, 0, i, rows]
        if f < HELD:
            return vel[f - VEL, 0, i, rows]
        if f < GAIN:
            return held[f - HELD, i, rows]
        if f == GAIN:
            return gain[i, rows]
        return (lam, mu, bu)[f - LAME][0, i, rows]

    sub = sublane((8, LANES))
    top, bottom = slice(0, 8), slice(ROWS - 8, ROWS)

    rows_z = LANES // TZ
    table = tiles[...]
    spots = table.shape[1]
    owner = jnp.where(table >= 0, jnp.floor((table.astype(F32) + 0.5) * (1.0 / per)) + 1.0, 0.0)
    spot = lane((8, spots))
    wide = jnp.where(spot // rows_z == sublane((8, spots)), jnp.broadcast_to(owner, (8, spots)), 0.0)
    spread = (lax.rem(sublane((spots, LANES)), rows_z) == lane((spots, LANES)) // TZ).astype(BF16)
    owners = jnp.dot(wide.astype(BF16), spread, preferred_element_type=F32) - 1.0
    out_map[...] = owners
    last = ROWS // TY - 1

    def edge_rows(f):
        if f == FIELDS:
            return jnp.broadcast_to(owners[0:1], (8, LANES)), jnp.broadcast_to(owners[last : last + 1], (8, LANES))
        lo, hi = get(f, 0, top), roll(get(f, 0, bottom), 2, 0)
        for i in range(1, 4):
            mine = sub // 2 == i
            lo = jnp.where(mine, roll(get(f, i, top), 2 * i, 0), lo)
            hi = jnp.where(mine, roll(get(f, i, bottom), 2 * i + 2, 0), hi)
        return lo, hi

    for f in range(FIELDS + 1):
        lo, hi = edge_rows(f)
        out_a[f * 8 : f * 8 + 8, :] = jnp.where(even, hi, lo)
        out_b[f * 8 : f * 8 + 8, :] = jnp.where(even, lo, hi)

    def write_corner(out, rows, strip):
        corner[...] = jnp.zeros_like(corner)
        for k, (f, i, r) in enumerate(rows):
            corner[k : k + 1, :] = get(f, i, slice(r % ROWS, r % ROWS + 1))
        corner[len(rows) : len(rows) + 1, :] = owners[strip : strip + 1]
        out[...] = corner[...].astype(BF16)

    @pl.when(even)
    def _():
        write_corner(out_e, BELOW, last)
        write_corner(out_d, ABOVE, 0)

    @pl.when(jnp.logical_not(even))
    def _():
        write_corner(out_e, ABOVE, 0)
        write_corner(out_d, BELOW, last)

    def write_layers(out, which, rest, ends):
        for k, (f, i) in enumerate(which):
            out[k * ROWS : (k + 1) * ROWS, :] = get(f, i).astype(BF16)
        if rest:
            out[len(which) * ROWS : (len(which) + rest) * ROWS, :] = jnp.zeros((rest * ROWS, LANES), BF16)
        corner[0:16, :] = jnp.zeros((16, LANES), F32)
        for k, (f, i, r) in enumerate(ends):
            corner[k : k + 1, :] = get(f, i, slice(r % ROWS, r % ROWS + 1))
        corner[ENDS_MAP : ENDS_MAP + last + 1, :] = owners[0 : last + 1]
        base = (len(which) + rest) * ROWS
        out[base : base + 16, :] = corner[0:16, :].astype(BF16)

    if merged:

        @pl.when(b < PY)
        def _():
            write_layers(out_c[0], LAST, LONGEST - len(LAST), ENDS_FIRST)

        @pl.when(b >= PY)
        def _():
            write_layers(out_c[0], FIRST, LONGEST - len(FIRST), ENDS_LAST)
    else:
        write_layers(out_c[0], LAST, 0, [])
        write_layers(out_c[1], FIRST, 0, [])


def route_kernel(n, after, t_lam, t_mu, t_bu, dest, out, near_lam, near_mu, near_bu, near_dest, rows, sems):
    pairs = ((t_lam, near_lam), (t_mu, near_mu), (t_bu, near_bu), (dest, near_dest))
    copies = [pltpu.make_async_copy(x, y, sems.at[k]) for k, (x, y) in enumerate(pairs)]
    for copy in copies:
        copy.start()
    for copy in copies:
        copy.wait()
    offsets = tile_offsets(n)
    chunk = tile_chunk(n)
    per = t_lam.shape[0]
    total = n * len(offsets)
    at = lane((1, per))
    stored = jnp.full((1, per), -1, jnp.int32)
    for t in range(per):
        stored = jnp.where(at == t, near_dest[t], stored)
    row = sublane((total, per))
    brick = lax.rem(row, n)
    for k, off in enumerate(offsets):
        brick = jnp.where(row // n == k, brick + off % n, brick)
    brick = jnp.where(brick >= n, brick - n, brick)
    route = (brick == stored).astype(BF16)
    cell, spot = sublane((2 * LANES, LANES)), lane((2 * LANES, LANES))
    half = lax.rem(spot, 64)
    cells = half // 16 * 64 + lax.rem(half, 16)
    low = jnp.logical_and(spot < 64, cell == cells).astype(BF16)
    high = jnp.logical_and(spot >= 64, cell == cells + 48).astype(BF16)
    left = lane((n, LANES)) < 64
    if chunk > 9 + 7 * len(sides_of(n)):
        rows[...] = jnp.zeros_like(rows)

    def put(j, value):
        rows[pl.ds(j, n, stride=chunk), :] = value

    for p, near in enumerate((near_lam, near_mu, near_bu)):
        tile = near[...]
        whole = jnp.dot(route, tile, preferred_element_type=F32)
        first = jnp.dot(route, jnp.dot(tile, low, preferred_element_type=F32).astype(BF16), preferred_element_type=F32)
        final = jnp.dot(route, jnp.dot(tile, high, preferred_element_type=F32).astype(BF16), preferred_element_type=F32)

        def slot(x, k):
            return x[k * n : (k + 1) * n]

        put(2 * p, slot(whole, 0)[:, :LANES])
        put(2 * p + 1, slot(whole, 0)[:, LANES:])
        put(6 + p, slot(first, 1) + slot(final, 2))
        for g in range(len(sides_of(n))):
            side = slot(whole, 3 + 3 * g)
            base = 9 + 7 * g
            if p < 2:
                put(base + p, jnp.where(left, side[:, :LANES], side[:, LANES:]))
            else:
                put(base + 2, side[:, :LANES])
                put(base + 3, side[:, LANES:])
            put(base + 4 + p, slot(first, 4 + 3 * g) + slot(final, 5 + 3 * g))
    out[...] = rows[...].astype(BF16)


def wave_kernel(n, *refs):
    merged = is_merged(n)
    (vel, st, mem, lam, mu, bu, dec, los, index, wave, maps, got_a, got_b, got_t) = refs[:14]
    refs = refs[14:]
    sides = len(sides_of(n))
    got_c, got_d, got_e = refs[:sides], refs[sides : 2 * sides], refs[2 * sides : 3 * sides]
    new_v, new_s, new_m, source, rows_t, spread_rows, tile_rows, near_rows, far_rows, end_rows = refs[3 * sides :]
    b = lax.axis_index("gx")
    even = lax.rem(b, 2) == 0
    first_x = b < PY
    chunk = tile_chunk(n)
    sub = sublane((8, LANES))

    def halo_blocks(near, far, f):
        x = near[f * 8 : f * 8 + 8, :]
        y = far[f * 8 : f * 8 + 8, :]
        return jnp.where(even, x, y), jnp.where(even, y, x)

    def halo_rows(blocks, i):
        after, before = blocks
        return jnp.where(sub < 2, roll(after, -2 * i, 0), roll(before, 6 - 2 * i, 0))

    rows_t[...] = got_t[...].astype(F32)
    col = lane((16, LANES))
    line = sublane((16, LANES))
    on_line = col // TZ == line
    spread = (lax.rem(sublane((LANES, LANES)), TZ) == lax.rem(lane((LANES, LANES)), TZ)).astype(BF16)

    def overlay(row, halves, wanted):
        def take(first, values):
            for s in range(16):
                for h in range(halves):
                    value = rows_t[pl.ds((first + s) * chunk + row + h, 1), :]
                    value = jnp.where(on_line, jnp.broadcast_to(value, (16, LANES)), 0.0)
                    at = (s * halves + h) * 16
                    spread_rows[at : at + 16, :] = value.astype(BF16)
            size = 16 * halves * 16
            tile_rows[0:size, :] = jnp.dot(spread_rows[0:size, :], spread, preferred_element_type=F32)
            done = []
            for value, (_, owner, at) in zip(values, wanted):
                for s in range(16):
                    here = tile_rows[s * halves * 16 + at : s * halves * 16 + at + 8, :]
                    value = jnp.where(owner == (first + s) * 1.0, here, value)
                done.append(value)
            return done

        values = [w[0] for w in wanted]
        if n == 16:
            return take(0, values)
        return lax.fori_loop(0, n // 16, lambda g, v: take(g * 16, v), values)

    column = {}
    rows_y = ROWS // TY

    def own(f, i):
        if f < VEL:
            return st[f, 0, i]
        if f < HELD:
            return vel[f - VEL, 0, i]
        if f < GAIN:
            value = st[f - HELD, 0, i] + courant * dec[0, i] * mem[f - HELD, 0, i]
            if f < HELD + 3:
                value = value + source[i * ROWS : (i + 1) * ROWS, :]
            return value
        if f == GAIN:
            return courant * (1.0 - (1.0 - dec[0, i]) * los[0, i])
        return (lam, mu, bu)[f - LAME][0, i]

    def main_tiles(mains, owners, row, halves, line_of):
        wanted = []
        for i, m in mains.items():
            for p in range(rows_y):
                owner = jnp.broadcast_to(owners[p : p + 1], (8, LANES))
                wanted.append((m[p * 8 : (p + 1) * 8], owner, line_of(i)))
        laid = overlay(row, halves, wanted)
        return {i: jnp.concatenate(laid[k * rows_y : (k + 1) * rows_y], 0) for k, i in enumerate(mains)}

    def halo_tiles(halos, after, before, row):
        zeros = jnp.zeros((8, LANES), F32)
        blocks = overlay(row, 1, [(zeros, after, 0), (zeros, before, 8)])
        covered = jnp.where(sub < 4, after, before) >= 0.0
        return {i: jnp.where(covered, halo_rows(blocks, i), h) for i, h in halos.items()}

    place_sources(source, index, wave, 0, index.shape[0])
    after, before = halo_blocks(got_a, got_b, FIELDS)
    for f in range(FIELDS):
        blocks = halo_blocks(got_a, got_b, f)
        main = {i: own(f, i) for i in range(4)}
        halo = {i: halo_rows(blocks, i) for i in range(4)}
        if f >= LAME:
            p = f - LAME
            main = main_tiles(main, maps[...], 2 * p, 2, lambda i: i * 8)
            halo = halo_tiles(halo, after, before, 6 + p)
        for i in range(4):
            column["own", f, i] = jnp.concatenate([main[i], halo[i]], 0)

    def corner_rows(table, rows, f, i, far_edge):
        value = None
        for k, (g, j, r) in enumerate(rows):
            if (g, j) == (f, i):
                row = jnp.broadcast_to(table[k : k + 1, :], (8, LANES))
                value = jnp.where(sub == (r % 8), row, 0.0 if value is None else value)
        return value

    for side, (name, which) in enumerate((("before", LAST), ("after", FIRST))):
        group = 0 if merged else side
        message = got_c[group]
        base = (LONGEST if merged else len(which)) * ROWS
        if merged:
            whole = first_x if name == "after" else jnp.logical_not(first_x)
        if group == side:
            near, far = got_e[group][...].astype(F32), got_d[group][...].astype(F32)
            near_rows[...] = jnp.where(even, near, far)
            far_rows[...] = jnp.where(even, far, near)
            end_rows[...] = message[base : base + 16, :].astype(F32)
        ends = ENDS_LAST if name == "before" else ENDS_FIRST
        after = jnp.broadcast_to(near_rows[len(ABOVE) : len(ABOVE) + 1, :], (8, LANES))
        before = jnp.broadcast_to(far_rows[len(BELOW) : len(BELOW) + 1, :], (8, LANES))
        owners = end_rows[ENDS_MAP : ENDS_MAP + 8, :]
        row = 9 + 7 * group
        mains, halos = {}, {}
        for k, (f, i) in enumerate(which):
            main = message[k * ROWS : (k + 1) * ROWS, :].astype(F32)
            if merged:
                only = [jnp.zeros((8, LANES), F32) for _ in range(rows_y)]
                for e, (g, j, r) in enumerate(ends):
                    if (g, j) == (f, i):
                        at = r % ROWS
                        line_rows = jnp.broadcast_to(end_rows[e : e + 1, :], (8, LANES))
                        only[at // 8] = jnp.where(sub == at % 8, line_rows, only[at // 8])
                main = jnp.where(whole, main, jnp.concatenate(only, 0))
            mains[f, i] = main
            above = corner_rows(near_rows, ABOVE, f, i, False)
            below = corner_rows(far_rows, BELOW, f, i, True)
            if above is None and below is None:
                halos[f, i] = jnp.zeros((8, LANES), F32)
            elif above is None or below is None:
                halos[f, i] = below if above is None else above
            else:
                halos[f, i] = jnp.where(sub < 4, above, below)
        for f in range(FIELDS):
            layers = sorted(i for g, i in which if g == f)
            main = {i: mains[f, i] for i in layers}
            halo = {i: halos[f, i] for i in layers}
            if f == BUOY:
                main = main_tiles(main, owners, row + 2, 2, lambda i: i * 8)
            elif f >= LAME:
                main = main_tiles(main, owners, row + f - LAME, 1, lambda i: 8 if i else 0)
            if f >= LAME:
                halo = halo_tiles(halo, after, before, row + 4 + f - LAME)
            for i in layers:
                column[name, f, i] = jnp.concatenate([main[i], halo[i]], 0)

    def layers_of(f):
        names = [("before", 2), ("before", 3)] + [("own", i) for i in range(4)] + [("after", 0), ("after", 1)]
        return [column.get((name, f, i)) for name, i in names]

    s0 = [layers_of(STRESS + c) for c in range(6)]
    v0 = [layers_of(VEL + c) for c in range(3)]
    held = [layers_of(HELD + c) for c in range(6)]
    gain, lame, shear, buoy = (layers_of(f) for f in (GAIN, LAME, MU, BUOY))

    tall = sublane((EXT, LANES))
    wide = lane((EXT, LANES))

    def linked(test):
        def of(step):
            q = lax.rem(b + step + n, n)
            return jnp.where(test(q), 1, 0)

        flags = jnp.where(tall < ROWS, of(0), jnp.where(tall < ROWS + 4, of(1), of(-1)))
        return flags == 1

    link_before = linked(lambda q: q >= PY)
    link_after = linked(lambda q: q < n - PY)

    def x_next(a, l):
        if l == 1:
            return jnp.where(link_before, a[2], 0.0)
        if l == 5:
            return jnp.where(link_after, a[6], 0.0)
        return a[l + 1]

    def x_prev(a, l):
        if l == 2:
            return jnp.where(link_before, a[1], 0.0)
        if l == 6:
            return jnp.where(link_after, a[5], 0.0)
        return a[l - 1]

    def y_next(a):
        return roll(a, -1, 0)

    def y_prev(a):
        return roll(a, 1, 0)

    def z_next(a):
        return jnp.where(wide == LANES - 1, 0.0, roll(a, -1, 1))

    def z_prev(a):
        return jnp.where(wide == 0, 0.0, roll(a, 1, 1))

    def move(v, s, spans):
        new = [[None] * 8 for _ in range(3)]
        for l in spans[0]:
            grad = (x_next(s[XX], l) - s[XX][l]) + (s[XY][l] - y_prev(s[XY][l])) + (s[XZ][l] - z_prev(s[XZ][l]))
            new[0][l] = v[0][l] + courant * buoy[l] * grad
        for l in spans[1]:
            grad = (s[XY][l] - x_prev(s[XY], l)) + (y_next(s[YY][l]) - s[YY][l]) + (s[YZ][l] - z_prev(s[YZ][l]))
            new[1][l] = v[1][l] + courant * buoy[l] * grad
            grad = (s[XZ][l] - x_prev(s[XZ], l)) + (s[YZ][l] - y_prev(s[YZ][l])) + (z_next(s[ZZ][l]) - s[ZZ][l])
            new[2][l] = v[2][l] + courant * buoy[l] * grad
        return new

    def rates_at(v, l, wanted):
        out = [None] * 6
        ex = v[0][l] - x_prev(v[0], l)
        ey = v[1][l] - y_prev(v[1][l])
        ez = v[2][l] - z_prev(v[2][l])
        spread_part = lame[l] * (ex + ey + ez)
        twice = 2.0 * shear[l]
        for c, e in ((XX, ex), (YY, ey), (ZZ, ez)):
            if c in wanted:
                out[c] = spread_part + twice * e
        if XY in wanted:
            out[XY] = shear[l] * ((y_next(v[0][l]) - v[0][l]) + (x_next(v[1], l) - v[1][l]))
        if XZ in wanted:
            out[XZ] = shear[l] * ((z_next(v[0][l]) - v[0][l]) + (x_next(v[2], l) - v[2][l]))
        if YZ in wanted:
            out[YZ] = shear[l] * ((z_next(v[1][l]) - v[1][l]) + (y_next(v[2][l]) - v[2][l]))
        return out

    v1 = move(v0, s0, (range(0, 7), range(1, 8)))
    s1 = [[None] * 8 for _ in range(6)]
    m1 = {}
    for l in range(1, 7):
        wanted = (XX, XY, XZ) if l == 1 else range(6)
        rates = rates_at(v1, l, wanted)
        for c in wanted:
            s1[c][l] = held[c][l] + gain[l] * rates[c]
            if 2 <= l < 6:
                d = dec[0, l - 2]
                m1[c, l] = d * mem[c, 0, l - 2] - (1.0 - d) * los[0, l - 2] * rates[c][:ROWS]
    v2 = move(v1, s1, (range(1, 6), range(2, 7)))
    place_sources(source, index, wave, 1, index.shape[0])
    for l in range(2, 6):
        i = l - 2
        rates = rates_at(v2, l, range(6))
        d = dec[0, i]
        lost = (1.0 - d) * los[0, i]
        for c in range(3):
            new_v[c, 0, i] = v2[c][l][:ROWS]
        for c in range(6):
            rate = rates[c][:ROWS]
            m2 = d * m1[c, l] - lost * rate
            new_m[c, 0, i] = m2
            value = s1[c][l][:ROWS] + courant * (rate + m2)
            if c < 3:
                value = value + source[i * ROWS : (i + 1) * ROWS, :]
            new_s[c, 0, i] = value


def body(
    velocity,
    stress,
    memory,
    lame_lambda,
    lame_mu,
    buoyancy,
    decay,
    loss,
    tile_lambda,
    tile_mu,
    tile_buoy,
    tile_dest,
    brick_tiles,
    src_index,
    src_wave,
):
    n = lax.axis_size("gx")
    merged = is_merged(n)
    sides = sides_of(n)
    on_core = pl.BlockSpec(memory_space=pltpu.VMEM)
    scalars = pl.BlockSpec(memory_space=pltpu.SMEM)
    away = pl.BlockSpec(memory_space=pltpu.HBM)
    waves = src_wave.T
    fields = (velocity, stress, memory, lame_lambda, lame_mu, buoyancy, decay, loss)
    if merged:
        c_rows = [LONGEST * ROWS + 16]
    else:
        c_rows = [len(LAST) * ROWS + 16, len(FIRST) * ROWS + 16]
    inputs = (decay, loss, src_index, waves, stress, memory, velocity, lame_lambda, lame_mu, buoyancy, brick_tiles)
    packed = pl.pallas_call(
        functools.partial(pack_kernel, n, tile_lambda.shape[0]),
        out_shape=[
            jax.ShapeDtypeStruct((BLOCK, LANES), F32),
            jax.ShapeDtypeStruct((BLOCK, LANES), F32),
            jax.ShapeDtypeStruct((CORNER, LANES), BF16),
            jax.ShapeDtypeStruct((CORNER, LANES), BF16),
            jax.ShapeDtypeStruct((8, LANES), F32),
        ]
        + [jax.ShapeDtypeStruct((r, LANES), BF16) for r in c_rows],
        in_specs=[away] * len(inputs),
        out_specs=[on_core] * (5 + len(c_rows)),
        scratch_shapes=[
            pltpu.SMEM(x.shape, x.dtype) if x is src_index else pltpu.VMEM(x.shape, x.dtype) for x in inputs
        ]
        + [
            pltpu.SemaphoreType.DMA((len(inputs),)),
            pltpu.VMEM((6, 4, ROWS, LANES), F32),
            pltpu.VMEM((4, ROWS, LANES), F32),
            pltpu.VMEM((4 * ROWS, LANES), F32),
            pltpu.VMEM((CORNER, LANES), F32),
        ],
        compiler_params=pltpu.CompilerParams(vmem_limit_bytes=56 * 1024 * 1024),
        name="pack",
    )(*inputs)
    out_a, out_b, out_d, out_e, own_map = packed[:5]
    out_c = packed[5:]
    chunk = tile_chunk(n)
    tiles = (tile_lambda, tile_mu, tile_buoy)
    out_t = pl.pallas_call(
        functools.partial(route_kernel, n),
        out_shape=jax.ShapeDtypeStruct((n * chunk, LANES), BF16),
        in_specs=[pl.BlockSpec(memory_space=pl.ANY)] + [away] * 4,
        out_specs=on_core,
        scratch_shapes=[pltpu.VMEM(x.shape, x.dtype) for x in tiles]
        + [
            pltpu.SMEM(tile_dest.shape, tile_dest.dtype),
            pltpu.VMEM((n * chunk, LANES), F32),
            pltpu.SemaphoreType.DMA((4,)),
        ],
        compiler_params=pltpu.CompilerParams(vmem_limit_bytes=40 * 1024 * 1024),
        name="route",
    )(own_map, *tiles, tile_dest)

    def permute(array, source_of):
        return lax.ppermute(array, "gx", [(source_of(i), i) for i in range(n)])

    got_c = [permute(c, lambda i, o=o: (i + o) % n) for c, o in zip(out_c, sides)]
    got_d = [permute(out_d, lambda i, o=o: pair_far((i + o) % n, n)) for o in sides]
    got_e = [permute(out_e, lambda i, o=o: pair_near((i + o) % n)) for o in sides]
    got_b = permute(out_b, lambda i: pair_far(i, n))
    got_a = permute(out_a, pair_near)
    got_t = lax.all_to_all(out_t, "gx", split_axis=0, concat_axis=0, tiled=True)

    return pl.pallas_call(
        functools.partial(wave_kernel, n),
        out_shape=[
            jax.ShapeDtypeStruct(velocity.shape, F32),
            jax.ShapeDtypeStruct(stress.shape, F32),
            jax.ShapeDtypeStruct(memory.shape, F32),
        ],
        in_specs=[on_core] * 8 + [scalars] + [on_core] * (5 + 3 * len(sides)),
        out_specs=[on_core] * 3,
        scratch_shapes=[
            pltpu.VMEM((4 * ROWS, LANES), F32),
            pltpu.VMEM((n * chunk, LANES), F32),
            pltpu.VMEM((16 * 32, LANES), BF16),
            pltpu.VMEM((16 * 32, LANES), F32),
            pltpu.VMEM((CORNER, LANES), F32),
            pltpu.VMEM((CORNER, LANES), F32),
            pltpu.VMEM((16, LANES), F32),
        ],
        compiler_params=pltpu.CompilerParams(vmem_limit_bytes=48 * 1024 * 1024),
        name="wave",
    )(*fields, src_index, waves, own_map, got_a, got_b, got_t, *got_c, *got_d, *got_e)


def solution(mesh):
    split = ("groups", "gx")
    whole = P(None, split, None, None, None)
    field = P(split, None, None, None)
    return jax.shard_map(
        body,
        mesh=mesh,
        in_specs=(whole,) * 3
        + (field,) * 5
        + (P(split, None),) * 3
        + (P(split), P(split, None), P(split), P(split, None)),
        out_specs=(whole,) * 3,
        check_vma=False,
    )
```

time: 47.2 us -> 26.3 us (0.56)
  the two profiles are of different devices: /device:TPU:1 before, /device:TPU:0 now
where the time goes in v2:
time: 26.3 us; the launch traced here: 26 us
  starting transfers between devices  13 us (49%)
  Pallas kernels  7.25 us (28%)
  waiting for transfers between devices  4.02 us (15%)
  between operations  0.92 us (3%)
  local copies, waits for them, and re-layouts  0.75 us (3%)
    ppermute x5, starting transfers between devices, permute(): return lax.ppermute(array, 'gx', [(source_of(i), i) for i in range(n)])  8.98 us
    all_to_all x1, starting transfers between devices, body(): got_t = lax.all_to_all(out_t, 'gx', split_axis=0, concat_axis=0, tiled=True)  4.06 us
    ppermute x5, waiting for transfers between devices, permute(): return lax.ppermute(array, 'gx', [(source_of(i), i) for i in range(n)])  4.01 us
    pallas_call x1, Pallas kernels, body(): pl.pallas_call(functools.partial(wave_kernel, n), out_shape=[jax.ShapeDty...  3.08 us
    pallas_call x1, Pallas kernels, body(): pl.pallas_call(functools.partial(pack_kernel, n, tile_lambda.shape[0]), o...  2.36 us
    pallas_call x1, Pallas kernels, body(): pl.pallas_call(functools.partial(route_kernel, n), out_shape=jax.ShapeDty...  1.81 us
    unnamed x36, local copies, waits for them, and re-layouts  0.75 us
  transfers between devices with their start and end apart: 6, of which 2 were waited for; matrix products, arithmetic and copies ran while one was open for 0% of the time, Pallas kernels for 7%

profile of v2, /device:TPU:0, one launch (start us, length us, event | category | flops | bytes accessed | tf_op | source)
XLA Modules:
  0.0 26.0 jit_solution(232434331045413143)
XLA Ops:
  0.6 0.0 copy-start.11
  0.6 0.0 copy-start.12
  0.7 0.0 copy-start.13
  0.7 0.0 copy-start.15
  0.7 0.0 copy-start
  0.7 0.0 copy-start.1
  0.7 0.0 copy-start.3
  0.7 0.0 copy-start.4
  0.7 0.0 copy-start.5
  0.7 0.0 copy-start.6
  0.7 0.0 copy-start.7
  0.7 2.4 %pack.1 = (f32[160,128]{1,0:T(8,128)}, f32[160,128]{1,0:T(8,128)}, bf16[48,128]{1,0:T(8,128)(2,1)}, bf16[48,128]{1,0:T(8,128)(2,1)}, f32[8,128]{1,0:T(8,128)}, /*index=5*/bf16[912,128]{1,0:T(8,128)(2,1)}) custom-call(f32[1,4,32,128]{3,2,1,0:T(8,128)} %refs_6_.3, f32[1,4,32,128]{3,2,1,0:T(8,128)} %refs_7_.3, s32[16]{0:T(128)} %refs_8_.3, f32[2,16]{1,0:T(2,128)} %bitcast.4, ...), custom_call_target="tpu_custom_call" | custom-call | tf_op jit(solution)/shard_map/pack/pallas_call | solution.py:562
  3.1 0.0 copy-start.2
  3.1 4.1 %collective-permute-start.2 = (bf16[912,128]{1,0:T(8,128)(2,1)}, bf16[912,128]{1,0:T(8,128)(2,1)S(1)}, u32[]{:S(2)}, u32[]{:S(2)}) collective-permute-start(bf16[912,128]{1,0:T(8,128)(2,1)} %get-tuple-element.12), channel_id=1, source_target_pairs={{8,0},{9,1},{10,2},{11,3},{12,4},{13,5},{14,6},{15,7},{0,8},{1,9},... | collective-permute-start | bytes 700424 | tf_op jit(solution)/shard_map/ppermute | solution.py:607
  7.2 0.0 copy-done.11
  7.2 0.0 copy-done.12
  7.2 0.0 copy-done.13
  7.2 0.0 copy-done.15
  7.2 0.0 copy-start.8
  7.3 0.7 %copy-done.8 = f32[8,128]{1,0:T(8,128)S(1)} copy-done((f32[8,128]{1,0:T(8,128)S(1)}, f32[8,128]{1,0:T(8,128)}, u32[]{:S(2)}) %copy-start.8) | copy-done | bytes 4120
  7.9 1.8 %route.1 = bf16[256,128]{1,0:T(8,128)(2,1)} custom-call(f32[8,128]{1,0:T(8,128)S(1)} %copy-done.8, bf16[8,256]{1,0:T(8,128)(2,1)S(1)} %copy-done.11, bf16[8,256]{1,0:T(8,128)(2,1)S(1)} %copy-done.12, bf16[8,256]{1,0:T(8,128)(2,1)S(1)} %copy-done.13, s32[8]{0:T(128)S(1)} %copy-done.15), custom_call_target="tpu_custom_call" | custom-call | tf_op jit(solution)/shard_map/route/pallas_call | solution.py:591
  9.7 0.0 copy-start.17
  9.8 0.0 copy-start.16
  9.8 4.1 %all-to-all-start = ((bf16[16,16,128]{2,1,0:T(8,128)(2,1)}), bf16[16,16,128]{2,1,0:T(8,128)(2,1)S(1)}, u32[]{:S(2)}, u32[]{:S(2)}) async-start(bf16[16,16,128]{2,1,0:T(8,128)(2,1)} %bitcast.1), calls=%async_computation | async-start | bytes 131072 | tf_op jit(solution)/shard_map/all_to_all | solution.py:614
  13.8 0.0 copy-start.9
  13.8 0.5 %collective-permute-start = (f32[160,128]{1,0:T(8,128)}, f32[160,128]{1,0:T(8,128)S(1)}, u32[]{:S(2)}, u32[]{:S(2)}) collective-permute-start(f32[160,128]{1,0:T(8,128)} %get-tuple-element.10), channel_id=1, source_target_pairs={{1,0},{0,1},{3,2},{2,3},{5,4},{4,5},{7,6},{6,7},{9,8},{8,9},{11,10... | collective-permute-start | bytes 245768 | tf_op jit(solution)/shard_map/ppermute | solution.py:607
  14.3 4.3 %collective-permute-start.1 = (f32[160,128]{1,0:T(8,128)}, f32[160,128]{1,0:T(8,128)S(1)}, u32[]{:S(2)}, u32[]{:S(2)}) collective-permute-start(f32[160,128]{1,0:T(8,128)} %get-tuple-element.11), channel_id=1, source_target_pairs={{15,0},{2,1},{1,2},{4,3},{3,4},{6,5},{5,6},{8,7},{7,8},{10,9},{9,1... | collective-permute-start | bytes 245768 | tf_op jit(solution)/shard_map/ppermute | solution.py:607
  18.6 0.0 copy-done.17
  18.6 0.0 collective-permute-start.3
  18.6 0.0 copy-done.16
  18.7 0.0 copy-start.10
  18.7 0.0 copy-start.14
  18.7 0.1 collective-permute-start.4
  18.8 3.9 %collective-permute-done.3.refs_15_ = bf16[48,128]{1,0:T(8,128)(2,1)S(1)} collective-permute-done((bf16[48,128]{1,0:T(8,128)(2,1)S(1)}, bf16[48,128]{1,0:T(8,128)(2,1)S(1)}, u32[]{:S(2)}, u32[]{:S(2)}) %collective-permute-start.3) | collective-permute-done | bytes 12320 | tf_op jit(solution)/shard_map/ppermute | solution.py:607
  22.7 0.1 collective-permute-done.4.refs_16_
  22.8 0.0 collective-permute-done.refs_11_
  22.8 0.0 collective-permute-done.1.refs_12_
  22.8 0.0 all-to-all-done
  22.8 0.0 collective-permute-done.2.refs_14_
  22.8 0.0 copy-done
  22.8 0.0 copy-done.1
  22.8 0.0 copy-done.3
  22.8 0.0 copy-done.4
  22.8 0.0 copy-done.5
  22.8 0.0 copy-done.6
  22.8 0.0 copy-done.7
  22.9 0.0 copy-done.2
  22.9 0.0 copy-done.9
  22.9 0.0 copy-done.10
  22.9 0.0 copy-done.14
  22.9 3.1 %wave.1 = (f32[3,1,4,32,128]{4,3,2,1,0:T(8,128)}, f32[6,1,4,32,128]{4,3,2,1,0:T(8,128)}, f32[6,1,4,32,128]{4,3,2,1,0:T(8,128)}) custom-call(f32[3,1,4,32,128]{4,3,2,1,0:T(8,128)S(1)} %copy-done.2, f32[6,1,4,32,128]{4,3,2,1,0:T(8,128)S(1)} %copy-done, f32[6,1,4,32,128]{4,3,2,1,0:T(8,128)S(1)} %copy-done.1, f32[1,4,32,128]{3,2,1,0:T(8,128)S(1)} %copy-done.3, ...), custom_call_target="tpu_custom_call" | custom-call | tf_op jit(solution)/shard_map/wave/pallas_call | solution.py:616
Async XLA Ops:
  0.6 6.6 %copy-start.11 = (bf16[8,256]{1,0:T(8,128)(2,1)S(1)}, bf16[8,256]{1,0:T(8,128)(2,1)}, u32[]{:S(2)}) copy-start(bf16[8,256]{1,0:T(8,128)(2,1)} %t_lam.1) | copy-start | bytes 12292
  0.6 6.6 %copy-start.12 = (bf16[8,256]{1,0:T(8,128)(2,1)S(1)}, bf16[8,256]{1,0:T(8,128)(2,1)}, u32[]{:S(2)}) copy-start(bf16[8,256]{1,0:T(8,128)(2,1)} %t_mu.1) | copy-start | bytes 12292
  0.7 6.6 %copy-start.13 = (bf16[8,256]{1,0:T(8,128)(2,1)S(1)}, bf16[8,256]{1,0:T(8,128)(2,1)}, u32[]{:S(2)}) copy-start(bf16[8,256]{1,0:T(8,128)(2,1)} %t_bu.1) | copy-start | bytes 12292
  0.7 6.6 %copy-start.15 = (s32[8]{0:T(128)S(1)}, s32[8]{0:T(128)}, u32[]{:S(2)}) copy-start(s32[8]{0:T(128)} %dest.1) | copy-start | bytes 100
  0.7 22.1 %copy-start = (f32[6,1,4,32,128]{4,3,2,1,0:T(8,128)S(1)}, f32[6,1,4,32,128]{4,3,2,1,0:T(8,128)}, u32[]{:S(2)}) copy-start(f32[6,1,4,32,128]{4,3,2,1,0:T(8,128)} %refs_1_.3) | copy-start | bytes 1179652
  0.7 22.1 %copy-start.1 = (f32[6,1,4,32,128]{4,3,2,1,0:T(8,128)S(1)}, f32[6,1,4,32,128]{4,3,2,1,0:T(8,128)}, u32[]{:S(2)}) copy-start(f32[6,1,4,32,128]{4,3,2,1,0:T(8,128)} %refs_2_.3) | copy-start | bytes 1179652
  0.7 22.1 %copy-start.3 = (f32[1,4,32,128]{3,2,1,0:T(8,128)S(1)}, f32[1,4,32,128]{3,2,1,0:T(8,128)}, u32[]{:S(2)}) copy-start(f32[1,4,32,128]{3,2,1,0:T(8,128)} %refs_3_.1) | copy-start | bytes 196612
  0.7 22.1 %copy-start.4 = (f32[1,4,32,128]{3,2,1,0:T(8,128)S(1)}, f32[1,4,32,128]{3,2,1,0:T(8,128)}, u32[]{:S(2)}) copy-start(f32[1,4,32,128]{3,2,1,0:T(8,128)} %refs_4_.3) | copy-start | bytes 196612
  0.7 22.1 %copy-start.5 = (f32[1,4,32,128]{3,2,1,0:T(8,128)S(1)}, f32[1,4,32,128]{3,2,1,0:T(8,128)}, u32[]{:S(2)}) copy-start(f32[1,4,32,128]{3,2,1,0:T(8,128)} %refs_5_.3) | copy-start | bytes 196612
  0.7 22.1 %copy-start.6 = (f32[1,4,32,128]{3,2,1,0:T(8,128)S(1)}, f32[1,4,32,128]{3,2,1,0:T(8,128)}, u32[]{:S(2)}) copy-start(f32[1,4,32,128]{3,2,1,0:T(8,128)} %refs_6_.3) | copy-start | bytes 196612
  0.7 22.1 %copy-start.7 = (f32[1,4,32,128]{3,2,1,0:T(8,128)S(1)}, f32[1,4,32,128]{3,2,1,0:T(8,128)}, u32[]{:S(2)}) copy-start(f32[1,4,32,128]{3,2,1,0:T(8,128)} %refs_7_.3) | copy-start | bytes 196612
  3.1 19.7 %copy-start.2 = (f32[3,1,4,32,128]{4,3,2,1,0:T(8,128)S(1)}, f32[3,1,4,32,128]{4,3,2,1,0:T(8,128)}, u32[]{:S(2)}) copy-start(f32[3,1,4,32,128]{4,3,2,1,0:T(8,128)} %refs_0_.3) | copy-start | bytes 589828
  3.1 19.7 %collective-permute-start.2 = (bf16[912,128]{1,0:T(8,128)(2,1)}, bf16[912,128]{1,0:T(8,128)(2,1)S(1)}, u32[]{:S(2)}, u32[]{:S(2)}) collective-permute-start(bf16[912,128]{1,0:T(8,128)(2,1)} %get-tuple-element.12), channel_id=1, source_target_pairs={{8,0},{9,1},{10,2},{11,3},{12,4},{13,5},{14,6},{15,7},{0,8},{1,9},... | collective-permute-start | bytes 700424 | tf_op jit(solution)/shard_map/ppermute | solution.py:607
  7.2 0.7 %copy-start.8 = (f32[8,128]{1,0:T(8,128)S(1)}, f32[8,128]{1,0:T(8,128)}, u32[]{:S(2)}) copy-start(f32[8,128]{1,0:T(8,128)} %get-tuple-element.9.after.refs_10_) | copy-start | bytes 12292
  9.7 8.9 %copy-start.17 = (bf16[48,128]{1,0:T(8,128)(2,1)S(1)}, bf16[48,128]{1,0:T(8,128)(2,1)}, u32[]{:S(2)}) copy-start(bf16[48,128]{1,0:T(8,128)(2,1)} %get-tuple-element.13) | copy-start | bytes 36868
  9.8 8.9 %copy-start.16 = (bf16[48,128]{1,0:T(8,128)(2,1)S(1)}, bf16[48,128]{1,0:T(8,128)(2,1)}, u32[]{:S(2)}) copy-start(bf16[48,128]{1,0:T(8,128)(2,1)} %get-tuple-element.14) | copy-start | bytes 36868
  9.8 13.0 %all-to-all-start = ((bf16[16,16,128]{2,1,0:T(8,128)(2,1)}), bf16[16,16,128]{2,1,0:T(8,128)(2,1)S(1)}, u32[]{:S(2)}, u32[]{:S(2)}) async-start(bf16[16,16,128]{2,1,0:T(8,128)(2,1)} %bitcast.1), calls=%async_computation | async-start | bytes 131072 | tf_op jit(solution)/shard_map/all_to_all | solution.py:614
  13.8 9.0 %copy-start.9 = (f32[8,128]{1,0:T(8,128)S(1)}, f32[8,128]{1,0:T(8,128)}, u32[]{:S(2)}) copy-start(f32[8,128]{1,0:T(8,128)} %get-tuple-element.9.after.refs_10_) | copy-start | bytes 12292
  13.8 8.9 %collective-permute-start = (f32[160,128]{1,0:T(8,128)}, f32[160,128]{1,0:T(8,128)S(1)}, u32[]{:S(2)}, u32[]{:S(2)}) collective-permute-start(f32[160,128]{1,0:T(8,128)} %get-tuple-element.10), channel_id=1, source_target_pairs={{1,0},{0,1},{3,2},{2,3},{5,4},{4,5},{7,6},{6,7},{9,8},{8,9},{11,10... | collective-permute-start | bytes 245768 | tf_op jit(solution)/shard_map/ppermute | solution.py:607
  14.3 8.5 %collective-permute-start.1 = (f32[160,128]{1,0:T(8,128)}, f32[160,128]{1,0:T(8,128)S(1)}, u32[]{:S(2)}, u32[]{:S(2)}) collective-permute-start(f32[160,128]{1,0:T(8,128)} %get-tuple-element.11), channel_id=1, source_target_pairs={{15,0},{2,1},{1,2},{4,3},{3,4},{6,5},{5,6},{8,7},{7,8},{10,9},{9,1... | collective-permute-start | bytes 245768 | tf_op jit(solution)/shard_map/ppermute | solution.py:607
  18.6 4.0 %collective-permute-start.3 = (bf16[48,128]{1,0:T(8,128)(2,1)S(1)}, bf16[48,128]{1,0:T(8,128)(2,1)S(1)}, u32[]{:S(2)}, u32[]{:S(2)}) collective-permute-start(bf16[48,128]{1,0:T(8,128)(2,1)S(1)} %copy-done.17), channel_id=1, source_target_pairs={{7,0},{10,1},{9,2},{12,3},{11,4},{14,5},{13,6},{0,7},{15,8},{2,9},... | collective-permute-start | bytes 36872 | tf_op jit(solution)/shard_map/ppermute | solution.py:607
  18.7 4.2 %copy-start.10 = (f32[16,2]{0,1:T(2,128)S(1)}, f32[16,2]{0,1:T(2,128)}, u32[]{:S(2)}) copy-start(f32[16,2]{0,1:T(2,128)} %param.29) | copy-start | bytes 388
  18.7 4.2 %copy-start.14 = (s32[16]{0:T(128)S(1)}, s32[16]{0:T(128)}, u32[]{:S(2)}) copy-start(s32[16]{0:T(128)} %refs_8_.3) | copy-start | bytes 196
  18.7 4.1 %collective-permute-start.4 = (bf16[48,128]{1,0:T(8,128)(2,1)S(1)}, bf16[48,128]{1,0:T(8,128)(2,1)S(1)}, u32[]{:S(2)}, u32[]{:S(2)}) collective-permute-start(bf16[48,128]{1,0:T(8,128)(2,1)S(1)} %copy-done.16), channel_id=1, source_target_pairs={{9,0},{8,1},{11,2},{10,3},{13,4},{12,5},{15,6},{14,7},{1,8},{0,9},... | collective-permute-start | bytes 36872 | tf_op jit(solution)/shard_map/ppermute | solution.py:607

commit v3 on v2

--- a/solution.py
+++ b/solution.py
@@ -17,12 +17,12 @@
 XX, YY, ZZ, XY, XZ, YZ = range(6)
 STRESS, VEL, HELD, GAIN, LAME, MU, BUOY = 0, 6, 9, 15, 16, 17, 18
 FIELDS = 19
-LAST = [(STRESS + c, i) for c in (XX, XY, XZ) for i in (2, 3)] + [(STRESS + c, 3) for c in (YY, ZZ, YZ)]
+LAST = [("gx", 2), ("gx", 3), ("gy", 3), ("gz", 3), (STRESS + XY, 3), (STRESS + XZ, 3)]
 LAST += [(VEL, 2), (VEL, 3), (VEL + 1, 3), (VEL + 2, 3), (BUOY, 2), (BUOY, 3)]
 LAST += [(HELD + c, 3) for c in (XX, XY, XZ)] + [(GAIN, 3), (LAME, 3), (MU, 3)]
-FIRST = [(STRESS + c, i) for c in range(6) for i in (0, 1)]
+FIRST = [("gx", 0), ("gy", 0), ("gz", 0), ("gy", 1), ("gz", 1), (STRESS + XX, 0)]
 FIRST += [(VEL, 0), (VEL + 1, 0), (VEL + 1, 1), (VEL + 2, 0), (VEL + 2, 1), (BUOY, 0), (BUOY, 1)]
-FIRST += [(HELD + c, 0) for c in range(6)] + [(GAIN, 0), (LAME, 0), (MU, 0)]
+FIRST += [(HELD + XX, 0), ("hy", 0), ("hz", 0), (GAIN, 0), (LAME, 0), (MU, 0)]
 BELOW_LAST = [(STRESS + c, 3) for c in range(6) if c != ZZ] + [(VEL, 3), (VEL + 1, 3), (HELD + XY, 3), (GAIN, 3)]
 BELOW_LAST = [(f, i, -1) for f, i in BELOW_LAST + [(MU, 3), (BUOY, 3), (STRESS + XY, 2)]] + [(STRESS + XY, 3, -2)]
 ABOVE_LAST = [(STRESS + c, 3) for c in range(6)] + [(VEL, 3), (VEL + 2, 3), (HELD + XZ, 3), (GAIN, 3)]
@@ -34,10 +34,11 @@
 ABOVE_FIRST = [(f, i, 0) for f, i in ABOVE_FIRST] + [(STRESS + XX, 0, 1), (STRESS + YY, 0, 1)]
 BELOW = BELOW_LAST + BELOW_FIRST
 ABOVE = ABOVE_LAST + ABOVE_FIRST
-ENDS_FIRST = [(STRESS + YY, 0, 0)] + [(f, 0, -1) for f in (STRESS + XY, STRESS + YY, STRESS + YZ, VEL + 1, BUOY)]
-ENDS_LAST = [(f, 3, 0) for f in (STRESS + XX, STRESS + XY, STRESS + XZ, STRESS + YY, VEL, BUOY)]
-ENDS_LAST += [(STRESS + XY, 3, -1), (STRESS + YZ, 3, -1)]
-ENDS_MAP = 8
+ENDS = [(STRESS + YY, 0, 0), (STRESS + XY, 0, -1), (STRESS + YZ, 0, -1)]
+ENDS += [("gy", 0, -1), (VEL + 1, 0, -1), (BUOY, 0, -1)]
+ENDS += [(STRESS + YY, 3, 0), (STRESS + XY, 3, -1), (STRESS + YZ, 3, -1)]
+ENDS += [("gx", 3, 0), (VEL, 3, 0), (BUOY, 3, 0)]
+ENDS_MAP = 12
 LONGEST = max(len(LAST), len(FIRST))
 ROWS = 32
 EXT = ROWS + 8
@@ -82,6 +83,14 @@
 
 def lane(shape):
     return lax.broadcasted_iota(jnp.int32, shape, 1)
+
+
+def z_after(a):
+    return jnp.where(lane(a.shape) == LANES - 1, 0.0, roll(a, -1, 1))
+
+
+def z_before(a):
+    return jnp.where(lane(a.shape) == 0, 0.0, roll(a, 1, 1))
 
 
 def place_sources(into, index, wave, step, count):
@@ -97,23 +106,26 @@
 
 def pack_kernel(n, per, *refs):
     merged = is_merged(n)
-    count = 7 if merged else 8
-    far_refs, outs = refs[:11], refs[11 : 11 + 5 + count - 6]
-    refs = refs[11 + 5 + count - 6 :]
-    out_a, out_b, out_d, out_e, out_map = outs[:5]
-    out_c = outs[5:]
-    near_refs, sems = refs[:11], refs[11]
-    held, gain, source, corner = refs[12:]
+    count = 6 + len(sides_of(n))
+    far_refs, outs = refs[:15], refs[15 : 15 + count]
+    refs = refs[15 + count :]
+    out_a, out_b, out_d, out_e, out_map, out_t = outs[:6]
+    out_c = outs[6:]
+    near_refs, sems = refs[:15], refs[15]
+    held, gain, source, corner, routed = refs[16:]
     copies = [pltpu.make_async_copy(x, y, sems.at[k]) for k, (x, y) in enumerate(zip(far_refs, near_refs))]
     for copy in copies:
         copy.start()
-    dec, los, index, wave, st, mem, vel, lam, mu, bu, tiles = near_refs
+    near_lam, near_mu, near_bu, near_dest, dec, los, index, wave, st, mem, vel, lam, mu, bu, tiles = near_refs
     b = lax.axis_index("gx")
     even = lax.rem(b, 2) == 0
     for copy in copies[:4]:
         copy.wait()
+    route_tiles(n, near_lam, near_mu, near_bu, near_dest, routed, out_t)
+    for copy in copies[4:8]:
+        copy.wait()
     place_sources(source, index, wave, 0, index.shape[0])
-    for copy in copies[4:6]:
+    for copy in copies[8:10]:
         copy.wait()
     for i in range(4):
         d = dec[0, i]
@@ -124,7 +136,7 @@
             if c < 3:
                 value = value + source[i * ROWS : (i + 1) * ROWS, :]
             held[c, i] = value
-    for copy in copies[6:]:
+    for copy in copies[10:]:
         copy.wait()
 
     def get(f, i, rows=slice(None)):
@@ -152,6 +164,40 @@
     out_map[...] = owners
     last = ROWS // TY - 1
 
+    def prev_y(a):
+        return jnp.where(sublane(a.shape) == 0, 0.0, roll(a, 1, 0))
+
+    def next_y(a):
+        return jnp.where(sublane(a.shape) == ROWS - 1, 0.0, roll(a, -1, 0))
+
+    def sums(kind, i):
+        def s(c, k):
+            return held[c, k] if kind[0] == "h" else st[c, 0, k]
+
+        def dy_prev(c):
+            return s(c, i) - prev_y(s(c, i))
+
+        def dy_next(c):
+            return next_y(s(c, i)) - s(c, i)
+
+        def dz_prev(c):
+            return s(c, i) - z_before(s(c, i))
+
+        def dz_next(c):
+            return z_after(s(c, i)) - s(c, i)
+
+        if kind == "gx":
+            along = s(XX, i + 1) - s(XX, i) if i < 3 else -s(XX, i)
+            return along + dy_prev(XY) + dz_prev(XZ)
+        cross = XY if kind[1] == "y" else XZ
+        along = s(cross, i) - s(cross, i - 1) if i > 0 else s(cross, i)
+        if kind[1] == "y":
+            return along + dy_next(YY) + dz_prev(YZ)
+        return along + dy_prev(YZ) + dz_next(ZZ)
+
+    def entry(f, i):
+        return sums(f, i) if isinstance(f, str) else get(f, i)
+
     def edge_rows(f):
         if f == FIELDS:
             return jnp.broadcast_to(owners[0:1], (8, LANES)), jnp.broadcast_to(owners[last : last + 1], (8, LANES))
@@ -184,42 +230,36 @@
         write_corner(out_e, ABOVE, 0)
         write_corner(out_d, BELOW, last)
 
-    def write_layers(out, which, rest, ends):
+    def write_layers(out, which, rest):
         for k, (f, i) in enumerate(which):
-            out[k * ROWS : (k + 1) * ROWS, :] = get(f, i).astype(BF16)
+            out[k * ROWS : (k + 1) * ROWS, :] = entry(f, i).astype(BF16)
         if rest:
             out[len(which) * ROWS : (len(which) + rest) * ROWS, :] = jnp.zeros((rest * ROWS, LANES), BF16)
-        corner[0:16, :] = jnp.zeros((16, LANES), F32)
-        for k, (f, i, r) in enumerate(ends):
-            corner[k : k + 1, :] = get(f, i, slice(r % ROWS, r % ROWS + 1))
-        corner[ENDS_MAP : ENDS_MAP + last + 1, :] = owners[0 : last + 1]
         base = (len(which) + rest) * ROWS
         out[base : base + 16, :] = corner[0:16, :].astype(BF16)
 
+    for k, (f, i, r) in enumerate(ENDS):
+        row = slice(r % ROWS, r % ROWS + 1)
+        corner[k : k + 1, :] = sums(f, i)[row] if isinstance(f, str) else get(f, i, row)
+    corner[ENDS_MAP : ENDS_MAP + last + 1, :] = owners[0 : last + 1]
     if merged:
 
         @pl.when(b < PY)
         def _():
-            write_layers(out_c[0], LAST, LONGEST - len(LAST), ENDS_FIRST)
+            write_layers(out_c[0], LAST, LONGEST - len(LAST))
 
         @pl.when(b >= PY)
         def _():
-            write_layers(out_c[0], FIRST, LONGEST - len(FIRST), ENDS_LAST)
+            write_layers(out_c[0], FIRST, LONGEST - len(FIRST))
     else:
-        write_layers(out_c[0], LAST, 0, [])
-        write_layers(out_c[1], FIRST, 0, [])
-
-
-def route_kernel(n, after, t_lam, t_mu, t_bu, dest, out, near_lam, near_mu, near_bu, near_dest, rows, sems):
-    pairs = ((t_lam, near_lam), (t_mu, near_mu), (t_bu, near_bu), (dest, near_dest))
-    copies = [pltpu.make_async_copy(x, y, sems.at[k]) for k, (x, y) in enumerate(pairs)]
-    for copy in copies:
-        copy.start()
-    for copy in copies:
-        copy.wait()
+        write_layers(out_c[0], LAST, 0)
+        write_layers(out_c[1], FIRST, 0)
+
+
+def route_tiles(n, near_lam, near_mu, near_bu, near_dest, rows, out):
     offsets = tile_offsets(n)
     chunk = tile_chunk(n)
-    per = t_lam.shape[0]
+    per = near_lam.shape[0]
     total = n * len(offsets)
     at = lane((1, per))
     stored = jnp.full((1, per), -1, jnp.int32)
@@ -363,7 +403,7 @@
         for i in range(4):
             column["own", f, i] = jnp.concatenate([main[i], halo[i]], 0)
 
-    def corner_rows(table, rows, f, i, far_edge):
+    def corner_rows(table, rows, f, i):
         value = None
         for k, (g, j, r) in enumerate(rows):
             if (g, j) == (f, i):
@@ -371,6 +411,8 @@
                 value = jnp.where(sub == (r % 8), row, 0.0 if value is None else value)
         return value
 
+    no_rows, no_halo = jnp.zeros((ROWS, LANES), F32), jnp.zeros((8, LANES), F32)
+    face = {}
     for side, (name, which) in enumerate((("before", LAST), ("after", FIRST))):
         group = 0 if merged else side
         message = got_c[group]
@@ -382,43 +424,63 @@
             near_rows[...] = jnp.where(even, near, far)
             far_rows[...] = jnp.where(even, far, near)
             end_rows[...] = message[base : base + 16, :].astype(F32)
-        ends = ENDS_LAST if name == "before" else ENDS_FIRST
         after = jnp.broadcast_to(near_rows[len(ABOVE) : len(ABOVE) + 1, :], (8, LANES))
         before = jnp.broadcast_to(far_rows[len(BELOW) : len(BELOW) + 1, :], (8, LANES))
-        owners = end_rows[ENDS_MAP : ENDS_MAP + 8, :]
+        owners = end_rows[8:16, :][ENDS_MAP - 8 :]
         row = 9 + 7 * group
-        mains, halos = {}, {}
-        for k, (f, i) in enumerate(which):
+
+        def end_row(f, i, r):
+            at = ENDS.index((f, i, r))
+            return jnp.broadcast_to(end_rows[at : at + 1, :], (8, LANES))
+
+        def main_rows(f, i):
+            if (f, i) not in which:
+                return no_rows
+            k = which.index((f, i))
             main = message[k * ROWS : (k + 1) * ROWS, :].astype(F32)
-            if merged:
-                only = [jnp.zeros((8, LANES), F32) for _ in range(rows_y)]
-                for e, (g, j, r) in enumerate(ends):
-                    if (g, j) == (f, i):
-                        at = r % ROWS
-                        line_rows = jnp.broadcast_to(end_rows[e : e + 1, :], (8, LANES))
-                        only[at // 8] = jnp.where(sub == at % 8, line_rows, only[at // 8])
-                main = jnp.where(whole, main, jnp.concatenate(only, 0))
-            mains[f, i] = main
-            above = corner_rows(near_rows, ABOVE, f, i, False)
-            below = corner_rows(far_rows, BELOW, f, i, True)
-            if above is None and below is None:
-                halos[f, i] = jnp.zeros((8, LANES), F32)
-            elif above is None or below is None:
-                halos[f, i] = below if above is None else above
-            else:
-                halos[f, i] = jnp.where(sub < 4, above, below)
+            if not merged:
+                return main
+            only = [no_halo] * rows_y
+            if (f, i, 0) in ENDS[3:6] + ENDS[9:12]:
+                only[0] = jnp.where(sub == 0, end_row(f, i, 0), 0.0)
+            if (f, i, -1) in ENDS[3:6] + ENDS[9:12]:
+                only[-1] = jnp.where(sub == 7, end_row(f, i, -1), 0.0)
+            return jnp.where(whole, main, jnp.concatenate(only, 0))
+
+        def corner_halo(f, i):
+            above = corner_rows(near_rows, ABOVE, f, i)
+            below = corner_rows(far_rows, BELOW, f, i)
+            if above is None or below is None:
+                return no_halo if above is below else (below if above is None else above)
+            return jnp.where(sub < 4, above, below)
+
+        edge = 3 if name == "before" else 0
+        layers = (2, 3) if name == "before" else (0, 1)
         for f in range(FIELDS):
-            layers = sorted(i for g, i in which if g == f)
-            main = {i: mains[f, i] for i in layers}
-            halo = {i: halos[f, i] for i in layers}
+            present = [i for i in layers if f < VEL or f in range(HELD, GAIN) or (f, i) in which]
+            halo = {i: corner_halo(f, i) for i in present}
+            main = {i: no_rows if f < VEL else main_rows(f, i) for i in present}
             if f == BUOY:
                 main = main_tiles(main, owners, row + 2, 2, lambda i: i * 8)
             elif f >= LAME:
                 main = main_tiles(main, owners, row + f - LAME, 1, lambda i: 8 if i else 0)
             if f >= LAME:
                 halo = halo_tiles(halo, after, before, row + 4 + f - LAME)
-            for i in layers:
+            for i in present:
                 column[name, f, i] = jnp.concatenate([main[i], halo[i]], 0)
+            if f < VEL and (f, edge) in which:
+                face[name, f] = jnp.concatenate([main_rows(f, edge), halo[edge]], 0)
+        for f, i in which:
+            if not isinstance(f, str):
+                continue
+            halo = no_halo
+            if i == edge and f == "gx":
+                halo = jnp.where(sub == 0, -end_row(STRESS + XY, i, -1), 0.0)
+            if i == edge and f == "gy":
+                halo = jnp.where(sub == 7, end_row(STRESS + YY, i, 0), 0.0)
+            if i == edge and f == "gz":
+                halo = jnp.where(sub == 0, -end_row(STRESS + YZ, i, -1), 0.0)
+            column[name, f, i] = jnp.concatenate([main_rows(f, i), halo], 0)
 
     def layers_of(f):
         names = [("before", 2), ("before", 3)] + [("own", i) for i in range(4)] + [("after", 0), ("after", 1)]
@@ -430,7 +492,6 @@
     gain, lame, shear, buoy = (layers_of(f) for f in (GAIN, LAME, MU, BUOY))
 
     tall = sublane((EXT, LANES))
-    wide = lane((EXT, LANES))
 
     def linked(test):
         def of(step):
@@ -443,16 +504,16 @@
     link_before = linked(lambda q: q >= PY)
     link_after = linked(lambda q: q < n - PY)
 
-    def x_next(a, l):
+    def x_next(a, l, across=None):
         if l == 1:
             return jnp.where(link_before, a[2], 0.0)
         if l == 5:
-            return jnp.where(link_after, a[6], 0.0)
+            return jnp.where(link_after, a[6] if across is None else across, 0.0)
         return a[l + 1]
 
-    def x_prev(a, l):
+    def x_prev(a, l, across=None):
         if l == 2:
-            return jnp.where(link_before, a[1], 0.0)
+            return jnp.where(link_before, a[1] if across is None else across, 0.0)
         if l == 6:
             return jnp.where(link_after, a[5], 0.0)
         return a[l - 1]
@@ -463,22 +524,24 @@
     def y_prev(a):
         return roll(a, 1, 0)
 
-    def z_next(a):
-        return jnp.where(wide == LANES - 1, 0.0, roll(a, -1, 1))
-
-    def z_prev(a):
-        return jnp.where(wide == 0, 0.0, roll(a, 1, 1))
-
-    def move(v, s, spans):
+    z_next, z_prev = z_after, z_before
+
+    def move(v, s, spans, sums, faces):
         new = [[None] * 8 for _ in range(3)]
+
+        def add(d, l, grad):
+            if sums[d][l] is not None:
+                grad = sums[d][l] + grad
+            new[d][l] = v[d][l] + courant * buoy[l] * grad
+
         for l in spans[0]:
-            grad = (x_next(s[XX], l) - s[XX][l]) + (s[XY][l] - y_prev(s[XY][l])) + (s[XZ][l] - z_prev(s[XZ][l]))
-            new[0][l] = v[0][l] + courant * buoy[l] * grad
+            ahead = x_next(s[XX], l, faces.get(XX))
+            add(0, l, (ahead - s[XX][l]) + (s[XY][l] - y_prev(s[XY][l])) + (s[XZ][l] - z_prev(s[XZ][l])))
         for l in spans[1]:
-            grad = (s[XY][l] - x_prev(s[XY], l)) + (y_next(s[YY][l]) - s[YY][l]) + (s[YZ][l] - z_prev(s[YZ][l]))
-            new[1][l] = v[1][l] + courant * buoy[l] * grad
-            grad = (s[XZ][l] - x_prev(s[XZ], l)) + (s[YZ][l] - y_prev(s[YZ][l])) + (z_next(s[ZZ][l]) - s[ZZ][l])
-            new[2][l] = v[2][l] + courant * buoy[l] * grad
+            behind = x_prev(s[XY], l, faces.get(XY))
+            add(1, l, (s[XY][l] - behind) + (y_next(s[YY][l]) - s[YY][l]) + (s[YZ][l] - z_prev(s[YZ][l])))
+            behind = x_prev(s[XZ], l, faces.get(XZ))
+            add(2, l, (s[XZ][l] - behind) + (s[YZ][l] - y_prev(s[YZ][l])) + (z_next(s[ZZ][l]) - s[ZZ][l]))
         return new
 
     def rates_at(v, l, wanted):
@@ -499,7 +562,8 @@
             out[YZ] = shear[l] * ((z_next(v[1][l]) - v[1][l]) + (y_next(v[2][l]) - v[2][l]))
         return out
 
-    v1 = move(v0, s0, (range(0, 7), range(1, 8)))
+    faces = {XX: face["after", STRESS + XX], XY: face["before", STRESS + XY], XZ: face["before", STRESS + XZ]}
+    v1 = move(v0, s0, (range(0, 7), range(1, 8)), [layers_of(g) for g in ("gx", "gy", "gz")], faces)
     s1 = [[None] * 8 for _ in range(6)]
     m1 = {}
     for l in range(1, 7):
@@ -510,7 +574,7 @@
             if 2 <= l < 6:
                 d = dec[0, l - 2]
                 m1[c, l] = d * mem[c, 0, l - 2] - (1.0 - d) * los[0, l - 2] * rates[c][:ROWS]
-    v2 = move(v1, s1, (range(1, 6), range(2, 7)))
+    v2 = move(v1, s1, (range(1, 6), range(2, 7)), [layers_of(h) for h in (None, "hy", "hz")], {})
     place_sources(source, index, wave, 1, index.shape[0])
     for l in range(2, 6):
         i = l - 2
@@ -549,6 +613,7 @@
     n = lax.axis_size("gx")
     merged = is_merged(n)
     sides = sides_of(n)
+    chunk = tile_chunk(n)
     on_core = pl.BlockSpec(memory_space=pltpu.VMEM)
     scalars = pl.BlockSpec(memory_space=pltpu.SMEM)
     away = pl.BlockSpec(memory_space=pltpu.HBM)
@@ -558,7 +623,8 @@
         c_rows = [LONGEST * ROWS + 16]
     else:
         c_rows = [len(LAST) * ROWS + 16, len(FIRST) * ROWS + 16]
-    inputs = (decay, loss, src_index, waves, stress, memory, velocity, lame_lambda, lame_mu, buoyancy, brick_tiles)
+    tiles = (tile_lambda, tile_mu, tile_buoy)
+    inputs = (*tiles, tile_dest, decay, loss, src_index, waves, stress, memory, velocity, lame_lambda, lame_mu, buoyancy, brick_tiles)
     packed = pl.pallas_call(
         functools.partial(pack_kernel, n, tile_lambda.shape[0]),
         out_shape=[
@@ -567,12 +633,13 @@
             jax.ShapeDtypeStruct((CORNER, LANES), BF16),
             jax.ShapeDtypeStruct((CORNER, LANES), BF16),
             jax.ShapeDtypeStruct((8, LANES), F32),
+            jax.ShapeDtypeStruct((n * chunk, LANES), BF16),
         ]
         + [jax.ShapeDtypeStruct((r, LANES), BF16) for r in c_rows],
         in_specs=[away] * len(inputs),
-        out_specs=[on_core] * (5 + len(c_rows)),
+        out_specs=[on_core] * (6 + len(c_rows)),
         scratch_shapes=[
-            pltpu.SMEM(x.shape, x.dtype) if x is src_index else pltpu.VMEM(x.shape, x.dtype) for x in inputs
+            pltpu.SMEM(x.shape, x.dtype) if x.ndim == 1 else pltpu.VMEM(x.shape, x.dtype) for x in inputs
         ]
         + [
             pltpu.SemaphoreType.DMA((len(inputs),)),
@@ -580,29 +647,25 @@
             pltpu.VMEM((4, ROWS, LANES), F32),
             pltpu.VMEM((4 * ROWS, LANES), F32),
             pltpu.VMEM((CORNER, LANES), F32),
+            pltpu.VMEM((n * chunk, LANES), F32),
         ],
         compiler_params=pltpu.CompilerParams(vmem_limit_bytes=56 * 1024 * 1024),
         name="pack",
     )(*inputs)
-    out_a, out_b, out_d, out_e, own_map = packed[:5]
-    out_c = packed[5:]
-    chunk = tile_chunk(n)
-    tiles = (tile_lambda, tile_mu, tile_buoy)
+    out_a, out_b, out_d, out_e, own_map, out_t = packed[:6]
+    out_c = packed[6:]
+
+    def hold(tiles_in, after, tiles_out):
+        pass
+
     out_t = pl.pallas_call(
-        functools.partial(route_kernel, n),
-        out_shape=jax.ShapeDtypeStruct((n * chunk, LANES), BF16),
-        in_specs=[pl.BlockSpec(memory_space=pl.ANY)] + [away] * 4,
-        out_specs=on_core,
-        scratch_shapes=[pltpu.VMEM(x.shape, x.dtype) for x in tiles]
-        + [
-            pltpu.SMEM(tile_dest.shape, tile_dest.dtype),
-            pltpu.VMEM((n * chunk, LANES), F32),
-            pltpu.SemaphoreType.DMA((4,)),
-        ],
-        compiler_params=pltpu.CompilerParams(vmem_limit_bytes=40 * 1024 * 1024),
-        name="route",
-    )(own_map, *tiles, tile_dest)
-
+        hold,
+        out_shape=jax.ShapeDtypeStruct(out_t.shape, out_t.dtype),
+        in_specs=[pl.BlockSpec(memory_space=pl.ANY)] * 2,
+        out_specs=pl.BlockSpec(memory_space=pl.ANY),
+        input_output_aliases={0: 0},
+        name="hold",
+    )(out_t, own_map)
     def permute(array, source_of):
         return lax.ppermute(array, "gx", [(source_of(i), i) for i in range(n)])
 

time: 26.3 us -> 24.2 us (0.920)
  Pallas kernels: 7.25 us -> 5.77 us
  local copies, waits for them, and re-layouts: 0.75 us -> 0.05 us
    pallas_call x1, Pallas kernels: 1.81 us -> 0.01 us  [body(): pl.pallas_call(hold, out_shape=jax.ShapeDtypeStruct(out_t.shape, out_t.dt...]
    unnamed x36 -> x24, local copies, waits for them, and re-layouts: 0.75 us -> 0.05 us
    pallas_call x1, Pallas kernels: 2.36 us -> 2.73 us  [body(): pl.pallas_call(functools.partial(pack_kernel, n, tile_lambda.shape[0]), o...]
  transfers between devices with their start and end apart: 6 -> 6, of which waited for: 2 -> 1; matrix products, arithmetic and copies ran while one was open for 0% -> 0% of each run, Pallas kernels for 7% -> 0%
where the time goes in v3:
time: 24.2 us; the launch traced here: 23.9 us
  starting transfers between devices  13.1 us (54%)
  Pallas kernels  5.77 us (24%)
  waiting for transfers between devices  4.16 us (17%)
  between operations  0.84 us (3%)
    ppermute x5, starting transfers between devices, permute(): return lax.ppermute(array, 'gx', [(source_of(i), i) for i in range(n)])  9.06 us
    ppermute x5, waiting for transfers between devices, permute(): return lax.ppermute(array, 'gx', [(source_of(i), i) for i in range(n)])  4.16 us
    all_to_all x1, starting transfers between devices, body(): got_t = lax.all_to_all(out_t, 'gx', split_axis=0, concat_axis=0, tiled=True)  4.04 us
    pallas_call x1, Pallas kernels, body(): pl.pallas_call(functools.partial(wave_kernel, n), out_shape=[jax.ShapeDty...  3.04 us
    pallas_call x1, Pallas kernels, body(): pl.pallas_call(functools.partial(pack_kernel, n, tile_lambda.shape[0]), o...  2.73 us
  transfers between devices with their start and end apart: 6, of which 1 were waited for; matrix products, arithmetic and copies ran while one was open for 0% of the time, Pallas kernels for 0%

profile of v3, /device:TPU:0, one launch (start us, length us, event | category | flops | bytes accessed | tf_op | source)
XLA Modules:
  0.0 23.9 jit_solution(17699698514269578499)
XLA Ops:
  0.6 0.0 copy-start
  0.6 0.0 copy-start.1
  0.7 0.0 copy-start.4
  0.7 0.0 copy-start.5
  0.7 0.0 copy-start.6
  0.7 0.0 copy-start.7
  0.7 2.7 %pack.1 = (f32[160,128]{1,0:T(8,128)}, f32[160,128]{1,0:T(8,128)}, bf16[48,128]{1,0:T(8,128)(2,1)}, bf16[48,128]{1,0:T(8,128)(2,1)}, f32[8,128]{1,0:T(8,128)}, /...) custom-call(bf16[8,256]{1,0:T(8,128)(2,1)} %refs_0_.2, bf16[8,256]{1,0:T(8,128)(2,1)} %refs_1_.2, ...), custom_call_target="tpu_custom_call" | custom-call | tf_op jit(solution)/shard_map/pack/pallas_call | solution.py:628
  3.4 0.0 copy-start.2
  3.4 4.2 %collective-permute-start.2 = (bf16[624,128]{1,0:T(8,128)(2,1)}, bf16[624,128]{1,0:T(8,128)(2,1)S(1)}, u32[]{:S(2)}, u32[]{:S(2)}) collective-permute-start(bf16[624,128]{1,0:T(8,128)(2,1)} %get-tuple-element.14), channel_id=1, source_target_pairs={{8,0},{9,1},{10,2},{11,3},{12,4},{13,5},{14,6},{15,7},{0,8},{1,9},... | collective-permute-start | bytes 479240 | tf_op jit(solution)/shard_map/ppermute | solution.py:670
  7.6 0.0 copy-start.11
  7.6 0.0 copy-start.3
  7.6 4.0 %all-to-all-start = ((bf16[16,16,128]{2,1,0:T(8,128)(2,1)}), bf16[16,16,128]{2,1,0:T(8,128)(2,1)S(1)}, u32[]{:S(2)}, u32[]{:S(2)}) async-start(bf16[16,16,128]{2,1,0:T(8,128)(2,1)} %bitcast.6), calls=%async_computation | async-start | bytes 131072 | tf_op jit(solution)/shard_map/all_to_all | solution.py:677
  11.7 0.0 copy-start.8
  11.7 0.5 %collective-permute-start = (f32[160,128]{1,0:T(8,128)}, f32[160,128]{1,0:T(8,128)S(1)}, u32[]{:S(2)}, u32[]{:S(2)}) collective-permute-start(f32[160,128]{1,0:T(8,128)} %get-tuple-element.11), channel_id=1, source_target_pairs={{1,0},{0,1},{3,2},{2,3},{5,4},{4,5},{7,6},{6,7},{9,8},{8,9},{11,10... | collective-permute-start | bytes 245768 | tf_op jit(solution)/shard_map/ppermute | solution.py:670
  12.2 4.3 %collective-permute-start.1 = (f32[160,128]{1,0:T(8,128)}, f32[160,128]{1,0:T(8,128)S(1)}, u32[]{:S(2)}, u32[]{:S(2)}) collective-permute-start(f32[160,128]{1,0:T(8,128)} %get-tuple-element.12), channel_id=1, source_target_pairs={{15,0},{2,1},{1,2},{4,3},{3,4},{6,5},{5,6},{8,7},{7,8},{10,9},{9,1... | collective-permute-start | bytes 245768 | tf_op jit(solution)/shard_map/ppermute | solution.py:670
  16.5 0.0 collective-permute-start.3
  16.5 0.0 copy-done.11
  16.5 0.0 copy-start.9
  16.5 0.0 copy-start.10
  16.5 0.1 collective-permute-start.4
  16.6 4.1 %collective-permute-done.3.refs_15_ = bf16[48,128]{1,0:T(8,128)(2,1)S(1)} collective-permute-done((bf16[48,128]{1,0:T(8,128)(2,1)}, bf16[48,128]{1,0:T(8,128)(2,1)S(1)}, u32[]{:S(2)}, u32[]{:S(2)}) %collective-permute-start.3) | collective-permute-done | bytes 12320 | tf_op jit(solution)/shard_map/ppermute | solution.py:670
  20.7 0.0 collective-permute-done.4.refs_16_
  20.7 0.0 collective-permute-done.refs_11_
  20.7 0.0 collective-permute-done.1.refs_12_
  20.8 0.0 all-to-all-done
  20.8 0.0 collective-permute-done.2.refs_14_
  20.8 0.0 copy-done
  20.8 0.0 copy-done.1
  20.8 0.0 copy-done.4
  20.8 0.0 copy-done.5
  20.8 0.0 copy-done.6
  20.8 0.0 copy-done.7
  20.8 0.0 copy-done.2
  20.8 0.0 copy-done.3
  20.9 0.0 copy-done.8
  20.9 0.0 copy-done.9
  20.9 0.0 copy-done.10
  20.9 3.0 %wave.1 = (f32[3,1,4,32,128]{4,3,2,1,0:T(8,128)}, f32[6,1,4,32,128]{4,3,2,1,0:T(8,128)}, f32[6,1,4,32,128]{4,3,2,1,0:T(8,128)}) custom-call(f32[3,1,4,32,128]{4,3,2,1,0:T(8,128)S(1)} %copy-done.2, f32[6,1,4,32,128]{4,3,2,1,0:T(8,128)S(1)} %copy-done, f32[6,1,4,32,128]{4,3,2,1,0:T(8,128)S(1)} %copy-done.1, f32[1,4,32,128]{3,2,1,0:T(8,128)S(1)} %copy-done.3, ...), custom_call_target="tpu_custom_call" | custom-call | tf_op jit(solution)/shard_map/wave/pallas_call | solution.py:679
  (1 shorter events, 0.0 us)
Async XLA Ops:
  0.6 20.1 %copy-start = (f32[6,1,4,32,128]{4,3,2,1,0:T(8,128)S(1)}, f32[6,1,4,32,128]{4,3,2,1,0:T(8,128)}, u32[]{:S(2)}) copy-start(f32[6,1,4,32,128]{4,3,2,1,0:T(8,128)} %refs_1_.3) | copy-start | bytes 1179652
  0.6 20.1 %copy-start.1 = (f32[6,1,4,32,128]{4,3,2,1,0:T(8,128)S(1)}, f32[6,1,4,32,128]{4,3,2,1,0:T(8,128)}, u32[]{:S(2)}) copy-start(f32[6,1,4,32,128]{4,3,2,1,0:T(8,128)} %refs_2_.3) | copy-start | bytes 1179652
  0.7 20.1 %copy-start.4 = (f32[1,4,32,128]{3,2,1,0:T(8,128)S(1)}, f32[1,4,32,128]{3,2,1,0:T(8,128)}, u32[]{:S(2)}) copy-start(f32[1,4,32,128]{3,2,1,0:T(8,128)} %refs_4_.3) | copy-start | bytes 196612
  0.7 20.1 %copy-start.5 = (f32[1,4,32,128]{3,2,1,0:T(8,128)S(1)}, f32[1,4,32,128]{3,2,1,0:T(8,128)}, u32[]{:S(2)}) copy-start(f32[1,4,32,128]{3,2,1,0:T(8,128)} %refs_5_.3) | copy-start | bytes 196612
  0.7 20.1 %copy-start.6 = (f32[1,4,32,128]{3,2,1,0:T(8,128)S(1)}, f32[1,4,32,128]{3,2,1,0:T(8,128)}, u32[]{:S(2)}) copy-start(f32[1,4,32,128]{3,2,1,0:T(8,128)} %refs_6_.3) | copy-start | bytes 196612
  0.7 20.1 %copy-start.7 = (f32[1,4,32,128]{3,2,1,0:T(8,128)S(1)}, f32[1,4,32,128]{3,2,1,0:T(8,128)}, u32[]{:S(2)}) copy-start(f32[1,4,32,128]{3,2,1,0:T(8,128)} %refs_7_.1) | copy-start | bytes 196612
  3.4 17.4 %copy-start.2 = (f32[3,1,4,32,128]{4,3,2,1,0:T(8,128)S(1)}, f32[3,1,4,32,128]{4,3,2,1,0:T(8,128)}, u32[]{:S(2)}) copy-start(f32[3,1,4,32,128]{4,3,2,1,0:T(8,128)} %refs_0_.3) | copy-start | bytes 589828
  3.4 17.3 %collective-permute-start.2 = (bf16[624,128]{1,0:T(8,128)(2,1)}, bf16[624,128]{1,0:T(8,128)(2,1)S(1)}, u32[]{:S(2)}, u32[]{:S(2)}) collective-permute-start(bf16[624,128]{1,0:T(8,128)(2,1)} %get-tuple-element.14), channel_id=1, source_target_pairs={{8,0},{9,1},{10,2},{11,3},{12,4},{13,5},{14,6},{15,7},{0,8},{1,9},... | collective-permute-start | bytes 479240 | tf_op jit(solution)/shard_map/ppermute | solution.py:670
  7.6 8.9 %copy-start.11 = (bf16[48,128]{1,0:T(8,128)(2,1)S(1)}, bf16[48,128]{1,0:T(8,128)(2,1)}, u32[]{:S(2)}) copy-start(bf16[48,128]{1,0:T(8,128)(2,1)} %get-tuple-element.16) | copy-start | bytes 36868
  7.6 13.2 %copy-start.3 = (f32[1,4,32,128]{3,2,1,0:T(8,128)S(1)}, f32[1,4,32,128]{3,2,1,0:T(8,128)}, u32[]{:S(2)}) copy-start(f32[1,4,32,128]{3,2,1,0:T(8,128)} %refs_3_.3) | copy-start | bytes 196612
  7.6 13.1 %all-to-all-start = ((bf16[16,16,128]{2,1,0:T(8,128)(2,1)}), bf16[16,16,128]{2,1,0:T(8,128)(2,1)S(1)}, u32[]{:S(2)}, u32[]{:S(2)}) async-start(bf16[16,16,128]{2,1,0:T(8,128)(2,1)} %bitcast.6), calls=%async_computation | async-start | bytes 131072 | tf_op jit(solution)/shard_map/all_to_all | solution.py:677
  11.7 9.2 %copy-start.8 = (f32[8,128]{1,0:T(8,128)S(1)}, f32[8,128]{1,0:T(8,128)}, u32[]{:S(2)}) copy-start(f32[8,128]{1,0:T(8,128)} %get-tuple-element.10.after.refs_10_) | copy-start | bytes 12292
  11.7 9.1 %collective-permute-start = (f32[160,128]{1,0:T(8,128)}, f32[160,128]{1,0:T(8,128)S(1)}, u32[]{:S(2)}, u32[]{:S(2)}) collective-permute-start(f32[160,128]{1,0:T(8,128)} %get-tuple-element.11), channel_id=1, source_target_pairs={{1,0},{0,1},{3,2},{2,3},{5,4},{4,5},{7,6},{6,7},{9,8},{8,9},{11,10... | collective-permute-start | bytes 245768 | tf_op jit(solution)/shard_map/ppermute | solution.py:670
  12.2 8.6 %collective-permute-start.1 = (f32[160,128]{1,0:T(8,128)}, f32[160,128]{1,0:T(8,128)S(1)}, u32[]{:S(2)}, u32[]{:S(2)}) collective-permute-start(f32[160,128]{1,0:T(8,128)} %get-tuple-element.12), channel_id=1, source_target_pairs={{15,0},{2,1},{1,2},{4,3},{3,4},{6,5},{5,6},{8,7},{7,8},{10,9},{9,1... | collective-permute-start | bytes 245768 | tf_op jit(solution)/shard_map/ppermute | solution.py:670
  16.5 4.2 %collective-permute-start.3 = (bf16[48,128]{1,0:T(8,128)(2,1)}, bf16[48,128]{1,0:T(8,128)(2,1)S(1)}, u32[]{:S(2)}, u32[]{:S(2)}) collective-permute-start(bf16[48,128]{1,0:T(8,128)(2,1)} %get-tuple-element.15), channel_id=1, source_target_pairs={{7,0},{10,1},{9,2},{12,3},{11,4},{14,5},{13,6},{0,7},{15,8},{2,9},... | collective-permute-start | bytes 36872 | tf_op jit(solution)/shard_map/ppermute | solution.py:670
  16.5 4.4 %copy-start.9 = (f32[16,2]{0,1:T(2,128)S(1)}, f32[16,2]{0,1:T(2,128)}, u32[]{:S(2)}) copy-start(f32[16,2]{0,1:T(2,128)} %param.29) | copy-start | bytes 388
  16.5 4.4 %copy-start.10 = (s32[16]{0:T(128)S(1)}, s32[16]{0:T(128)}, u32[]{:S(2)}) copy-start(s32[16]{0:T(128)} %refs_8_.3) | copy-start | bytes 196
  16.5 4.2 %collective-permute-start.4 = (bf16[48,128]{1,0:T(8,128)(2,1)S(1)}, bf16[48,128]{1,0:T(8,128)(2,1)S(1)}, u32[]{:S(2)}, u32[]{:S(2)}) collective-permute-start(bf16[48,128]{1,0:T(8,128)(2,1)S(1)} %copy-done.11), channel_id=1, source_target_pairs={{9,0},{8,1},{11,2},{10,3},{13,4},{12,5},{15,6},{14,7},{1,8},{0,9},... | collective-permute-start | bytes 36872 | tf_op jit(solution)/shard_map/ppermute | solution.py:670

commit v4 on v3

--- a/solution.py
+++ b/solution.py
@@ -93,51 +93,56 @@
     return jnp.where(lane(a.shape) == 0, 0.0, roll(a, 1, 1))
 
 
-def place_sources(into, index, wave, step, count):
-    into[...] = jnp.zeros_like(into)
-    lanes = lane((1, LANES))
-    for e in range(count):
-        cell = index[e]
-        row = lax.shift_right_logical(cell, 7)
-        strength = jnp.broadcast_to(wave[step : step + 1, e : e + 1], (1, LANES))
-        here = jnp.where(lanes == (cell & (LANES - 1)), strength, 0.0)
-        into[pl.ds(row, 1), :] = into[pl.ds(row, 1), :] + here
+def place_sources(index, wave, step):
+    count = index.shape[1]
+    cells = jnp.broadcast_to(index[...], (LANES, count))
+    place = sublane((LANES, count))
+    rows = (lax.shift_right_logical(cells, 7) == place).astype(F32)
+    at = ((cells & (LANES - 1)) == place).astype(F32)
+    left = wave[step : step + 1, :]
+    parts = []
+    for _ in range(3):
+        part = left.astype(BF16).astype(F32)
+        parts.append((at * part).astype(BF16))
+        left = left - part
+    total = None
+    for part in parts:
+        done = lax.dot_general(rows.astype(BF16), part, (((1,), (1,)), ((), ())), preferred_element_type=F32)
+        total = done if total is None else total + done
+    return total
 
 
 def pack_kernel(n, per, *refs):
     merged = is_merged(n)
-    count = 6 + len(sides_of(n))
-    far_refs, outs = refs[:15], refs[15 : 15 + count]
-    refs = refs[15 + count :]
+    sides = len(sides_of(n))
+    far_refs, outs, refs = refs[:15], refs[15 : 31 + sides], refs[31 + sides :]
     out_a, out_b, out_d, out_e, out_map, out_t = outs[:6]
-    out_c = outs[6:]
-    near_refs, sems = refs[:15], refs[15]
-    held, gain, source, corner, routed = refs[16:]
-    copies = [pltpu.make_async_copy(x, y, sems.at[k]) for k, (x, y) in enumerate(zip(far_refs, near_refs))]
-    for copy in copies:
-        copy.start()
-    near_lam, near_mu, near_bu, near_dest, dec, los, index, wave, st, mem, vel, lam, mu, bu, tiles = near_refs
+    dec, los, st, mem, vel, lam, mu, bu = outs[6:14]
+    held, later = outs[14:16]
+    out_c = outs[16:]
+    near_lam, near_mu, near_bu, near_dest, index, wave, tiles, sems = refs[:8]
+    gain, source, corner, ends, routed, routed_out = refs[8:]
+    near_refs = (near_lam, near_mu, near_bu, near_dest, dec, los, index, wave, st, mem, vel, lam, mu, bu, tiles)
     b = lax.axis_index("gx")
     even = lax.rem(b, 2) == 0
-    for copy in copies[:4]:
-        copy.wait()
-    route_tiles(n, near_lam, near_mu, near_bu, near_dest, routed, out_t)
-    for copy in copies[4:8]:
-        copy.wait()
-    place_sources(source, index, wave, 0, index.shape[0])
-    for copy in copies[8:10]:
-        copy.wait()
-    for i in range(4):
-        d = dec[0, i]
-        gain[i] = courant * (1.0 - (1.0 - d) * los[0, i])
-        kept = courant * d
-        for c in range(6):
-            value = st[c, 0, i] + kept * mem[c, 0, i]
-            if c < 3:
-                value = value + source[i * ROWS : (i + 1) * ROWS, :]
-            held[c, i] = value
-    for copy in copies[10:]:
-        copy.wait()
+    first_x = b < PY
+    top, bottom = slice(0, 8), slice(ROWS - 8, ROWS)
+    copies = {}
+    for k in (0, 1, 2, 3, 14, 6, 7, 8, 10, 13, 11, 12, 4, 5, 9):
+        copies[k] = pltpu.make_async_copy(far_refs[k], near_refs[k], sems.at[k])
+        copies[k].start()
+
+    def arrive(*which):
+        for k in which:
+            copies[k].wait()
+
+    arrive(0, 1, 2, 3)
+    route_tiles(n, near_lam, near_mu, near_bu, near_dest, routed, routed_out)
+    leave = pltpu.make_async_copy(routed_out, out_t, sems.at[15])
+    leave.start()
+    arrive(6, 7, 14)
+    source[...] = place_sources(index, wave, 0)
+    later[...] = place_sources(index, wave, 1)
 
     def get(f, i, rows=slice(None)):
         if f < VEL:
@@ -151,7 +156,6 @@
         return (lam, mu, bu)[f - LAME][0, i, rows]
 
     sub = sublane((8, LANES))
-    top, bottom = slice(0, 8), slice(ROWS - 8, ROWS)
 
     rows_z = LANES // TZ
     table = tiles[...]
@@ -208,52 +212,82 @@
             hi = jnp.where(mine, roll(get(f, i, bottom), 2 * i + 2, 0), hi)
         return lo, hi
 
-    for f in range(FIELDS + 1):
-        lo, hi = edge_rows(f)
-        out_a[f * 8 : f * 8 + 8, :] = jnp.where(even, hi, lo)
-        out_b[f * 8 : f * 8 + 8, :] = jnp.where(even, lo, hi)
-
-    def write_corner(out, rows, strip):
-        corner[...] = jnp.zeros_like(corner)
+    def write_edges(which):
+        for f in which:
+            lo, hi = edge_rows(f)
+            out_a[f * 8 : f * 8 + 8, :] = jnp.where(even, hi, lo)
+            out_b[f * 8 : f * 8 + 8, :] = jnp.where(even, lo, hi)
+
+    def write_corner(rows, which, strip, at):
         for k, (f, i, r) in enumerate(rows):
-            corner[k : k + 1, :] = get(f, i, slice(r % ROWS, r % ROWS + 1))
-        corner[len(rows) : len(rows) + 1, :] = owners[strip : strip + 1]
-        out[...] = corner[...].astype(BF16)
-
-    @pl.when(even)
-    def _():
-        write_corner(out_e, BELOW, last)
-        write_corner(out_d, ABOVE, 0)
-
-    @pl.when(jnp.logical_not(even))
-    def _():
-        write_corner(out_e, ABOVE, 0)
-        write_corner(out_d, BELOW, last)
-
-    def write_layers(out, which, rest):
-        for k, (f, i) in enumerate(which):
-            out[k * ROWS : (k + 1) * ROWS, :] = entry(f, i).astype(BF16)
-        if rest:
-            out[len(which) * ROWS : (len(which) + rest) * ROWS, :] = jnp.zeros((rest * ROWS, LANES), BF16)
-        base = (len(which) + rest) * ROWS
-        out[base : base + 16, :] = corner[0:16, :].astype(BF16)
-
-    for k, (f, i, r) in enumerate(ENDS):
-        row = slice(r % ROWS, r % ROWS + 1)
-        corner[k : k + 1, :] = sums(f, i)[row] if isinstance(f, str) else get(f, i, row)
-    corner[ENDS_MAP : ENDS_MAP + last + 1, :] = owners[0 : last + 1]
-    if merged:
-
-        @pl.when(b < PY)
-        def _():
-            write_layers(out_c[0], LAST, LONGEST - len(LAST))
-
-        @pl.when(b >= PY)
-        def _():
-            write_layers(out_c[0], FIRST, LONGEST - len(FIRST))
-    else:
-        write_layers(out_c[0], LAST, 0)
-        write_layers(out_c[1], FIRST, 0)
+            if f in which:
+                corner[at + k : at + k + 1, :] = get(f, i, slice(r % ROWS, r % ROWS + 1))
+        if FIELDS in which:
+            corner[at + len(rows) : at + len(rows) + 1, :] = owners[strip : strip + 1]
+
+    def write_layers(out, entries, which):
+        for k, (f, i) in enumerate(entries):
+            if f in which:
+                out[k * ROWS : (k + 1) * ROWS, :] = entry(f, i).astype(BF16)
+
+    def write_ends(which):
+        for k, (f, i, r) in enumerate(ENDS):
+            if f in which:
+                row = slice(r % ROWS, r % ROWS + 1)
+                ends[k : k + 1, :] = sums(f, i)[row] if isinstance(f, str) else get(f, i, row)
+
+    def write(*which):
+        write_edges([f for f in which if not isinstance(f, str)])
+        write_corner(BELOW, which, last, 0)
+        write_corner(ABOVE, which, 0, CORNER)
+        write_ends(which)
+        if merged:
+
+            @pl.when(first_x)
+            def _():
+                write_layers(out_c[0], LAST, which)
+
+            @pl.when(jnp.logical_not(first_x))
+            def _():
+                write_layers(out_c[0], FIRST, which)
+        else:
+            write_layers(out_c[0], LAST, which)
+            write_layers(out_c[1], FIRST, which)
+
+    corner[...] = jnp.zeros_like(corner)
+    ends[ENDS_MAP : ENDS_MAP + last + 1, :] = owners[0 : last + 1]
+    arrive(8)
+    write(FIELDS, *range(STRESS, VEL), "gx", "gy", "gz")
+    arrive(10, 13, 11, 12)
+    write(*range(VEL, HELD), LAME, MU, BUOY)
+    arrive(4, 5)
+    for i in range(4):
+        gain[i] = courant * (1.0 - (1.0 - dec[0, i]) * los[0, i])
+    write(GAIN)
+    arrive(9)
+    for i in range(4):
+        kept = courant * dec[0, i]
+        for c in range(6):
+            value = st[c, 0, i] + kept * mem[c, 0, i]
+            if c < 3:
+                value = value + source[i * ROWS : (i + 1) * ROWS, :]
+            held[c, i] = value
+    write(*range(HELD, GAIN), "hy", "hz")
+    below, above = corner[0:CORNER, :].astype(BF16), corner[CORNER : 2 * CORNER, :].astype(BF16)
+    out_e[...] = jnp.where(even, below, above)
+    out_d[...] = jnp.where(even, above, below)
+    for out, entries in zip(out_c, (LAST, FIRST)):
+        if merged:
+            base = LONGEST * ROWS
+
+            @pl.when(first_x)
+            def _():
+                rest = (LONGEST - len(LAST)) * ROWS
+                out[len(LAST) * ROWS : base, :] = jnp.zeros((rest, LANES), BF16)
+        else:
+            base = len(entries) * ROWS
+        out[base : base + 16, :] = ends[...].astype(BF16)
+    leave.wait()
 
 
 def route_tiles(n, near_lam, near_mu, near_bu, near_dest, rows, out):
@@ -307,56 +341,137 @@
     out[...] = rows[...].astype(BF16)
 
 
-def wave_kernel(n, *refs):
-    merged = is_merged(n)
-    (vel, st, mem, lam, mu, bu, dec, los, index, wave, maps, got_a, got_b, got_t) = refs[:14]
-    refs = refs[14:]
+def halo_blocks(even, near, far, f):
+    x = near[f * 8 : f * 8 + 8, :]
+    y = far[f * 8 : f * 8 + 8, :]
+    return jnp.where(even, x, y), jnp.where(even, y, x)
+
+
+def halo_rows(blocks, i):
+    after, before = blocks
+    sub = sublane((8, LANES))
+    return jnp.where(sub < 2, roll(after, -2 * i, 0), roll(before, 6 - 2 * i, 0))
+
+
+def side_messages(n, got_c):
+    first_x = lax.axis_index("gx") < PY
+    if is_merged(n):
+        message, base = got_c[0], LONGEST * ROWS
+        return [("before", LAST, message, base, jnp.logical_not(first_x)), ("after", FIRST, message, base, first_x)]
+    return [
+        (name, which, message, len(which) * ROWS, None)
+        for name, which, message in (("before", LAST, got_c[0]), ("after", FIRST, got_c[1]))
+    ]
+
+
+def side_rows(which, message, whole, ends, f, i):
+    k = which.index((f, i))
+    main = message[k * ROWS : (k + 1) * ROWS, :].astype(F32)
+    if whole is None:
+        return main
+    sub = sublane((8, LANES))
+    only = [jnp.zeros((8, LANES), F32)] * (ROWS // 8)
+    for e in (3, 4, 5, 9, 10, 11):
+        if ENDS[e][:2] == (f, i):
+            at = ENDS[e][2] % ROWS
+            only[at // 8] = jnp.where(sub == at % 8, jnp.broadcast_to(ends[e : e + 1, :], (8, LANES)), 0.0)
+    return jnp.where(whole, main, jnp.concatenate(only, 0))
+
+
+SIDES = [("before", f, i) for f, i in LAST] + [("after", f, i) for f, i in FIRST]
+
+
+def side_kernel(n, *refs):
     sides = len(sides_of(n))
-    got_c, got_d, got_e = refs[:sides], refs[sides : 2 * sides], refs[2 * sides : 3 * sides]
-    new_v, new_s, new_m, source, rows_t, spread_rows, tile_rows, near_rows, far_rows, end_rows = refs[3 * sides :]
-    b = lax.axis_index("gx")
-    even = lax.rem(b, 2) == 0
-    first_x = b < PY
+    got_c, (side, ends) = refs[:sides], refs[sides:]
+    sub = sublane((8, LANES))
+    for name, which, message, base, whole in side_messages(n, got_c):
+        ends[...] = message[base : base + 16, :].astype(F32)
+
+        def end_row(f, i, r):
+            at = ENDS.index((f, i, r))
+            return jnp.broadcast_to(ends[at : at + 1, :], (8, LANES))
+
+        edge = 3 if name == "before" else 0
+        for f, i in which:
+            k = SIDES.index((name, f, i))
+            side[k, 0:ROWS] = side_rows(which, message, whole, ends, f, i)
+            if isinstance(f, str):
+                halo = jnp.zeros((8, LANES), F32)
+                if i == edge and f == "gx":
+                    halo = jnp.where(sub == 0, -end_row(STRESS + XY, i, -1), 0.0)
+                if i == edge and f == "gy":
+                    halo = jnp.where(sub == 7, end_row(STRESS + YY, i, 0), 0.0)
+                if i == edge and f == "gz":
+                    halo = jnp.where(sub == 0, -end_row(STRESS + YZ, i, -1), 0.0)
+                side[k, ROWS:EXT] = halo
+
+
+def line_layout(n):
+    at, layout = 0, {}
+    spans = [(2 * p, 2) for p in range(3)] + [(6 + p, 1) for p in range(3)]
+    for g in range(len(sides_of(n))):
+        spans += [(9 + 7 * g, 1), (10 + 7 * g, 1), (11 + 7 * g, 2)] + [(13 + 7 * g + p, 1) for p in range(3)]
+    for row, halves in spans:
+        layout[row] = at, halves
+        at += n * 16 * halves
+    return layout, at
+
+
+def tile_kernel(n, got_t, out, rows_t, spread_rows):
     chunk = tile_chunk(n)
-    sub = sublane((8, LANES))
-
-    def halo_blocks(near, far, f):
-        x = near[f * 8 : f * 8 + 8, :]
-        y = far[f * 8 : f * 8 + 8, :]
-        return jnp.where(even, x, y), jnp.where(even, y, x)
-
-    def halo_rows(blocks, i):
-        after, before = blocks
-        return jnp.where(sub < 2, roll(after, -2 * i, 0), roll(before, 6 - 2 * i, 0))
-
     rows_t[...] = got_t[...].astype(F32)
-    col = lane((16, LANES))
-    line = sublane((16, LANES))
-    on_line = col // TZ == line
+    on_line = lane((16, LANES)) // TZ == sublane((16, LANES))
     spread = (lax.rem(sublane((LANES, LANES)), TZ) == lax.rem(lane((LANES, LANES)), TZ)).astype(BF16)
-
-    def overlay(row, halves, wanted):
-        def take(first, values):
+    for row, (base, halves) in line_layout(n)[0].items():
+
+        def group(q, _, row=row, base=base, halves=halves):
             for s in range(16):
                 for h in range(halves):
-                    value = rows_t[pl.ds((first + s) * chunk + row + h, 1), :]
+                    value = rows_t[pl.ds((q * 16 + s) * chunk + row + h, 1), :]
                     value = jnp.where(on_line, jnp.broadcast_to(value, (16, LANES)), 0.0)
                     at = (s * halves + h) * 16
                     spread_rows[at : at + 16, :] = value.astype(BF16)
-            size = 16 * halves * 16
-            tile_rows[0:size, :] = jnp.dot(spread_rows[0:size, :], spread, preferred_element_type=F32)
+            size = 256 * halves
+            done = jnp.dot(spread_rows[0:size, :], spread, preferred_element_type=F32)
+            out[pl.ds(base + q * size, size), :] = done
+            return 0
+
+        if n == 16:
+            group(0, 0)
+        else:
+            lax.fori_loop(0, n // 16, group, 0)
+
+
+def wave_kernel(n, *refs):
+    merged = is_merged(n)
+    (vel, st, mem, lam, mu, bu, dec, los, kept, side, source, maps, got_a, got_b, lines) = refs[:15]
+    refs = refs[15:]
+    sides = len(sides_of(n))
+    got_c, got_d, got_e = refs[:sides], refs[sides : 2 * sides], refs[2 * sides : 3 * sides]
+    far_outs, refs = refs[3 * sides : 3 * sides + 3], refs[3 * sides + 3 :]
+    near_rows, far_rows, end_rows, new_v, new_s, new_m, sems = refs
+    b = lax.axis_index("gx")
+    even = lax.rem(b, 2) == 0
+    sub = sublane((8, LANES))
+    layout, _ = line_layout(n)
+
+    def overlay(row, wanted):
+        base, halves = layout[row]
+
+        def take(s, values):
             done = []
             for value, (_, owner, at) in zip(values, wanted):
-                for s in range(16):
-                    here = tile_rows[s * halves * 16 + at : s * halves * 16 + at + 8, :]
-                    value = jnp.where(owner == (first + s) * 1.0, here, value)
-                done.append(value)
+                here = lines[pl.ds(base + s * halves * 16 + at, 8), :]
+                done.append(jnp.where(owner == s.astype(F32) if n > 16 else owner == s * 1.0, here, value))
             return done
 
         values = [w[0] for w in wanted]
         if n == 16:
-            return take(0, values)
-        return lax.fori_loop(0, n // 16, lambda g, v: take(g * 16, v), values)
+            for s in range(n):
+                values = take(s, values)
+            return values
+        return lax.fori_loop(0, n, take, values)
 
     column = {}
     rows_y = ROWS // TY
@@ -367,38 +482,34 @@
         if f < HELD:
             return vel[f - VEL, 0, i]
         if f < GAIN:
-            value = st[f - HELD, 0, i] + courant * dec[0, i] * mem[f - HELD, 0, i]
-            if f < HELD + 3:
-                value = value + source[i * ROWS : (i + 1) * ROWS, :]
-            return value
+            return kept[f - HELD, i]
         if f == GAIN:
             return courant * (1.0 - (1.0 - dec[0, i]) * los[0, i])
         return (lam, mu, bu)[f - LAME][0, i]
 
-    def main_tiles(mains, owners, row, halves, line_of):
+    def main_tiles(mains, owners, row, line_of):
         wanted = []
         for i, m in mains.items():
             for p in range(rows_y):
                 owner = jnp.broadcast_to(owners[p : p + 1], (8, LANES))
                 wanted.append((m[p * 8 : (p + 1) * 8], owner, line_of(i)))
-        laid = overlay(row, halves, wanted)
+        laid = overlay(row, wanted)
         return {i: jnp.concatenate(laid[k * rows_y : (k + 1) * rows_y], 0) for k, i in enumerate(mains)}
 
     def halo_tiles(halos, after, before, row):
         zeros = jnp.zeros((8, LANES), F32)
-        blocks = overlay(row, 1, [(zeros, after, 0), (zeros, before, 8)])
+        blocks = overlay(row, [(zeros, after, 0), (zeros, before, 8)])
         covered = jnp.where(sub < 4, after, before) >= 0.0
         return {i: jnp.where(covered, halo_rows(blocks, i), h) for i, h in halos.items()}
 
-    place_sources(source, index, wave, 0, index.shape[0])
-    after, before = halo_blocks(got_a, got_b, FIELDS)
+    after, before = halo_blocks(even, got_a, got_b, FIELDS)
     for f in range(FIELDS):
-        blocks = halo_blocks(got_a, got_b, f)
+        blocks = halo_blocks(even, got_a, got_b, f)
         main = {i: own(f, i) for i in range(4)}
         halo = {i: halo_rows(blocks, i) for i in range(4)}
         if f >= LAME:
             p = f - LAME
-            main = main_tiles(main, maps[...], 2 * p, 2, lambda i: i * 8)
+            main = main_tiles(main, maps[...], 2 * p, lambda i: i * 8)
             halo = halo_tiles(halo, after, before, 6 + p)
         for i in range(4):
             column["own", f, i] = jnp.concatenate([main[i], halo[i]], 0)
@@ -413,13 +524,11 @@
 
     no_rows, no_halo = jnp.zeros((ROWS, LANES), F32), jnp.zeros((8, LANES), F32)
     face = {}
-    for side, (name, which) in enumerate((("before", LAST), ("after", FIRST))):
-        group = 0 if merged else side
+    for order, (name, which) in enumerate((("before", LAST), ("after", FIRST))):
+        group = 0 if merged else order
         message = got_c[group]
         base = (LONGEST if merged else len(which)) * ROWS
-        if merged:
-            whole = first_x if name == "after" else jnp.logical_not(first_x)
-        if group == side:
+        if group == order:
             near, far = got_e[group][...].astype(F32), got_d[group][...].astype(F32)
             near_rows[...] = jnp.where(even, near, far)
             far_rows[...] = jnp.where(even, far, near)
@@ -429,23 +538,8 @@
         owners = end_rows[8:16, :][ENDS_MAP - 8 :]
         row = 9 + 7 * group
 
-        def end_row(f, i, r):
-            at = ENDS.index((f, i, r))
-            return jnp.broadcast_to(end_rows[at : at + 1, :], (8, LANES))
-
         def main_rows(f, i):
-            if (f, i) not in which:
-                return no_rows
-            k = which.index((f, i))
-            main = message[k * ROWS : (k + 1) * ROWS, :].astype(F32)
-            if not merged:
-                return main
-            only = [no_halo] * rows_y
-            if (f, i, 0) in ENDS[3:6] + ENDS[9:12]:
-                only[0] = jnp.where(sub == 0, end_row(f, i, 0), 0.0)
-            if (f, i, -1) in ENDS[3:6] + ENDS[9:12]:
-                only[-1] = jnp.where(sub == 7, end_row(f, i, -1), 0.0)
-            return jnp.where(whole, main, jnp.concatenate(only, 0))
+            return side[SIDES.index((name, f, i)), 0:ROWS] if (f, i) in which else no_rows
 
         def corner_halo(f, i):
             above = corner_rows(near_rows, ABOVE, f, i)
@@ -461,9 +555,9 @@
             halo = {i: corner_halo(f, i) for i in present}
             main = {i: no_rows if f < VEL else main_rows(f, i) for i in present}
             if f == BUOY:
-                main = main_tiles(main, owners, row + 2, 2, lambda i: i * 8)
+                main = main_tiles(main, owners, row + 2, lambda i: i * 8)
             elif f >= LAME:
-                main = main_tiles(main, owners, row + f - LAME, 1, lambda i: 8 if i else 0)
+                main = main_tiles(main, owners, row + f - LAME, lambda i: 8 if i else 0)
             if f >= LAME:
                 halo = halo_tiles(halo, after, before, row + 4 + f - LAME)
             for i in present:
@@ -471,16 +565,8 @@
             if f < VEL and (f, edge) in which:
                 face[name, f] = jnp.concatenate([main_rows(f, edge), halo[edge]], 0)
         for f, i in which:
-            if not isinstance(f, str):
-                continue
-            halo = no_halo
-            if i == edge and f == "gx":
-                halo = jnp.where(sub == 0, -end_row(STRESS + XY, i, -1), 0.0)
-            if i == edge and f == "gy":
-                halo = jnp.where(sub == 7, end_row(STRESS + YY, i, 0), 0.0)
-            if i == edge and f == "gz":
-                halo = jnp.where(sub == 0, -end_row(STRESS + YZ, i, -1), 0.0)
-            column[name, f, i] = jnp.concatenate([main_rows(f, i), halo], 0)
+            if isinstance(f, str):
+                column[name, f, i] = side[SIDES.index((name, f, i))]
 
     def layers_of(f):
         names = [("before", 2), ("before", 3)] + [("own", i) for i in range(4)] + [("after", 0), ("after", 1)]
@@ -575,14 +661,22 @@
                 d = dec[0, l - 2]
                 m1[c, l] = d * mem[c, 0, l - 2] - (1.0 - d) * los[0, l - 2] * rates[c][:ROWS]
     v2 = move(v1, s1, (range(1, 6), range(2, 7)), [layers_of(h) for h in (None, "hy", "hz")], {})
-    place_sources(source, index, wave, 1, index.shape[0])
-    for l in range(2, 6):
-        i = l - 2
+    copies = []
+
+    def send(k, i):
+        near, far = (new_v, new_s, new_m)[k], far_outs[k]
+        copies.append(pltpu.make_async_copy(near.at[:, :, i], far.at[:, :, i], sems.at[k, i]))
+        copies[-1].start()
+
+    for i in range(4):
+        for c in range(3):
+            new_v[c, 0, i] = v2[c][i + 2][:ROWS]
+        send(0, i)
+    for i in range(4):
+        l = i + 2
         rates = rates_at(v2, l, range(6))
         d = dec[0, i]
         lost = (1.0 - d) * los[0, i]
-        for c in range(3):
-            new_v[c, 0, i] = v2[c][l][:ROWS]
         for c in range(6):
             rate = rates[c][:ROWS]
             m2 = d * m1[c, l] - lost * rate
@@ -591,6 +685,10 @@
             if c < 3:
                 value = value + source[i * ROWS : (i + 1) * ROWS, :]
             new_s[c, 0, i] = value
+        send(1, i)
+        send(2, i)
+    for copy in copies:
+        copy.wait()
 
 
 def body(
@@ -615,16 +713,21 @@
     sides = sides_of(n)
     chunk = tile_chunk(n)
     on_core = pl.BlockSpec(memory_space=pltpu.VMEM)
-    scalars = pl.BlockSpec(memory_space=pltpu.SMEM)
     away = pl.BlockSpec(memory_space=pltpu.HBM)
+    def vmem(*shape):
+        return jax.ShapeDtypeStruct(shape, F32)
+
     waves = src_wave.T
+    cells = src_index[None, :]
     fields = (velocity, stress, memory, lame_lambda, lame_mu, buoyancy, decay, loss)
     if merged:
         c_rows = [LONGEST * ROWS + 16]
     else:
         c_rows = [len(LAST) * ROWS + 16, len(FIRST) * ROWS + 16]
     tiles = (tile_lambda, tile_mu, tile_buoy)
-    inputs = (*tiles, tile_dest, decay, loss, src_index, waves, stress, memory, velocity, lame_lambda, lame_mu, buoyancy, brick_tiles)
+    kept = (decay, loss, stress, memory, velocity, lame_lambda, lame_mu, buoyancy)
+    inputs = (*tiles, tile_dest, decay, loss, cells, waves, stress, memory, velocity, lame_lambda, lame_mu, buoyancy, brick_tiles)
+    inputs = tuple(pltpu.with_memory_space_constraint(x, pltpu.HBM) for x in inputs)
     packed = pl.pallas_call(
         functools.partial(pack_kernel, n, tile_lambda.shape[0]),
         out_shape=[
@@ -635,37 +738,33 @@
             jax.ShapeDtypeStruct((8, LANES), F32),
             jax.ShapeDtypeStruct((n * chunk, LANES), BF16),
         ]
+        + [jax.ShapeDtypeStruct(x.shape, x.dtype) for x in kept]
+        + [vmem(6, 4, ROWS, LANES), vmem(4 * ROWS, LANES)]
         + [jax.ShapeDtypeStruct((r, LANES), BF16) for r in c_rows],
         in_specs=[away] * len(inputs),
-        out_specs=[on_core] * (6 + len(c_rows)),
+        out_specs=[on_core] * 5 + [away] + [on_core] * (10 + len(c_rows)),
         scratch_shapes=[
-            pltpu.SMEM(x.shape, x.dtype) if x.ndim == 1 else pltpu.VMEM(x.shape, x.dtype) for x in inputs
+            pltpu.SMEM(x.shape, x.dtype) if x.ndim == 1 else pltpu.VMEM(x.shape, x.dtype)
+            for x in (*tiles, tile_dest, cells, waves, brick_tiles)
         ]
         + [
-            pltpu.SemaphoreType.DMA((len(inputs),)),
-            pltpu.VMEM((6, 4, ROWS, LANES), F32),
+            pltpu.SemaphoreType.DMA((16,)),
             pltpu.VMEM((4, ROWS, LANES), F32),
             pltpu.VMEM((4 * ROWS, LANES), F32),
-            pltpu.VMEM((CORNER, LANES), F32),
+            pltpu.VMEM((2 * CORNER, LANES), F32),
+            pltpu.VMEM((16, LANES), F32),
             pltpu.VMEM((n * chunk, LANES), F32),
+            pltpu.VMEM((n * chunk, LANES), BF16),
         ],
-        compiler_params=pltpu.CompilerParams(vmem_limit_bytes=56 * 1024 * 1024),
+        compiler_params=pltpu.CompilerParams(vmem_limit_bytes=16 * 1024 * 1024),
         name="pack",
     )(*inputs)
     out_a, out_b, out_d, out_e, own_map, out_t = packed[:6]
-    out_c = packed[6:]
-
-    def hold(tiles_in, after, tiles_out):
-        pass
-
-    out_t = pl.pallas_call(
-        hold,
-        out_shape=jax.ShapeDtypeStruct(out_t.shape, out_t.dtype),
-        in_specs=[pl.BlockSpec(memory_space=pl.ANY)] * 2,
-        out_specs=pl.BlockSpec(memory_space=pl.ANY),
-        input_output_aliases={0: 0},
-        name="hold",
-    )(out_t, own_map)
+    held, later = packed[14:16]
+    out_c = packed[16:]
+    dec, los, st, mem, vel, lam, mu, bu = packed[6:14]
+    fields = (vel, st, mem, lam, mu, bu, dec, los)
+
     def permute(array, source_of):
         return lax.ppermute(array, "gx", [(source_of(i), i) for i in range(n)])
 
@@ -676,27 +775,40 @@
     got_a = permute(out_a, pair_near)
     got_t = lax.all_to_all(out_t, "gx", split_axis=0, concat_axis=0, tiled=True)
 
+    side = pl.pallas_call(
+        functools.partial(side_kernel, n),
+        out_shape=vmem(len(SIDES), EXT, LANES),
+        in_specs=[on_core] * len(sides),
+        out_specs=on_core,
+        scratch_shapes=[pltpu.VMEM((16, LANES), F32)],
+        compiler_params=pltpu.CompilerParams(vmem_limit_bytes=16 * 1024 * 1024),
+        name="sides",
+    )(*got_c)
+    lines = pl.pallas_call(
+        functools.partial(tile_kernel, n),
+        out_shape=vmem(line_layout(n)[1], LANES),
+        in_specs=[on_core],
+        out_specs=on_core,
+        scratch_shapes=[pltpu.VMEM((n * chunk, LANES), F32), pltpu.VMEM((16 * 32, LANES), BF16)],
+        compiler_params=pltpu.CompilerParams(vmem_limit_bytes=40 * 1024 * 1024),
+        name="tiles",
+    )(got_t)
+    outs = (velocity, stress, memory)
     return pl.pallas_call(
         functools.partial(wave_kernel, n),
-        out_shape=[
-            jax.ShapeDtypeStruct(velocity.shape, F32),
-            jax.ShapeDtypeStruct(stress.shape, F32),
-            jax.ShapeDtypeStruct(memory.shape, F32),
-        ],
-        in_specs=[on_core] * 8 + [scalars] + [on_core] * (5 + 3 * len(sides)),
-        out_specs=[on_core] * 3,
+        out_shape=[jax.ShapeDtypeStruct(x.shape, F32) for x in outs],
+        in_specs=[on_core] * (15 + 3 * len(sides)),
+        out_specs=[away] * 3,
         scratch_shapes=[
-            pltpu.VMEM((4 * ROWS, LANES), F32),
-            pltpu.VMEM((n * chunk, LANES), F32),
-            pltpu.VMEM((16 * 32, LANES), BF16),
-            pltpu.VMEM((16 * 32, LANES), F32),
             pltpu.VMEM((CORNER, LANES), F32),
             pltpu.VMEM((CORNER, LANES), F32),
             pltpu.VMEM((16, LANES), F32),
-        ],
+        ]
+        + [pltpu.VMEM(x.shape, F32) for x in outs]
+        + [pltpu.SemaphoreType.DMA((3, 4))],
         compiler_params=pltpu.CompilerParams(vmem_limit_bytes=48 * 1024 * 1024),
         name="wave",
-    )(*fields, src_index, waves, own_map, got_a, got_b, got_t, *got_c, *got_d, *got_e)
+    )(*fields, held, side, later, own_map, got_a, got_b, lines, *got_c, *got_d, *got_e)
 
 
 def solution(mesh):

time: 24.2 us -> 22.1 us (0.913)
  Pallas kernels: 5.77 us -> 4.86 us
  waiting for transfers between devices: 4.16 us -> 3.54 us
  starting transfers between devices: 13.1 us -> 12.8 us
    ppermute x5, waiting for transfers between devices: 4.16 us -> 0.93 us  [permute(): return lax.ppermute(array, 'gx', [(source_of(i), i) for i in range(n)])]
    all_to_all x1, waiting for transfers between devices: 0.01 us -> 2.61 us  [body(): got_t = lax.all_to_all(out_t, 'gx', split_axis=0, concat_axis=0, tiled=True)]
    pallas_call x1, Pallas kernels: 3.04 us -> 2.11 us  [body(): pl.pallas_call(functools.partial(wave_kernel, n), out_shape=[jax.ShapeDty...]
    pallas_call x1 -> x2, Pallas kernels: 0.01 us -> 0.54 us  [the longest x1 0.49 us: body(): pl.pallas_call(functools.partial(tile_kernel, n), out_shape=vmem(line_lay...]
    pallas_call x1, Pallas kernels: 2.73 us -> 2.21 us  [body(): pl.pallas_call(functools.partial(pack_kernel, n, tile_lambda.shape[0]), o...]
  transfers between devices with their start and end apart: 6 -> 6, of which waited for: 1 -> 3; matrix products, arithmetic and copies ran while one was open for 0% -> 0% of each run, Pallas kernels for 0% -> 2%
where the time goes in v4:
time: 22.1 us; the launch traced here: 21.9 us
  starting transfers between devices  12.8 us (58%)
  Pallas kernels  4.86 us (22%)
  waiting for transfers between devices  3.54 us (16%)
  between operations  0.68 us (3%)
    ppermute x5, starting transfers between devices, permute(): return lax.ppermute(array, 'gx', [(source_of(i), i) for i in range(n)])  8.89 us
    all_to_all x1, starting transfers between devices, body(): got_t = lax.all_to_all(out_t, 'gx', split_axis=0, concat_axis=0, tiled=True)  3.91 us
    all_to_all x1, waiting for transfers between devices, body(): got_t = lax.all_to_all(out_t, 'gx', split_axis=0, concat_axis=0, tiled=True)  2.61 us
    pallas_call x1, Pallas kernels, body(): pl.pallas_call(functools.partial(pack_kernel, n, tile_lambda.shape[0]), o...  2.21 us
    pallas_call x1, Pallas kernels, body(): pl.pallas_call(functools.partial(wave_kernel, n), out_shape=[jax.ShapeDty...  2.11 us
    ppermute x5, waiting for transfers between devices, permute(): return lax.ppermute(array, 'gx', [(source_of(i), i) for i in range(n)])  0.93 us
    pallas_call x1, Pallas kernels, body(): pl.pallas_call(functools.partial(tile_kernel, n), out_shape=vmem(line_lay...  0.49 us
  transfers between devices with their start and end apart: 6, of which 3 were waited for; matrix products, arithmetic and copies ran while one was open for 0% of the time, Pallas kernels for 2%

profile of v4, /device:TPU:0, one launch (start us, length us, event | category | flops | bytes accessed | tf_op | source)
XLA Modules:
  0.0 21.9 jit_solution(12754490686077652542)
XLA Ops:
  0.6 2.2 %pack.1 = (f32[160,128]{1,0:T(8,128)S(1)}, f32[160,128]{1,0:T(8,128)S(1)}, bf16[48,128]{1,0:T(8,128)(2,1)S(1)}, bf16[48,128]{1,0:T(8,128)(2,1)S(1)}, f32[8,128]{...) custom-call(bf16[8,256]{1,0:T(8,128)(2,1)} %refs_0_.1, ...), custom_call_target="tpu_custom_call" | custom-call | tf_op jit(solution)/shard_map/pack/pallas_call | solution.py:731
  2.9 4.1 %collective-permute-start = (bf16[624,128]{1,0:T(8,128)(2,1)S(1)}, bf16[624,128]{1,0:T(8,128)(2,1)S(1)}, u32[]{:S(2)}, u32[]{:S(2)}) collective-permute-start(bf16[624,128]{1,0:T(8,128)(2,1)S(1)} %get-tuple-element.29), channel_id=1, source_target_pairs={{8,0},{9,1},{10,2},{11,3},{12,4},{13,5},{14,6},{15,7},{0,8},{1,9},... | collective-permute-start | bytes 479240 | tf_op jit(solution)/shard_map/ppermute | solution.py:769
  7.0 3.9 %all-to-all-start = ((bf16[16,16,128]{2,1,0:T(8,128)(2,1)}), bf16[16,16,128]{2,1,0:T(8,128)(2,1)S(1)}, u32[]{:S(2)}, u32[]{:S(2)}) async-start(bf16[16,16,128]{2,1,0:T(8,128)(2,1)} %bitcast.2), calls=%async_computation | async-start | bytes 131072 | tf_op jit(solution)/shard_map/all_to_all | solution.py:776
  10.9 0.4 %collective-permute-start.1 = (f32[160,128]{1,0:T(8,128)S(1)}, f32[160,128]{1,0:T(8,128)S(1)}, u32[]{:S(2)}, u32[]{:S(2)}) collective-permute-start(f32[160,128]{1,0:T(8,128)S(1)} %get-tuple-element.32), channel_id=1, source_target_pairs={{1,0},{0,1},{3,2},{2,3},{5,4},{4,5},{7,6},{6,7},{9,8},{8,9},{11,10... | collective-permute-start | bytes 245768 | tf_op jit(solution)/shard_map/ppermute | solution.py:769
  11.3 4.3 %collective-permute-start.2 = (f32[160,128]{1,0:T(8,128)S(1)}, f32[160,128]{1,0:T(8,128)S(1)}, u32[]{:S(2)}, u32[]{:S(2)}) collective-permute-start(f32[160,128]{1,0:T(8,128)S(1)} %get-tuple-element.33), channel_id=1, source_target_pairs={{15,0},{2,1},{1,2},{4,3},{3,4},{6,5},{5,6},{8,7},{7,8},{10,9},{9,1... | collective-permute-start | bytes 245768 | tf_op jit(solution)/shard_map/ppermute | solution.py:769
  15.7 0.0 collective-permute-start.3
  15.7 0.0 collective-permute-start.4
  15.7 2.6 %all-to-all-done = bf16[16,16,128]{2,1,0:T(8,128)(2,1)S(1)} async-done(((bf16[16,16,128]{2,1,0:T(8,128)(2,1)}), bf16[16,16,128]{2,1,0:T(8,128)(2,1)S(1)}, u32[]{:S(2)}, u32[]{:S(2)}) %all-to-all-start) | async-done | bytes 65568 | tf_op jit(solution)/shard_map/all_to_all | solution.py:776
  18.3 0.5 %tiles.1.refs_14_ = f32[4096,128]{1,0:T(8,128)S(1)} custom-call(bf16[256,128]{1,0:T(8,128)(2,1)S(1)} %bitcast.4), custom_call_target="tpu_custom_call" | custom-call | tf_op jit(solution)/shard_map/tiles/pallas_call | solution.py:787
  18.8 0.0 collective-permute-done.refs_0_.refs_15_
  18.8 0.1 sides.1.refs_9_
  18.8 0.8 %collective-permute-done.3.refs_16_ = bf16[48,128]{1,0:T(8,128)(2,1)S(1)} collective-permute-done((bf16[48,128]{1,0:T(8,128)(2,1)S(1)}, bf16[48,128]{1,0:T(8,128)(2,1)S(1)}, u32[]{:S(2)}, u32[]{:S(2)}) %collective-permute-start.3) | collective-permute-done | bytes 12320 | tf_op jit(solution)/shard_map/ppermute | solution.py:769
  19.7 0.1 collective-permute-done.4.refs_17_
  19.8 0.0 collective-permute-done.1.refs_12_
  19.8 0.0 collective-permute-done.2.refs_13_
  19.8 2.1 %wave.1 = (f32[3,1,4,32,128]{4,3,2,1,0:T(8,128)}, f32[6,1,4,32,128]{4,3,2,1,0:T(8,128)}, f32[6,1,4,32,128]{4,3,2,1,0:T(8,128)}) custom-call(f32[3,1,4,32,128]{4,3,2,1,0:T(8,128)S(1)} %get-tuple-element.20.refs_0_, f32[6,1,4,32,128]{4,3,2,1,0:T(8,128)S(1)} %get-tuple-element.21.refs_1_, f32[6,1,4,32,128]{4,3,2,1,0:T(8,128)S(1)} %get-tuple-element.22.refs_2_, ...), custom_call_target="tpu_custom_call" | custom-call | tf_op jit(solution)/shard_map/wave/pallas_call | solution.py:797
Async XLA Ops:
  2.9 15.9 %collective-permute-start = (bf16[624,128]{1,0:T(8,128)(2,1)S(1)}, bf16[624,128]{1,0:T(8,128)(2,1)S(1)}, u32[]{:S(2)}, u32[]{:S(2)}) collective-permute-start(bf16[624,128]{1,0:T(8,128)(2,1)S(1)} %get-tuple-element.29), channel_id=1, source_target_pairs={{8,0},{9,1},{10,2},{11,3},{12,4},{13,5},{14,6},{15,7},{0,8},{1,9},... | collective-permute-start | bytes 479240 | tf_op jit(solution)/shard_map/ppermute | solution.py:769
  7.0 11.3 %all-to-all-start = ((bf16[16,16,128]{2,1,0:T(8,128)(2,1)}), bf16[16,16,128]{2,1,0:T(8,128)(2,1)S(1)}, u32[]{:S(2)}, u32[]{:S(2)}) async-start(bf16[16,16,128]{2,1,0:T(8,128)(2,1)} %bitcast.2), calls=%async_computation | async-start | bytes 131072 | tf_op jit(solution)/shard_map/all_to_all | solution.py:776
  10.9 8.9 %collective-permute-start.1 = (f32[160,128]{1,0:T(8,128)S(1)}, f32[160,128]{1,0:T(8,128)S(1)}, u32[]{:S(2)}, u32[]{:S(2)}) collective-permute-start(f32[160,128]{1,0:T(8,128)S(1)} %get-tuple-element.32), channel_id=1, source_target_pairs={{1,0},{0,1},{3,2},{2,3},{5,4},{4,5},{7,6},{6,7},{9,8},{8,9},{11,10... | collective-permute-start | bytes 245768 | tf_op jit(solution)/shard_map/ppermute | solution.py:769
  11.3 8.4 %collective-permute-start.2 = (f32[160,128]{1,0:T(8,128)S(1)}, f32[160,128]{1,0:T(8,128)S(1)}, u32[]{:S(2)}, u32[]{:S(2)}) collective-permute-start(f32[160,128]{1,0:T(8,128)S(1)} %get-tuple-element.33), channel_id=1, source_target_pairs={{15,0},{2,1},{1,2},{4,3},{3,4},{6,5},{5,6},{8,7},{7,8},{10,9},{9,1... | collective-permute-start | bytes 245768 | tf_op jit(solution)/shard_map/ppermute | solution.py:769
  15.7 4.0 %collective-permute-start.3 = (bf16[48,128]{1,0:T(8,128)(2,1)S(1)}, bf16[48,128]{1,0:T(8,128)(2,1)S(1)}, u32[]{:S(2)}, u32[]{:S(2)}) collective-permute-start(bf16[48,128]{1,0:T(8,128)(2,1)S(1)} %get-tuple-element.35), channel_id=1, source_target_pairs={{7,0},{10,1},{9,2},{12,3},{11,4},{14,5},{13,6},{0,7},{15,8},{2,9},... | collective-permute-start | bytes 36872 | tf_op jit(solution)/shard_map/ppermute | solution.py:769
  15.7 4.1 %collective-permute-start.4 = (bf16[48,128]{1,0:T(8,128)(2,1)S(1)}, bf16[48,128]{1,0:T(8,128)(2,1)S(1)}, u32[]{:S(2)}, u32[]{:S(2)}) collective-permute-start(bf16[48,128]{1,0:T(8,128)(2,1)S(1)} %get-tuple-element.36), channel_id=1, source_target_pairs={{9,0},{8,1},{11,2},{10,3},{13,4},{12,5},{15,6},{14,7},{1,8},{0,9},... | collective-permute-start | bytes 36872 | tf_op jit(solution)/shard_map/ppermute | solution.py:769

commit v5 on v4

--- a/solution.py
+++ b/solution.py
@@ -308,8 +308,7 @@
     cell, spot = sublane((2 * LANES, LANES)), lane((2 * LANES, LANES))
     half = lax.rem(spot, 64)
     cells = half // 16 * 64 + lax.rem(half, 16)
-    low = jnp.logical_and(spot < 64, cell == cells).astype(BF16)
-    high = jnp.logical_and(spot >= 64, cell == cells + 48).astype(BF16)
+    ends = (cell == cells + jnp.where(spot < 64, 0, 48)).astype(BF16)
     left = lane((n, LANES)) < 64
     if chunk > 9 + 7 * len(sides_of(n)):
         rows[...] = jnp.zeros_like(rows)
@@ -317,18 +316,20 @@
     def put(j, value):
         rows[pl.ds(j, n, stride=chunk), :] = value
 
-    for p, near in enumerate((near_lam, near_mu, near_bu)):
-        tile = near[...]
+    tiles = [near[...] for near in (near_lam, near_mu, near_bu)]
+    stacked = jnp.concatenate([tile.astype(F32) for tile in tiles], 0).astype(BF16)
+    halves = jnp.dot(stacked, ends, preferred_element_type=F32)
+    for p, tile in enumerate(tiles):
         whole = jnp.dot(route, tile, preferred_element_type=F32)
-        first = jnp.dot(route, jnp.dot(tile, low, preferred_element_type=F32).astype(BF16), preferred_element_type=F32)
-        final = jnp.dot(route, jnp.dot(tile, high, preferred_element_type=F32).astype(BF16), preferred_element_type=F32)
+        outer = halves[p * per : (p + 1) * per].astype(BF16)
+        outer = jnp.dot(route, outer, preferred_element_type=F32)
 
         def slot(x, k):
             return x[k * n : (k + 1) * n]
 
         put(2 * p, slot(whole, 0)[:, :LANES])
         put(2 * p + 1, slot(whole, 0)[:, LANES:])
-        put(6 + p, slot(first, 1) + slot(final, 2))
+        put(6 + p, jnp.where(left, slot(outer, 1), slot(outer, 2)))
         for g in range(len(sides_of(n))):
             side = slot(whole, 3 + 3 * g)
             base = 9 + 7 * g
@@ -337,7 +338,7 @@
             else:
                 put(base + 2, side[:, :LANES])
                 put(base + 3, side[:, LANES:])
-            put(base + 4 + p, slot(first, 4 + 3 * g) + slot(final, 5 + 3 * g))
+            put(base + 4 + p, jnp.where(left, slot(outer, 4 + 3 * g), slot(outer, 5 + 3 * g)))
     out[...] = rows[...].astype(BF16)
 
 
@@ -378,7 +379,9 @@
     return jnp.where(whole, main, jnp.concatenate(only, 0))
 
 
+PLAIN = GAIN + 1
 SIDES = [("before", f, i) for f, i in LAST] + [("after", f, i) for f, i in FIRST]
+SIDE_PROPS = [s for s in SIDES if s[1] in (LAME, MU, BUOY)]
 
 
 def side_kernel(n, *refs):
@@ -407,175 +410,85 @@
                 side[k, ROWS:EXT] = halo
 
 
-def line_layout(n):
-    at, layout = 0, {}
-    spans = [(2 * p, 2) for p in range(3)] + [(6 + p, 1) for p in range(3)]
-    for g in range(len(sides_of(n))):
-        spans += [(9 + 7 * g, 1), (10 + 7 * g, 1), (11 + 7 * g, 2)] + [(13 + 7 * g + p, 1) for p in range(3)]
-    for row, halves in spans:
-        layout[row] = at, halves
-        at += n * 16 * halves
-    return layout, at
-
-
-def tile_kernel(n, got_t, out, rows_t, spread_rows):
+def tile_kernel(n, *refs):
+    sides = len(sides_of(n))
+    (lam, mu, bu, maps, got_t) = refs[:5]
+    got_c = refs[5 : 5 + sides]
+    own, side, corner, rows_t, spread_rows, tile_rows, ends = refs[5 + sides :]
     chunk = tile_chunk(n)
     rows_t[...] = got_t[...].astype(F32)
     on_line = lane((16, LANES)) // TZ == sublane((16, LANES))
     spread = (lax.rem(sublane((LANES, LANES)), TZ) == lax.rem(lane((LANES, LANES)), TZ)).astype(BF16)
-    for row, (base, halves) in line_layout(n)[0].items():
-
-        def group(q, _, row=row, base=base, halves=halves):
-            for s in range(16):
-                for h in range(halves):
-                    value = rows_t[pl.ds((q * 16 + s) * chunk + row + h, 1), :]
-                    value = jnp.where(on_line, jnp.broadcast_to(value, (16, LANES)), 0.0)
-                    at = (s * halves + h) * 16
-                    spread_rows[at : at + 16, :] = value.astype(BF16)
-            size = 256 * halves
-            done = jnp.dot(spread_rows[0:size, :], spread, preferred_element_type=F32)
-            out[pl.ds(base + q * size, size), :] = done
-            return 0
-
-        if n == 16:
-            group(0, 0)
-        else:
-            lax.fori_loop(0, n // 16, group, 0)
-
-
-def wave_kernel(n, *refs):
-    merged = is_merged(n)
-    (vel, st, mem, lam, mu, bu, dec, los, kept, side, source, maps, got_a, got_b, lines) = refs[:15]
-    refs = refs[15:]
-    sides = len(sides_of(n))
-    got_c, got_d, got_e = refs[:sides], refs[sides : 2 * sides], refs[2 * sides : 3 * sides]
-    far_outs, refs = refs[3 * sides : 3 * sides + 3], refs[3 * sides + 3 :]
-    near_rows, far_rows, end_rows, new_v, new_s, new_m, sems = refs
-    b = lax.axis_index("gx")
-    even = lax.rem(b, 2) == 0
-    sub = sublane((8, LANES))
-    layout, _ = line_layout(n)
-
-    def overlay(row, wanted):
-        base, halves = layout[row]
-
-        def take(s, values):
+
+    def lines(first, row, halves):
+        for s in range(16):
+            for h in range(halves):
+                value = rows_t[pl.ds((first + s) * chunk + row + h, 1), :]
+                value = jnp.where(on_line, jnp.broadcast_to(value, (16, LANES)), 0.0)
+                at = (s * halves + h) * 16
+                spread_rows[at : at + 16, :] = value.astype(BF16)
+        return jnp.dot(spread_rows[0 : 256 * halves, :], spread, preferred_element_type=F32)
+
+    def overlay(row, halves, wanted):
+        def take(first, values):
+            tile_rows[0 : 256 * halves, :] = lines(first, row, halves)
             done = []
             for value, (_, owner, at) in zip(values, wanted):
-                here = lines[pl.ds(base + s * halves * 16 + at, 8), :]
-                done.append(jnp.where(owner == s.astype(F32) if n > 16 else owner == s * 1.0, here, value))
+                for s in range(16):
+                    here = tile_rows[s * halves * 16 + at : s * halves * 16 + at + 8, :]
+                    value = jnp.where(owner == (first + s) * 1.0, here, value)
+                done.append(value)
             return done
 
         values = [w[0] for w in wanted]
         if n == 16:
-            for s in range(n):
-                values = take(s, values)
-            return values
-        return lax.fori_loop(0, n, take, values)
-
-    column = {}
+            return take(0, values)
+        return lax.fori_loop(0, n // 16, lambda g, v: take(g * 16, v), values)
+
     rows_y = ROWS // TY
 
-    def own(f, i):
-        if f < VEL:
-            return st[f, 0, i]
-        if f < HELD:
-            return vel[f - VEL, 0, i]
-        if f < GAIN:
-            return kept[f - HELD, i]
-        if f == GAIN:
-            return courant * (1.0 - (1.0 - dec[0, i]) * los[0, i])
-        return (lam, mu, bu)[f - LAME][0, i]
-
-    def main_tiles(mains, owners, row, line_of):
+    def main_tiles(mains, owners, row, halves, line_of):
         wanted = []
         for i, m in mains.items():
             for p in range(rows_y):
                 owner = jnp.broadcast_to(owners[p : p + 1], (8, LANES))
                 wanted.append((m[p * 8 : (p + 1) * 8], owner, line_of(i)))
-        laid = overlay(row, wanted)
+        laid = overlay(row, halves, wanted)
         return {i: jnp.concatenate(laid[k * rows_y : (k + 1) * rows_y], 0) for k, i in enumerate(mains)}
 
-    def halo_tiles(halos, after, before, row):
-        zeros = jnp.zeros((8, LANES), F32)
-        blocks = overlay(row, [(zeros, after, 0), (zeros, before, 8)])
-        covered = jnp.where(sub < 4, after, before) >= 0.0
-        return {i: jnp.where(covered, halo_rows(blocks, i), h) for i, h in halos.items()}
-
-    after, before = halo_blocks(even, got_a, got_b, FIELDS)
-    for f in range(FIELDS):
-        blocks = halo_blocks(even, got_a, got_b, f)
-        main = {i: own(f, i) for i in range(4)}
-        halo = {i: halo_rows(blocks, i) for i in range(4)}
-        if f >= LAME:
-            p = f - LAME
-            main = main_tiles(main, maps[...], 2 * p, lambda i: i * 8)
-            halo = halo_tiles(halo, after, before, 6 + p)
+    for p, ref in enumerate((lam, mu, bu)):
+        main = main_tiles({i: ref[0, i] for i in range(4)}, maps[...], 2 * p, 2, lambda i: i * 8)
         for i in range(4):
-            column["own", f, i] = jnp.concatenate([main[i], halo[i]], 0)
-
-    def corner_rows(table, rows, f, i):
-        value = None
-        for k, (g, j, r) in enumerate(rows):
-            if (g, j) == (f, i):
-                row = jnp.broadcast_to(table[k : k + 1, :], (8, LANES))
-                value = jnp.where(sub == (r % 8), row, 0.0 if value is None else value)
-        return value
-
-    no_rows, no_halo = jnp.zeros((ROWS, LANES), F32), jnp.zeros((8, LANES), F32)
-    face = {}
-    for order, (name, which) in enumerate((("before", LAST), ("after", FIRST))):
-        group = 0 if merged else order
-        message = got_c[group]
-        base = (LONGEST if merged else len(which)) * ROWS
-        if group == order:
-            near, far = got_e[group][...].astype(F32), got_d[group][...].astype(F32)
-            near_rows[...] = jnp.where(even, near, far)
-            far_rows[...] = jnp.where(even, far, near)
-            end_rows[...] = message[base : base + 16, :].astype(F32)
-        after = jnp.broadcast_to(near_rows[len(ABOVE) : len(ABOVE) + 1, :], (8, LANES))
-        before = jnp.broadcast_to(far_rows[len(BELOW) : len(BELOW) + 1, :], (8, LANES))
-        owners = end_rows[8:16, :][ENDS_MAP - 8 :]
+            own[p, i] = main[i]
+    for at, (name, which, message, base, whole) in enumerate(side_messages(n, got_c)):
+        group = 0 if whole is not None else at
+        ends[...] = message[base : base + 16, :].astype(F32)
+        owners = ends[8:16, :][ENDS_MAP - 8 :]
         row = 9 + 7 * group
-
-        def main_rows(f, i):
-            return side[SIDES.index((name, f, i)), 0:ROWS] if (f, i) in which else no_rows
-
-        def corner_halo(f, i):
-            above = corner_rows(near_rows, ABOVE, f, i)
-            below = corner_rows(far_rows, BELOW, f, i)
-            if above is None or below is None:
-                return no_halo if above is below else (below if above is None else above)
-            return jnp.where(sub < 4, above, below)
-
-        edge = 3 if name == "before" else 0
-        layers = (2, 3) if name == "before" else (0, 1)
-        for f in range(FIELDS):
-            present = [i for i in layers if f < VEL or f in range(HELD, GAIN) or (f, i) in which]
-            halo = {i: corner_halo(f, i) for i in present}
-            main = {i: no_rows if f < VEL else main_rows(f, i) for i in present}
+        for f in (LAME, MU, BUOY):
+            main = {i: side_rows(which, message, whole, ends, f, i) for g, i in which if g == f}
             if f == BUOY:
-                main = main_tiles(main, owners, row + 2, lambda i: i * 8)
-            elif f >= LAME:
-                main = main_tiles(main, owners, row + f - LAME, lambda i: 8 if i else 0)
-            if f >= LAME:
-                halo = halo_tiles(halo, after, before, row + 4 + f - LAME)
-            for i in present:
-                column[name, f, i] = jnp.concatenate([main[i], halo[i]], 0)
-            if f < VEL and (f, edge) in which:
-                face[name, f] = jnp.concatenate([main_rows(f, edge), halo[edge]], 0)
-        for f, i in which:
-            if isinstance(f, str):
-                column[name, f, i] = side[SIDES.index((name, f, i))]
-
-    def layers_of(f):
-        names = [("before", 2), ("before", 3)] + [("own", i) for i in range(4)] + [("after", 0), ("after", 1)]
-        return [column.get((name, f, i)) for name, i in names]
-
-    s0 = [layers_of(STRESS + c) for c in range(6)]
-    v0 = [layers_of(VEL + c) for c in range(3)]
-    held = [layers_of(HELD + c) for c in range(6)]
-    gain, lame, shear, buoy = (layers_of(f) for f in (GAIN, LAME, MU, BUOY))
+                main = main_tiles(main, owners, row + 2, 2, lambda i: i * 8)
+            else:
+                main = main_tiles(main, owners, row + f - LAME, 1, lambda i: 8 if i else 0)
+            for i, value in main.items():
+                side[SIDE_PROPS.index((name, f, i))] = value
+    for g in range(1 + sides):
+        for p in range(3):
+            row = 6 + 7 * g + p
+            if n == 16:
+                corner[3 * g + p] = lines(0, row, 1)
+            else:
+
+                def spread_group(q, _, g=g, p=p, row=row):
+                    corner[3 * g + p, pl.ds(q * 256, 256)] = lines(q * 16, row, 1)
+                    return 0
+
+                lax.fori_loop(0, n // 16, spread_group, 0)
+
+
+def rules(n, lame, shear, buoy):
+    b = lax.axis_index("gx")
 
     tall = sublane((EXT, LANES))
 
@@ -612,23 +525,20 @@
 
     z_next, z_prev = z_after, z_before
 
-    def move(v, s, spans, sums, faces):
-        new = [[None] * 8 for _ in range(3)]
-
-        def add(d, l, grad):
+    def move(new, v, s, l, spans, sums, faces):
+        def add(d, grad):
             if sums[d][l] is not None:
                 grad = sums[d][l] + grad
             new[d][l] = v[d][l] + courant * buoy[l] * grad
 
-        for l in spans[0]:
+        if l in spans[0]:
             ahead = x_next(s[XX], l, faces.get(XX))
-            add(0, l, (ahead - s[XX][l]) + (s[XY][l] - y_prev(s[XY][l])) + (s[XZ][l] - z_prev(s[XZ][l])))
-        for l in spans[1]:
+            add(0, (ahead - s[XX][l]) + (s[XY][l] - y_prev(s[XY][l])) + (s[XZ][l] - z_prev(s[XZ][l])))
+        if l in spans[1]:
             behind = x_prev(s[XY], l, faces.get(XY))
-            add(1, l, (s[XY][l] - behind) + (y_next(s[YY][l]) - s[YY][l]) + (s[YZ][l] - z_prev(s[YZ][l])))
+            add(1, (s[XY][l] - behind) + (y_next(s[YY][l]) - s[YY][l]) + (s[YZ][l] - z_prev(s[YZ][l])))
             behind = x_prev(s[XZ], l, faces.get(XZ))
-            add(2, l, (s[XZ][l] - behind) + (s[YZ][l] - y_prev(s[YZ][l])) + (z_next(s[ZZ][l]) - s[ZZ][l]))
-        return new
+            add(2, (s[XZ][l] - behind) + (s[YZ][l] - y_prev(s[YZ][l])) + (z_next(s[ZZ][l]) - s[ZZ][l]))
 
     def rates_at(v, l, wanted):
         out = [None] * 6
@@ -648,19 +558,169 @@
             out[YZ] = shear[l] * ((z_next(v[1][l]) - v[1][l]) + (y_next(v[2][l]) - v[2][l]))
         return out
 
+    return move, rates_at, link_before, link_after
+
+
+def tile_rows_around(n, line_tiles, group, after, before):
+    laid = []
+    for p in range(3):
+        low = high = jnp.zeros((8, LANES), F32)
+        for s in range(n):
+            low = jnp.where(after == s * 1.0, line_tiles[3 * group + p, s * 16 : s * 16 + 8], low)
+            high = jnp.where(before == s * 1.0, line_tiles[3 * group + p, s * 16 + 8 : s * 16 + 16], high)
+        laid.append((low, high))
+    return laid, jnp.where(sublane((8, LANES)) < 4, after, before) >= 0.0
+
+
+OUTER = (2, 5)
+INNER = (3, 4)
+
+
+def first_kernel(n, *refs):
+    (vel, st, mem, dec, los, kept, side, own_props, line_tiles, got_a, got_b) = refs[:11]
+    out_props, out_gain, out_held, out_cross, out_v, out_s, out_m = refs[11:]
+    even = lax.rem(lax.axis_index("gx"), 2) == 0
+    laid, covered = tile_rows_around(n, line_tiles, 0, *halo_blocks(even, got_a, got_b, FIELDS))
+    column = {}
+    for f in range(FIELDS):
+        blocks = halo_blocks(even, got_a, got_b, f)
+        for i in range(4):
+            halo = halo_rows(blocks, i)
+            if f >= LAME:
+                halo = jnp.where(covered, halo_rows(laid[f - LAME], i), halo)
+            if f < VEL:
+                main = st[f, 0, i]
+            elif f < HELD:
+                main = vel[f - VEL, 0, i]
+            elif f < GAIN:
+                main = kept[f - HELD, i]
+            elif f == GAIN:
+                main = courant * (1.0 - (1.0 - dec[0, i]) * los[0, i])
+            else:
+                main = own_props[f - LAME, i]
+            column[f, i] = jnp.concatenate([main, halo], 0)
+
+    def layers_of(f):
+        return [None, None] + [column[f, i] for i in range(4)] + [None, None]
+
+    def face_of(name, c, i):
+        return jnp.concatenate([side[SIDES.index((name, STRESS + c, i)), 0:ROWS], jnp.zeros((8, LANES), F32)], 0)
+
+    s0 = [layers_of(STRESS + c) for c in range(6)]
+    v0 = [layers_of(VEL + c) for c in range(3)]
+    held = [layers_of(HELD + c) for c in range(6)]
+    gain, lame, shear, buoy = (layers_of(f) for f in (GAIN, LAME, MU, BUOY))
+    move, rates_at, _, _ = rules(n, lame, shear, buoy)
+    faces = {XX: face_of("after", XX, 0), XY: face_of("before", XY, 3), XZ: face_of("before", XZ, 3)}
+    v1 = [[None] * 8 for _ in range(3)]
+    for l in range(2, 6):
+        move(v1, v0, s0, l, (range(2, 6), range(2, 6)), [[None] * 8] * 3, faces)
+        for c in range(3):
+            out_v[c, l - 2] = v1[c][l]
+        out_gain[l - 2] = gain[l]
+        for p, values in enumerate((lame, shear, buoy)):
+            out_props[p, l - 2] = values[l]
+    for k, l in enumerate(OUTER):
+        for c in range(6):
+            out_held[c, k] = held[c][l]
+    for k, value in enumerate((s0[XX][2], s0[XY][5], s0[XZ][5])):
+        out_cross[k] = value
+    for k, l in enumerate(INNER):
+        i = l - 2
+        rates = rates_at(v1, l, range(6))
+        lost = (1.0 - dec[0, i]) * los[0, i]
+        for c in range(6):
+            out_s[c, k] = held[c][l] + gain[l] * rates[c]
+            out_m[c, k] = dec[0, i] * mem[c, 0, i] - lost * rates[c][:ROWS]
+
+
+def wave_kernel(n, *refs):
+    merged = is_merged(n)
+    sides = len(sides_of(n))
+    (mem, dec, los, side, source, side_props, line_tiles) = refs[:7]
+    (own_props, own_gain, own_held, cross, own_v, own_s, own_m) = refs[7:14]
+    got_d, got_e = refs[14 : 14 + sides], refs[14 + sides : 14 + 2 * sides]
+    refs = refs[14 + 2 * sides :]
+    far_outs, (near_rows, far_rows, new_v, new_s, new_m, sems) = refs[:3], refs[3:]
+    even = lax.rem(lax.axis_index("gx"), 2) == 0
+    sub = sublane((8, LANES))
+    no_rows, no_halo = jnp.zeros((ROWS, LANES), F32), jnp.zeros((8, LANES), F32)
+
+    column = {}
+    for i in range(4):
+        column["own", GAIN, i] = own_gain[i]
+        for p in range(3):
+            column["own", LAME + p, i] = own_props[p, i]
+    for k, l in enumerate(OUTER):
+        for c in range(6):
+            column["own", HELD + c, l - 2] = own_held[c, k]
+    for k, (c, i) in enumerate(((XX, 0), (XY, 3), (XZ, 3))):
+        column["own", STRESS + c, i] = cross[k]
+
+    def corner_rows(table, rows, f, i):
+        value = None
+        for k, (g, j, r) in enumerate(rows):
+            if (g, j) == (f, i):
+                row = jnp.broadcast_to(table[k : k + 1, :], (8, LANES))
+                value = jnp.where(sub == (r % 8), row, 0.0 if value is None else value)
+        return value
+
+    face = {}
+    for at, (name, which) in enumerate((("before", LAST), ("after", FIRST))):
+        group = 0 if merged else at
+        if group == at:
+            near, far = got_e[group][...].astype(F32), got_d[group][...].astype(F32)
+            near_rows[...] = jnp.where(even, near, far)
+            far_rows[...] = jnp.where(even, far, near)
+            after = jnp.broadcast_to(near_rows[len(ABOVE) : len(ABOVE) + 1, :], (8, LANES))
+            before = jnp.broadcast_to(far_rows[len(BELOW) : len(BELOW) + 1, :], (8, LANES))
+            laid, covered = tile_rows_around(n, line_tiles, 1 + group, after, before)
+
+        def corner_halo(f, i):
+            above = corner_rows(near_rows, ABOVE, f, i)
+            below = corner_rows(far_rows, BELOW, f, i)
+            if above is None or below is None:
+                halo = no_halo if above is below else (below if above is None else above)
+            else:
+                halo = jnp.where(sub < 4, above, below)
+            if f >= LAME:
+                halo = jnp.where(covered, halo_rows(laid[f - LAME], i), halo)
+            return halo
+
+        edge = 3 if name == "before" else 0
+        layers = (2, 3) if name == "before" else (0, 1)
+        for f in range(FIELDS):
+            for i in layers:
+                if not (f < VEL or f in range(HELD, GAIN) or (f, i) in which):
+                    continue
+                halo = corner_halo(f, i)
+                main = no_rows
+                if f >= LAME:
+                    main = side_props[SIDE_PROPS.index((name, f, i))]
+                elif (f, i) in which:
+                    main = side[SIDES.index((name, f, i)), 0:ROWS]
+                if f < VEL:
+                    column[name, f, i] = jnp.concatenate([no_rows, halo], 0)
+                    if (f, i) in which:
+                        face[name, f] = jnp.concatenate([main, halo], 0)
+                else:
+                    column[name, f, i] = jnp.concatenate([main, halo], 0)
+        for f, i in which:
+            if isinstance(f, str):
+                column[name, f, i] = side[SIDES.index((name, f, i))]
+
+    def layers_of(f):
+        names = [("before", 2), ("before", 3)] + [("own", i) for i in range(4)] + [("after", 0), ("after", 1)]
+        return [column.get((name, f, i)) for name, i in names]
+
+    s0 = [layers_of(STRESS + c) for c in range(6)]
+    v0 = [layers_of(VEL + c) for c in range(3)]
+    held = [layers_of(HELD + c) for c in range(6)]
+    gain, lame, shear, buoy = (layers_of(f) for f in (GAIN, LAME, MU, BUOY))
+
+    move, rates_at, link_before, link_after = rules(n, lame, shear, buoy)
     faces = {XX: face["after", STRESS + XX], XY: face["before", STRESS + XY], XZ: face["before", STRESS + XZ]}
-    v1 = move(v0, s0, (range(0, 7), range(1, 8)), [layers_of(g) for g in ("gx", "gy", "gz")], faces)
-    s1 = [[None] * 8 for _ in range(6)]
-    m1 = {}
-    for l in range(1, 7):
-        wanted = (XX, XY, XZ) if l == 1 else range(6)
-        rates = rates_at(v1, l, wanted)
-        for c in wanted:
-            s1[c][l] = held[c][l] + gain[l] * rates[c]
-            if 2 <= l < 6:
-                d = dec[0, l - 2]
-                m1[c, l] = d * mem[c, 0, l - 2] - (1.0 - d) * los[0, l - 2] * rates[c][:ROWS]
-    v2 = move(v1, s1, (range(1, 6), range(2, 7)), [layers_of(h) for h in (None, "hy", "hz")], {})
+    faces = {XX: face["after", STRESS + XX], XY: face["before", STRESS + XY], XZ: face["before", STRESS + XZ]}
     copies = []
 
     def send(k, i):
@@ -668,25 +728,60 @@
         copies.append(pltpu.make_async_copy(near.at[:, :, i], far.at[:, :, i], sems.at[k, i]))
         copies[-1].start()
 
-    for i in range(4):
+    v1, v2 = ([[None] * 8 for _ in range(3)] for _ in range(2))
+    s1 = [[None] * 8 for _ in range(6)]
+    m1 = {}
+    sums1 = [layers_of(g) for g in ("gx", "gy", "gz")]
+    sums2 = [layers_of(h) for h in (None, "hy", "hz")]
+    for l in range(2, 6):
         for c in range(3):
-            new_v[c, 0, i] = v2[c][i + 2][:ROWS]
-        send(0, i)
-    for i in range(4):
-        l = i + 2
-        rates = rates_at(v2, l, range(6))
-        d = dec[0, i]
-        lost = (1.0 - d) * los[0, i]
+            v1[c][l] = own_v[c, l - 2]
+    for k, l in enumerate(INNER):
         for c in range(6):
-            rate = rates[c][:ROWS]
-            m2 = d * m1[c, l] - lost * rate
-            new_m[c, 0, i] = m2
-            value = s1[c][l][:ROWS] + courant * (rate + m2)
-            if c < 3:
-                value = value + source[i * ROWS : (i + 1) * ROWS, :]
-            new_s[c, 0, i] = value
-        send(1, i)
-        send(2, i)
+            s1[c][l] = own_s[c, k]
+            m1[c, l] = own_m[c, k]
+
+    def at_corner(d, l, link, sign, c):
+        more = sign * courant * buoy[l][ROWS:] * jnp.where(link[ROWS:], faces[c][ROWS:], 0.0)
+        v1[d][l] = jnp.concatenate([v1[d][l][:ROWS], v1[d][l][ROWS:] + more], 0)
+
+    at_corner(0, 5, link_after, 1.0, XX)
+    at_corner(1, 2, link_before, -1.0, XY)
+    at_corner(2, 2, link_before, -1.0, XZ)
+    for at in range(9):
+        move(v1, v0, s0, at, ((0, 1, 6), (1, 6, 7)), sums1, {})
+        l = at - 1
+        if l in (1, 2, 5, 6):
+            wanted = (XX, XY, XZ) if l == 1 else range(6)
+            rates = rates_at(v1, l, wanted)
+            for c in wanted:
+                s1[c][l] = held[c][l] + gain[l] * rates[c]
+                if 2 <= l < 6:
+                    i = l - 2
+                    lost = (1.0 - dec[0, i]) * los[0, i]
+                    m1[c, l] = dec[0, i] * mem[c, 0, i] - lost * rates[c][:ROWS]
+        l = at - 2
+        move(v2, v1, s1, l, (range(1, 6), range(2, 7)), sums2, {})
+        if l in range(2, 6):
+            for c in range(3):
+                new_v[c, 0, l - 2] = v2[c][l][:ROWS]
+            send(0, l - 2)
+        l = at - 3
+        if l in range(2, 6):
+            i = l - 2
+            rates = rates_at(v2, l, range(6))
+            d = dec[0, i]
+            lost = (1.0 - d) * los[0, i]
+            for c in range(6):
+                rate = rates[c][:ROWS]
+                m2 = d * m1[c, l] - lost * rate
+                new_m[c, 0, i] = m2
+                value = s1[c][l][:ROWS] + courant * (rate + m2)
+                if c < 3:
+                    value = value + source[i * ROWS : (i + 1) * ROWS, :]
+                new_s[c, 0, i] = value
+            send(1, i)
+            send(2, i)
     for copy in copies:
         copy.wait()
 
@@ -763,7 +858,6 @@
     held, later = packed[14:16]
     out_c = packed[16:]
     dec, los, st, mem, vel, lam, mu, bu = packed[6:14]
-    fields = (vel, st, mem, lam, mu, bu, dec, los)
 
     def permute(array, source_of):
         return lax.ppermute(array, "gx", [(source_of(i), i) for i in range(n)])
@@ -784,31 +878,55 @@
         compiler_params=pltpu.CompilerParams(vmem_limit_bytes=16 * 1024 * 1024),
         name="sides",
     )(*got_c)
-    lines = pl.pallas_call(
+    own_props, side_props, line_tiles = pl.pallas_call(
         functools.partial(tile_kernel, n),
-        out_shape=vmem(line_layout(n)[1], LANES),
-        in_specs=[on_core],
-        out_specs=on_core,
-        scratch_shapes=[pltpu.VMEM((n * chunk, LANES), F32), pltpu.VMEM((16 * 32, LANES), BF16)],
-        compiler_params=pltpu.CompilerParams(vmem_limit_bytes=40 * 1024 * 1024),
+        out_shape=[
+            vmem(3, 4, ROWS, LANES),
+            vmem(len(SIDE_PROPS), ROWS, LANES),
+            vmem(3 + 3 * len(sides), n * 16, LANES),
+        ],
+        in_specs=[on_core] * (5 + len(sides)),
+        out_specs=[on_core] * 3,
+        scratch_shapes=[
+            pltpu.VMEM((n * chunk, LANES), F32),
+            pltpu.VMEM((16 * 32, LANES), BF16),
+            pltpu.VMEM((16 * 32, LANES), F32),
+            pltpu.VMEM((16, LANES), F32),
+        ],
+        compiler_params=pltpu.CompilerParams(vmem_limit_bytes=16 * 1024 * 1024),
         name="tiles",
-    )(got_t)
+    )(lam, mu, bu, own_map, got_t, *got_c)
+    first = pl.pallas_call(
+        functools.partial(first_kernel, n),
+        out_shape=[
+            vmem(3, 4, EXT, LANES),
+            vmem(4, EXT, LANES),
+            vmem(6, 2, EXT, LANES),
+            vmem(3, EXT, LANES),
+            vmem(3, 4, EXT, LANES),
+            vmem(6, 2, EXT, LANES),
+            vmem(6, 2, ROWS, LANES),
+        ],
+        in_specs=[on_core] * 11,
+        out_specs=[on_core] * 7,
+        compiler_params=pltpu.CompilerParams(vmem_limit_bytes=16 * 1024 * 1024),
+        name="first",
+    )(vel, st, mem, dec, los, held, side, own_props, line_tiles, got_a, got_b)
     outs = (velocity, stress, memory)
     return pl.pallas_call(
         functools.partial(wave_kernel, n),
         out_shape=[jax.ShapeDtypeStruct(x.shape, F32) for x in outs],
-        in_specs=[on_core] * (15 + 3 * len(sides)),
+        in_specs=[on_core] * (14 + 2 * len(sides)),
         out_specs=[away] * 3,
         scratch_shapes=[
             pltpu.VMEM((CORNER, LANES), F32),
             pltpu.VMEM((CORNER, LANES), F32),
-            pltpu.VMEM((16, LANES), F32),
         ]
         + [pltpu.VMEM(x.shape, F32) for x in outs]
         + [pltpu.SemaphoreType.DMA((3, 4))],
         compiler_params=pltpu.CompilerParams(vmem_limit_bytes=48 * 1024 * 1024),
         name="wave",
-    )(*fields, held, side, later, own_map, got_a, got_b, lines, *got_c, *got_d, *got_e)
+    )(mem, dec, los, side, later, side_props, line_tiles, *first, *got_d, *got_e)
 
 
 def solution(mesh):

time: 22.1 us -> 21.2 us (0.959)
  waiting for transfers between devices: 3.54 us -> 3.01 us
  Pallas kernels: 4.86 us -> 4.49 us
    pallas_call x1, Pallas kernels: 2.11 us -> 1.51 us  [body(): pl.pallas_call(functools.partial(wave_kernel, n), out_shape=[jax.ShapeDty...]
    pallas_call x1 -> x2, Pallas kernels: 0.49 us -> 1.01 us  [the longest x1 0.7 us: body(): pl.pallas_call(functools.partial(tile_kernel, n), out_shape=[vmem(3, 4, R...]
    ppermute x5, waiting for transfers between devices: 0.93 us -> 0.47 us  [permute(): return lax.ppermute(array, 'gx', [(source_of(i), i) for i in range(n)])]
    pallas_call x1, Pallas kernels: 2.21 us -> 1.92 us  [body(): pl.pallas_call(functools.partial(pack_kernel, n, tile_lambda.shape[0]), o...]
  transfers between devices with their start and end apart: 6 -> 6, of which waited for: 3 -> 3; matrix products, arithmetic and copies ran while one was open for 0% -> 0% of each run, Pallas kernels for 2% -> 5%
where the time goes in v5:
time: 21.2 us; the launch traced here: 21 us
  starting transfers between devices  12.8 us (60%)
  Pallas kernels  4.49 us (21%)
  waiting for transfers between devices  3.01 us (14%)
  between operations  0.69 us (3%)
    ppermute x5, starting transfers between devices, permute(): return lax.ppermute(array, 'gx', [(source_of(i), i) for i in range(n)])  8.9 us
    all_to_all x1, starting transfers between devices, body(): got_t = lax.all_to_all(out_t, 'gx', split_axis=0, concat_axis=0, tiled=True)  3.91 us
    all_to_all x1, waiting for transfers between devices, body(): got_t = lax.all_to_all(out_t, 'gx', split_axis=0, concat_axis=0, tiled=True)  2.54 us
    pallas_call x1, Pallas kernels, body(): pl.pallas_call(functools.partial(pack_kernel, n, tile_lambda.shape[0]), o...  1.92 us
    pallas_call x1, Pallas kernels, body(): pl.pallas_call(functools.partial(wave_kernel, n), out_shape=[jax.ShapeDty...  1.51 us
    pallas_call x1, Pallas kernels, body(): pl.pallas_call(functools.partial(tile_kernel, n), out_shape=[vmem(3, 4, R...  0.7 us
    ppermute x5, waiting for transfers between devices, permute(): return lax.ppermute(array, 'gx', [(source_of(i), i) for i in range(n)])  0.47 us
  transfers between devices with their start and end apart: 6, of which 3 were waited for; matrix products, arithmetic and copies ran while one was open for 0% of the time, Pallas kernels for 5%

profile of v5, /device:TPU:0, one launch (start us, length us, event | category | flops | bytes accessed | tf_op | source)
XLA Modules:
  0.0 21.0 jit_solution(8765169785977962010)
XLA Ops:
  0.6 1.9 %pack.1 = (f32[160,128]{1,0:T(8,128)S(1)}, f32[160,128]{1,0:T(8,128)S(1)}, bf16[48,128]{1,0:T(8,128)(2,1)S(1)}, bf16[48,128]{1,0:T(8,128)(2,1)S(1)}, f32[8,128]{...) custom-call(bf16[8,256]{1,0:T(8,128)(2,1)} %refs_0_.1, ...), custom_call_target="tpu_custom_call" | custom-call | tf_op jit(solution)/shard_map/pack/pallas_call | solution.py:826
  2.6 4.2 %collective-permute-start = (bf16[624,128]{1,0:T(8,128)(2,1)S(1)}, bf16[624,128]{1,0:T(8,128)(2,1)S(1)}, u32[]{:S(2)}, u32[]{:S(2)}) collective-permute-start(bf16[624,128]{1,0:T(8,128)(2,1)S(1)} %get-tuple-element.33), channel_id=1, source_target_pairs={{8,0},{9,1},{10,2},{11,3},{12,4},{13,5},{14,6},{15,7},{0,8},{1,9},... | collective-permute-start | bytes 479240 | tf_op jit(solution)/shard_map/ppermute | solution.py:863
  6.7 3.9 %all-to-all-start = ((bf16[16,16,128]{2,1,0:T(8,128)(2,1)}), bf16[16,16,128]{2,1,0:T(8,128)(2,1)S(1)}, u32[]{:S(2)}, u32[]{:S(2)}) async-start(bf16[16,16,128]{2,1,0:T(8,128)(2,1)} %bitcast.2), calls=%async_computation | async-start | bytes 131072 | tf_op jit(solution)/shard_map/all_to_all | solution.py:870
  10.6 0.4 %collective-permute-start.1 = (f32[160,128]{1,0:T(8,128)S(1)}, f32[160,128]{1,0:T(8,128)S(1)}, u32[]{:S(2)}, u32[]{:S(2)}) collective-permute-start(f32[160,128]{1,0:T(8,128)S(1)} %get-tuple-element.46), channel_id=1, source_target_pairs={{1,0},{0,1},{3,2},{2,3},{5,4},{4,5},{7,6},{6,7},{9,8},{8,9},{11,10... | collective-permute-start | bytes 245768 | tf_op jit(solution)/shard_map/ppermute | solution.py:863
  11.0 4.3 %collective-permute-start.2 = (f32[160,128]{1,0:T(8,128)S(1)}, f32[160,128]{1,0:T(8,128)S(1)}, u32[]{:S(2)}, u32[]{:S(2)}) collective-permute-start(f32[160,128]{1,0:T(8,128)S(1)} %get-tuple-element.47), channel_id=1, source_target_pairs={{15,0},{2,1},{1,2},{4,3},{3,4},{6,5},{5,6},{8,7},{7,8},{10,9},{9,1... | collective-permute-start | bytes 245768 | tf_op jit(solution)/shard_map/ppermute | solution.py:863
  15.4 0.0 collective-permute-start.3
  15.4 0.0 collective-permute-start.4
  15.4 0.0 collective-permute-done.refs_0_.refs_5_
  15.4 0.1 sides.1.refs_6_.refs_3_
  15.4 2.5 %all-to-all-done = bf16[16,16,128]{2,1,0:T(8,128)(2,1)S(1)} async-done(((bf16[16,16,128]{2,1,0:T(8,128)(2,1)}), bf16[16,16,128]{2,1,0:T(8,128)(2,1)S(1)}, u32[]{:S(2)}, u32[]{:S(2)}) %all-to-all-start) | async-done | bytes 65568 | tf_op jit(solution)/shard_map/all_to_all | solution.py:870
  18.0 0.7 %tiles.1 = (f32[3,4,32,128]{3,2,1,0:T(8,128)S(1)}, f32[8,32,128]{2,1,0:T(8,128)S(1)}, f32[6,256,128]{2,1,0:T(8,128)S(1)}) custom-call(f32[1,4,32,128]{3,2,1,0:T(8,128)S(1)} %get-tuple-element.35.refs_0_, f32[1,4,32,128]{3,2,1,0:T(8,128)S(1)} %get-tuple-element.36.refs_1_, f32[1,4,32,128]{3,2,1,0:T(8,128)S(1)} %get-tuple-element.37.refs_2_, ...), custom_call_target="tpu_custom_call" | custom-call | tf_op jit(solution)/shard_map/tiles/pallas_call | solution.py:881
  18.7 0.0 collective-permute-done.1.refs_9_
  18.7 0.0 collective-permute-done.2.refs_10_
  18.7 0.3 %first.1 = (f32[3,4,40,128]{3,2,1,0:T(8,128)S(1)}, f32[4,40,128]{2,1,0:T(8,128)S(1)}, f32[6,2,40,128]{3,2,1,0:T(8,128)S(1)}, f32[3,40,128]{2,1,0:T(8,128)S(1)}, ...) custom-call(f32[3,1,4,32,128]{4,3,2,1,0:T(8,128)S(1)} %get-tuple-element.42.refs_0_, ...), custom_call_target="tpu_custom_call" | custom-call | tf_op jit(solution)/shard_map/first/pallas_call | solution.py:899
  19.0 0.4 %collective-permute-done.3.refs_14_ = bf16[48,128]{1,0:T(8,128)(2,1)S(1)} collective-permute-done((bf16[48,128]{1,0:T(8,128)(2,1)S(1)}, bf16[48,128]{1,0:T(8,128)(2,1)S(1)}, u32[]{:S(2)}, u32[]{:S(2)}) %collective-permute-start.3) | collective-permute-done | bytes 12320 | tf_op jit(solution)/shard_map/ppermute | solution.py:863
  19.4 0.1 collective-permute-done.4.refs_15_
  19.5 1.5 %wave.1 = (f32[3,1,4,32,128]{4,3,2,1,0:T(8,128)}, f32[6,1,4,32,128]{4,3,2,1,0:T(8,128)}, f32[6,1,4,32,128]{4,3,2,1,0:T(8,128)}) custom-call(f32[6,1,4,32,128]{4,3,2,1,0:T(8,128)S(1)} %get-tuple-element.30.refs_2_.refs_0_, f32[1,4,32,128]{3,2,1,0:T(8,128)S(1)} %get-tuple-element.31.refs_3_.refs_1_, f32[1,4,32,128]{3,2,1,0:T(8,128)S(1)} %get-tuple-element.32.refs_4_.refs_2_, ...), custom_call_target="tpu_custom_call" | custom-call | tf_op jit(solution)/shard_map/wave/pallas_call | solution.py:916
Async XLA Ops:
  2.6 12.8 %collective-permute-start = (bf16[624,128]{1,0:T(8,128)(2,1)S(1)}, bf16[624,128]{1,0:T(8,128)(2,1)S(1)}, u32[]{:S(2)}, u32[]{:S(2)}) collective-permute-start(bf16[624,128]{1,0:T(8,128)(2,1)S(1)} %get-tuple-element.33), channel_id=1, source_target_pairs={{8,0},{9,1},{10,2},{11,3},{12,4},{13,5},{14,6},{15,7},{0,8},{1,9},... | collective-permute-start | bytes 479240 | tf_op jit(solution)/shard_map/ppermute | solution.py:863
  6.7 11.3 %all-to-all-start = ((bf16[16,16,128]{2,1,0:T(8,128)(2,1)}), bf16[16,16,128]{2,1,0:T(8,128)(2,1)S(1)}, u32[]{:S(2)}, u32[]{:S(2)}) async-start(bf16[16,16,128]{2,1,0:T(8,128)(2,1)} %bitcast.2), calls=%async_computation | async-start | bytes 131072 | tf_op jit(solution)/shard_map/all_to_all | solution.py:870
  10.6 8.1 %collective-permute-start.1 = (f32[160,128]{1,0:T(8,128)S(1)}, f32[160,128]{1,0:T(8,128)S(1)}, u32[]{:S(2)}, u32[]{:S(2)}) collective-permute-start(f32[160,128]{1,0:T(8,128)S(1)} %get-tuple-element.46), channel_id=1, source_target_pairs={{1,0},{0,1},{3,2},{2,3},{5,4},{4,5},{7,6},{6,7},{9,8},{8,9},{11,10... | collective-permute-start | bytes 245768 | tf_op jit(solution)/shard_map/ppermute | solution.py:863
  11.0 7.7 %collective-permute-start.2 = (f32[160,128]{1,0:T(8,128)S(1)}, f32[160,128]{1,0:T(8,128)S(1)}, u32[]{:S(2)}, u32[]{:S(2)}) collective-permute-start(f32[160,128]{1,0:T(8,128)S(1)} %get-tuple-element.47), channel_id=1, source_target_pairs={{15,0},{2,1},{1,2},{4,3},{3,4},{6,5},{5,6},{8,7},{7,8},{10,9},{9,1... | collective-permute-start | bytes 245768 | tf_op jit(solution)/shard_map/ppermute | solution.py:863
  15.4 4.0 %collective-permute-start.3 = (bf16[48,128]{1,0:T(8,128)(2,1)S(1)}, bf16[48,128]{1,0:T(8,128)(2,1)S(1)}, u32[]{:S(2)}, u32[]{:S(2)}) collective-permute-start(bf16[48,128]{1,0:T(8,128)(2,1)S(1)} %get-tuple-element.55), channel_id=1, source_target_pairs={{7,0},{10,1},{9,2},{12,3},{11,4},{14,5},{13,6},{0,7},{15,8},{2,9},... | collective-permute-start | bytes 36872 | tf_op jit(solution)/shard_map/ppermute | solution.py:863
  15.4 4.1 %collective-permute-start.4 = (bf16[48,128]{1,0:T(8,128)(2,1)S(1)}, bf16[48,128]{1,0:T(8,128)(2,1)S(1)}, u32[]{:S(2)}, u32[]{:S(2)}) collective-permute-start(bf16[48,128]{1,0:T(8,128)(2,1)S(1)} %get-tuple-element.56), channel_id=1, source_target_pairs={{9,0},{8,1},{11,2},{10,3},{13,4},{12,5},{15,6},{14,7},{1,8},{0,9},... | collective-permute-start | bytes 36872 | tf_op jit(solution)/shard_map/ppermute | solution.py:863

commit v6 on v5

--- a/solution.py
+++ b/solution.py
@@ -136,11 +136,8 @@
         for k in which:
             copies[k].wait()
 
-    arrive(0, 1, 2, 3)
+    arrive(0, 1, 2, 3, 6, 7, 14)
     route_tiles(n, near_lam, near_mu, near_bu, near_dest, routed, routed_out)
-    leave = pltpu.make_async_copy(routed_out, out_t, sems.at[15])
-    leave.start()
-    arrive(6, 7, 14)
     source[...] = place_sources(index, wave, 0)
     later[...] = place_sources(index, wave, 1)
 
@@ -258,13 +255,11 @@
     ends[ENDS_MAP : ENDS_MAP + last + 1, :] = owners[0 : last + 1]
     arrive(8)
     write(FIELDS, *range(STRESS, VEL), "gx", "gy", "gz")
-    arrive(10, 13, 11, 12)
-    write(*range(VEL, HELD), LAME, MU, BUOY)
-    arrive(4, 5)
+    leave = pltpu.make_async_copy(routed_out, out_t, sems.at[15])
+    leave.start()
+    arrive(10, 13, 11, 12, 4, 5, 9)
     for i in range(4):
         gain[i] = courant * (1.0 - (1.0 - dec[0, i]) * los[0, i])
-    write(GAIN)
-    arrive(9)
     for i in range(4):
         kept = courant * dec[0, i]
         for c in range(6):
@@ -272,7 +267,7 @@
             if c < 3:
                 value = value + source[i * ROWS : (i + 1) * ROWS, :]
             held[c, i] = value
-    write(*range(HELD, GAIN), "hy", "hz")
+    write(*range(VEL, FIELDS), "hy", "hz")
     below, above = corner[0:CORNER, :].astype(BF16), corner[CORNER : 2 * CORNER, :].astype(BF16)
     out_e[...] = jnp.where(even, below, above)
     out_d[...] = jnp.where(even, above, below)

time: 21.2 us -> 21.5 us (1.014)
  Pallas kernels: 4.49 us -> 4.76 us
    pallas_call x1, Pallas kernels: 1.92 us -> 2.18 us  [body(): pl.pallas_call(functools.partial(pack_kernel, n, tile_lambda.shape[0]), o...]
where the time goes in v6:
time: 21.5 us; the launch traced here: 21.2 us
  starting transfers between devices  12.8 us (60%)
  Pallas kernels  4.76 us (22%)
  waiting for transfers between devices  3.01 us (14%)
  between operations  0.69 us (3%)
    ppermute x5, starting transfers between devices, permute(): return lax.ppermute(array, 'gx', [(source_of(i), i) for i in range(n)])  8.86 us
    all_to_all x1, starting transfers between devices, body(): got_t = lax.all_to_all(out_t, 'gx', split_axis=0, concat_axis=0, tiled=True)  3.91 us
    all_to_all x1, waiting for transfers between devices, body(): got_t = lax.all_to_all(out_t, 'gx', split_axis=0, concat_axis=0, tiled=True)  2.54 us
    pallas_call x1, Pallas kernels, body(): pl.pallas_call(functools.partial(pack_kernel, n, tile_lambda.shape[0]), o...  2.18 us
    pallas_call x1, Pallas kernels, body(): pl.pallas_call(functools.partial(wave_kernel, n), out_shape=[jax.ShapeDty...  1.51 us
    pallas_call x1, Pallas kernels, body(): pl.pallas_call(functools.partial(tile_kernel, n), out_shape=[vmem(3, 4, R...  0.7 us
    ppermute x5, waiting for transfers between devices, permute(): return lax.ppermute(array, 'gx', [(source_of(i), i) for i in range(n)])  0.47 us
  transfers between devices with their start and end apart: 6, of which 3 were waited for; matrix products, arithmetic and copies ran while one was open for 0% of the time, Pallas kernels for 5%

profile of v6, /device:TPU:0, one launch (start us, length us, event | category | flops | bytes accessed | tf_op | source)
XLA Modules:
  0.0 21.2 jit_solution(7736152238500618257)
XLA Ops:
  0.6 2.2 %pack.1 = (f32[160,128]{1,0:T(8,128)S(1)}, f32[160,128]{1,0:T(8,128)S(1)}, bf16[48,128]{1,0:T(8,128)(2,1)S(1)}, bf16[48,128]{1,0:T(8,128)(2,1)S(1)}, f32[8,128]{...) custom-call(bf16[8,256]{1,0:T(8,128)(2,1)} %refs_0_.1, ...), custom_call_target="tpu_custom_call" | custom-call | tf_op jit(solution)/shard_map/pack/pallas_call | solution.py:821
  2.8 4.1 %collective-permute-start = (bf16[624,128]{1,0:T(8,128)(2,1)S(1)}, bf16[624,128]{1,0:T(8,128)(2,1)S(1)}, u32[]{:S(2)}, u32[]{:S(2)}) collective-permute-start(bf16[624,128]{1,0:T(8,128)(2,1)S(1)} %get-tuple-element.33), channel_id=1, source_target_pairs={{8,0},{9,1},{10,2},{11,3},{12,4},{13,5},{14,6},{15,7},{0,8},{1,9},... | collective-permute-start | bytes 479240 | tf_op jit(solution)/shard_map/ppermute | solution.py:858
  6.9 3.9 %all-to-all-start = ((bf16[16,16,128]{2,1,0:T(8,128)(2,1)}), bf16[16,16,128]{2,1,0:T(8,128)(2,1)S(1)}, u32[]{:S(2)}, u32[]{:S(2)}) async-start(bf16[16,16,128]{2,1,0:T(8,128)(2,1)} %bitcast.2), calls=%async_computation | async-start | bytes 131072 | tf_op jit(solution)/shard_map/all_to_all | solution.py:865
  10.9 0.4 %collective-permute-start.1 = (f32[160,128]{1,0:T(8,128)S(1)}, f32[160,128]{1,0:T(8,128)S(1)}, u32[]{:S(2)}, u32[]{:S(2)}) collective-permute-start(f32[160,128]{1,0:T(8,128)S(1)} %get-tuple-element.46), channel_id=1, source_target_pairs={{1,0},{0,1},{3,2},{2,3},{5,4},{4,5},{7,6},{6,7},{9,8},{8,9},{11,10... | collective-permute-start | bytes 245768 | tf_op jit(solution)/shard_map/ppermute | solution.py:858
  11.3 4.3 %collective-permute-start.2 = (f32[160,128]{1,0:T(8,128)S(1)}, f32[160,128]{1,0:T(8,128)S(1)}, u32[]{:S(2)}, u32[]{:S(2)}) collective-permute-start(f32[160,128]{1,0:T(8,128)S(1)} %get-tuple-element.47), channel_id=1, source_target_pairs={{15,0},{2,1},{1,2},{4,3},{3,4},{6,5},{5,6},{8,7},{7,8},{10,9},{9,1... | collective-permute-start | bytes 245768 | tf_op jit(solution)/shard_map/ppermute | solution.py:858
  15.6 0.0 collective-permute-start.3
  15.6 0.0 collective-permute-start.4
  15.6 0.0 collective-permute-done.refs_0_.refs_5_
  15.6 0.1 sides.1.refs_6_.refs_3_
  15.7 2.5 %all-to-all-done = bf16[16,16,128]{2,1,0:T(8,128)(2,1)S(1)} async-done(((bf16[16,16,128]{2,1,0:T(8,128)(2,1)}), bf16[16,16,128]{2,1,0:T(8,128)(2,1)S(1)}, u32[]{:S(2)}, u32[]{:S(2)}) %all-to-all-start) | async-done | bytes 65568 | tf_op jit(solution)/shard_map/all_to_all | solution.py:865
  18.2 0.7 %tiles.1 = (f32[3,4,32,128]{3,2,1,0:T(8,128)S(1)}, f32[8,32,128]{2,1,0:T(8,128)S(1)}, f32[6,256,128]{2,1,0:T(8,128)S(1)}) custom-call(f32[1,4,32,128]{3,2,1,0:T(8,128)S(1)} %get-tuple-element.35.refs_0_, f32[1,4,32,128]{3,2,1,0:T(8,128)S(1)} %get-tuple-element.36.refs_1_, f32[1,4,32,128]{3,2,1,0:T(8,128)S(1)} %get-tuple-element.37.refs_2_, ...), custom_call_target="tpu_custom_call" | custom-call | tf_op jit(solution)/shard_map/tiles/pallas_call | solution.py:876
  18.9 0.0 collective-permute-done.1.refs_9_
  18.9 0.0 collective-permute-done.2.refs_10_
  18.9 0.3 %first.1 = (f32[3,4,40,128]{3,2,1,0:T(8,128)S(1)}, f32[4,40,128]{2,1,0:T(8,128)S(1)}, f32[6,2,40,128]{3,2,1,0:T(8,128)S(1)}, f32[3,40,128]{2,1,0:T(8,128)S(1)}, ...) custom-call(f32[3,1,4,32,128]{4,3,2,1,0:T(8,128)S(1)} %get-tuple-element.42.refs_0_, ...), custom_call_target="tpu_custom_call" | custom-call | tf_op jit(solution)/shard_map/first/pallas_call | solution.py:894
  19.3 0.4 %collective-permute-done.3.refs_14_ = bf16[48,128]{1,0:T(8,128)(2,1)S(1)} collective-permute-done((bf16[48,128]{1,0:T(8,128)(2,1)S(1)}, bf16[48,128]{1,0:T(8,128)(2,1)S(1)}, u32[]{:S(2)}, u32[]{:S(2)}) %collective-permute-start.3) | collective-permute-done | bytes 12320 | tf_op jit(solution)/shard_map/ppermute | solution.py:858
  19.6 0.1 collective-permute-done.4.refs_15_
  19.7 1.5 %wave.1 = (f32[3,1,4,32,128]{4,3,2,1,0:T(8,128)}, f32[6,1,4,32,128]{4,3,2,1,0:T(8,128)}, f32[6,1,4,32,128]{4,3,2,1,0:T(8,128)}) custom-call(f32[6,1,4,32,128]{4,3,2,1,0:T(8,128)S(1)} %get-tuple-element.30.refs_2_.refs_0_, f32[1,4,32,128]{3,2,1,0:T(8,128)S(1)} %get-tuple-element.31.refs_3_.refs_1_, f32[1,4,32,128]{3,2,1,0:T(8,128)S(1)} %get-tuple-element.32.refs_4_.refs_2_, ...), custom_call_target="tpu_custom_call" | custom-call | tf_op jit(solution)/shard_map/wave/pallas_call | solution.py:911
Async XLA Ops:
  2.8 12.8 %collective-permute-start = (bf16[624,128]{1,0:T(8,128)(2,1)S(1)}, bf16[624,128]{1,0:T(8,128)(2,1)S(1)}, u32[]{:S(2)}, u32[]{:S(2)}) collective-permute-start(bf16[624,128]{1,0:T(8,128)(2,1)S(1)} %get-tuple-element.33), channel_id=1, source_target_pairs={{8,0},{9,1},{10,2},{11,3},{12,4},{13,5},{14,6},{15,7},{0,8},{1,9},... | collective-permute-start | bytes 479240 | tf_op jit(solution)/shard_map/ppermute | solution.py:858
  6.9 11.3 %all-to-all-start = ((bf16[16,16,128]{2,1,0:T(8,128)(2,1)}), bf16[16,16,128]{2,1,0:T(8,128)(2,1)S(1)}, u32[]{:S(2)}, u32[]{:S(2)}) async-start(bf16[16,16,128]{2,1,0:T(8,128)(2,1)} %bitcast.2), calls=%async_computation | async-start | bytes 131072 | tf_op jit(solution)/shard_map/all_to_all | solution.py:865
  10.9 8.1 %collective-permute-start.1 = (f32[160,128]{1,0:T(8,128)S(1)}, f32[160,128]{1,0:T(8,128)S(1)}, u32[]{:S(2)}, u32[]{:S(2)}) collective-permute-start(f32[160,128]{1,0:T(8,128)S(1)} %get-tuple-element.46), channel_id=1, source_target_pairs={{1,0},{0,1},{3,2},{2,3},{5,4},{4,5},{7,6},{6,7},{9,8},{8,9},{11,10... | collective-permute-start | bytes 245768 | tf_op jit(solution)/shard_map/ppermute | solution.py:858
  11.3 7.7 %collective-permute-start.2 = (f32[160,128]{1,0:T(8,128)S(1)}, f32[160,128]{1,0:T(8,128)S(1)}, u32[]{:S(2)}, u32[]{:S(2)}) collective-permute-start(f32[160,128]{1,0:T(8,128)S(1)} %get-tuple-element.47), channel_id=1, source_target_pairs={{15,0},{2,1},{1,2},{4,3},{3,4},{6,5},{5,6},{8,7},{7,8},{10,9},{9,1... | collective-permute-start | bytes 245768 | tf_op jit(solution)/shard_map/ppermute | solution.py:858
  15.6 4.0 %collective-permute-start.3 = (bf16[48,128]{1,0:T(8,128)(2,1)S(1)}, bf16[48,128]{1,0:T(8,128)(2,1)S(1)}, u32[]{:S(2)}, u32[]{:S(2)}) collective-permute-start(bf16[48,128]{1,0:T(8,128)(2,1)S(1)} %get-tuple-element.55), channel_id=1, source_target_pairs={{7,0},{10,1},{9,2},{12,3},{11,4},{14,5},{13,6},{0,7},{15,8},{2,9},... | collective-permute-start | bytes 36872 | tf_op jit(solution)/shard_map/ppermute | solution.py:858
  15.6 4.1 %collective-permute-start.4 = (bf16[48,128]{1,0:T(8,128)(2,1)S(1)}, bf16[48,128]{1,0:T(8,128)(2,1)S(1)}, u32[]{:S(2)}, u32[]{:S(2)}) collective-permute-start(bf16[48,128]{1,0:T(8,128)(2,1)S(1)} %get-tuple-element.56), channel_id=1, source_target_pairs={{9,0},{8,1},{11,2},{10,3},{13,4},{12,5},{15,6},{14,7},{1,8},{0,9},... | collective-permute-start | bytes 36872 | tf_op jit(solution)/shard_map/ppermute | solution.py:858

commit v7 on v5

--- a/solution.py
+++ b/solution.py
@@ -305,10 +305,16 @@
         brick = jnp.where(row // n == k, brick + off % n, brick)
     brick = jnp.where(brick >= n, brick - n, brick)
     route = (brick == stored).astype(BF16)
-    cell, spot = sublane((2 * LANES, LANES)), lane((2 * LANES, LANES))
-    half = lax.rem(spot, 64)
-    cells = half // 16 * 64 + lax.rem(half, 16)
-    ends = (cell == cells + jnp.where(spot < 64, 0, 48)).astype(BF16)
+    part = lane((per, LANES)) // 16
+
+    def outer_cells(tile):
+        x, y = tile[:, :LANES], tile[:, LANES:]
+        moves = ((x, 0), (x, -48), (y, 32), (y, -16), (x, 16), (x, -32), (y, 48), (y, 0))
+        out = x
+        for k, (half, by) in enumerate(moves[1:], 1):
+            out = jnp.where(part == k, roll(half, by, 1), out)
+        return out
+
     left = lane((n, LANES)) < 64
     if chunk > 9 + 7 * len(sides_of(n)):
         rows[...] = jnp.zeros_like(rows)
@@ -317,12 +323,9 @@
         rows[pl.ds(j, n, stride=chunk), :] = value
 
     tiles = [near[...] for near in (near_lam, near_mu, near_bu)]
-    stacked = jnp.concatenate([tile.astype(F32) for tile in tiles], 0).astype(BF16)
-    halves = jnp.dot(stacked, ends, preferred_element_type=F32)
     for p, tile in enumerate(tiles):
         whole = jnp.dot(route, tile, preferred_element_type=F32)
-        outer = halves[p * per : (p + 1) * per].astype(BF16)
-        outer = jnp.dot(route, outer, preferred_element_type=F32)
+        outer = jnp.dot(route, outer_cells(tile.astype(F32)).astype(BF16), preferred_element_type=F32)
 
         def slot(x, k):
             return x[k * n : (k + 1) * n]

time: 21.2 us -> 21.2 us (level)
  no operation moved by 1% of the time
where the time goes in v7:
time: 21.2 us; the launch traced here: 20.9 us
  starting transfers between devices  12.8 us (60%)
  Pallas kernels  4.44 us (21%)
  waiting for transfers between devices  3.01 us (14%)
  between operations  0.69 us (3%)
    ppermute x5, starting transfers between devices, permute(): return lax.ppermute(array, 'gx', [(source_of(i), i) for i in range(n)])  8.9 us
    all_to_all x1, starting transfers between devices, body(): got_t = lax.all_to_all(out_t, 'gx', split_axis=0, concat_axis=0, tiled=True)  3.91 us
    all_to_all x1, waiting for transfers between devices, body(): got_t = lax.all_to_all(out_t, 'gx', split_axis=0, concat_axis=0, tiled=True)  2.54 us
    pallas_call x1, Pallas kernels, body(): pl.pallas_call(functools.partial(pack_kernel, n, tile_lambda.shape[0]), o...  1.86 us
    pallas_call x1, Pallas kernels, body(): pl.pallas_call(functools.partial(wave_kernel, n), out_shape=[jax.ShapeDty...  1.51 us
    pallas_call x1, Pallas kernels, body(): pl.pallas_call(functools.partial(tile_kernel, n), out_shape=[vmem(3, 4, R...  0.7 us
    ppermute x5, waiting for transfers between devices, permute(): return lax.ppermute(array, 'gx', [(source_of(i), i) for i in range(n)])  0.47 us
  transfers between devices with their start and end apart: 6, of which 3 were waited for; matrix products, arithmetic and copies ran while one was open for 0% of the time, Pallas kernels for 5%

profile of v7, /device:TPU:0, one launch (start us, length us, event | category | flops | bytes accessed | tf_op | source)
XLA Modules:
  0.0 20.9 jit_solution(12580805565552523827)
XLA Ops:
  0.6 1.9 %pack.1 = (f32[160,128]{1,0:T(8,128)S(1)}, f32[160,128]{1,0:T(8,128)S(1)}, bf16[48,128]{1,0:T(8,128)(2,1)S(1)}, bf16[48,128]{1,0:T(8,128)(2,1)S(1)}, f32[8,128]{...) custom-call(bf16[8,256]{1,0:T(8,128)(2,1)} %refs_0_.1, ...), custom_call_target="tpu_custom_call" | custom-call | tf_op jit(solution)/shard_map/pack/pallas_call | solution.py:829
  2.5 4.1 %collective-permute-start = (bf16[624,128]{1,0:T(8,128)(2,1)S(1)}, bf16[624,128]{1,0:T(8,128)(2,1)S(1)}, u32[]{:S(2)}, u32[]{:S(2)}) collective-permute-start(bf16[624,128]{1,0:T(8,128)(2,1)S(1)} %get-tuple-element.33), channel_id=1, source_target_pairs={{8,0},{9,1},{10,2},{11,3},{12,4},{13,5},{14,6},{15,7},{0,8},{1,9},... | collective-permute-start | bytes 479240 | tf_op jit(solution)/shard_map/ppermute | solution.py:866
  6.7 3.9 %all-to-all-start = ((bf16[16,16,128]{2,1,0:T(8,128)(2,1)}), bf16[16,16,128]{2,1,0:T(8,128)(2,1)S(1)}, u32[]{:S(2)}, u32[]{:S(2)}) async-start(bf16[16,16,128]{2,1,0:T(8,128)(2,1)} %bitcast.2), calls=%async_computation | async-start | bytes 131072 | tf_op jit(solution)/shard_map/all_to_all | solution.py:873
  10.6 0.4 %collective-permute-start.1 = (f32[160,128]{1,0:T(8,128)S(1)}, f32[160,128]{1,0:T(8,128)S(1)}, u32[]{:S(2)}, u32[]{:S(2)}) collective-permute-start(f32[160,128]{1,0:T(8,128)S(1)} %get-tuple-element.46), channel_id=1, source_target_pairs={{1,0},{0,1},{3,2},{2,3},{5,4},{4,5},{7,6},{6,7},{9,8},{8,9},{11,10... | collective-permute-start | bytes 245768 | tf_op jit(solution)/shard_map/ppermute | solution.py:866
  11.0 4.3 %collective-permute-start.2 = (f32[160,128]{1,0:T(8,128)S(1)}, f32[160,128]{1,0:T(8,128)S(1)}, u32[]{:S(2)}, u32[]{:S(2)}) collective-permute-start(f32[160,128]{1,0:T(8,128)S(1)} %get-tuple-element.47), channel_id=1, source_target_pairs={{15,0},{2,1},{1,2},{4,3},{3,4},{6,5},{5,6},{8,7},{7,8},{10,9},{9,1... | collective-permute-start | bytes 245768 | tf_op jit(solution)/shard_map/ppermute | solution.py:866
  15.3 0.0 collective-permute-start.3
  15.3 0.0 collective-permute-start.4
  15.3 0.0 collective-permute-done.refs_0_.refs_5_
  15.3 0.1 sides.1.refs_6_.refs_3_
  15.4 2.5 %all-to-all-done = bf16[16,16,128]{2,1,0:T(8,128)(2,1)S(1)} async-done(((bf16[16,16,128]{2,1,0:T(8,128)(2,1)}), bf16[16,16,128]{2,1,0:T(8,128)(2,1)S(1)}, u32[]{:S(2)}, u32[]{:S(2)}) %all-to-all-start) | async-done | bytes 65568 | tf_op jit(solution)/shard_map/all_to_all | solution.py:873
  17.9 0.7 %tiles.1 = (f32[3,4,32,128]{3,2,1,0:T(8,128)S(1)}, f32[8,32,128]{2,1,0:T(8,128)S(1)}, f32[6,256,128]{2,1,0:T(8,128)S(1)}) custom-call(f32[1,4,32,128]{3,2,1,0:T(8,128)S(1)} %get-tuple-element.35.refs_0_, f32[1,4,32,128]{3,2,1,0:T(8,128)S(1)} %get-tuple-element.36.refs_1_, f32[1,4,32,128]{3,2,1,0:T(8,128)S(1)} %get-tuple-element.37.refs_2_, ...), custom_call_target="tpu_custom_call" | custom-call | tf_op jit(solution)/shard_map/tiles/pallas_call | solution.py:884
  18.6 0.0 collective-permute-done.1.refs_9_
  18.6 0.0 collective-permute-done.2.refs_10_
  18.7 0.3 %first.1 = (f32[3,4,40,128]{3,2,1,0:T(8,128)S(1)}, f32[4,40,128]{2,1,0:T(8,128)S(1)}, f32[6,2,40,128]{3,2,1,0:T(8,128)S(1)}, f32[3,40,128]{2,1,0:T(8,128)S(1)}, ...) custom-call(f32[3,1,4,32,128]{4,3,2,1,0:T(8,128)S(1)} %get-tuple-element.42.refs_0_, ...), custom_call_target="tpu_custom_call" | custom-call | tf_op jit(solution)/shard_map/first/pallas_call | solution.py:902
  19.0 0.4 %collective-permute-done.3.refs_14_ = bf16[48,128]{1,0:T(8,128)(2,1)S(1)} collective-permute-done((bf16[48,128]{1,0:T(8,128)(2,1)S(1)}, bf16[48,128]{1,0:T(8,128)(2,1)S(1)}, u32[]{:S(2)}, u32[]{:S(2)}) %collective-permute-start.3) | collective-permute-done | bytes 12320 | tf_op jit(solution)/shard_map/ppermute | solution.py:866
  19.3 0.1 collective-permute-done.4.refs_15_
  19.4 1.5 %wave.1 = (f32[3,1,4,32,128]{4,3,2,1,0:T(8,128)}, f32[6,1,4,32,128]{4,3,2,1,0:T(8,128)}, f32[6,1,4,32,128]{4,3,2,1,0:T(8,128)}) custom-call(f32[6,1,4,32,128]{4,3,2,1,0:T(8,128)S(1)} %get-tuple-element.30.refs_2_.refs_0_, f32[1,4,32,128]{3,2,1,0:T(8,128)S(1)} %get-tuple-element.31.refs_3_.refs_1_, f32[1,4,32,128]{3,2,1,0:T(8,128)S(1)} %get-tuple-element.32.refs_4_.refs_2_, ...), custom_call_target="tpu_custom_call" | custom-call | tf_op jit(solution)/shard_map/wave/pallas_call | solution.py:919
Async XLA Ops:
  2.5 12.8 %collective-permute-start = (bf16[624,128]{1,0:T(8,128)(2,1)S(1)}, bf16[624,128]{1,0:T(8,128)(2,1)S(1)}, u32[]{:S(2)}, u32[]{:S(2)}) collective-permute-start(bf16[624,128]{1,0:T(8,128)(2,1)S(1)} %get-tuple-element.33), channel_id=1, source_target_pairs={{8,0},{9,1},{10,2},{11,3},{12,4},{13,5},{14,6},{15,7},{0,8},{1,9},... | collective-permute-start | bytes 479240 | tf_op jit(solution)/shard_map/ppermute | solution.py:866
  6.7 11.3 %all-to-all-start = ((bf16[16,16,128]{2,1,0:T(8,128)(2,1)}), bf16[16,16,128]{2,1,0:T(8,128)(2,1)S(1)}, u32[]{:S(2)}, u32[]{:S(2)}) async-start(bf16[16,16,128]{2,1,0:T(8,128)(2,1)} %bitcast.2), calls=%async_computation | async-start | bytes 131072 | tf_op jit(solution)/shard_map/all_to_all | solution.py:873
  10.6 8.1 %collective-permute-start.1 = (f32[160,128]{1,0:T(8,128)S(1)}, f32[160,128]{1,0:T(8,128)S(1)}, u32[]{:S(2)}, u32[]{:S(2)}) collective-permute-start(f32[160,128]{1,0:T(8,128)S(1)} %get-tuple-element.46), channel_id=1, source_target_pairs={{1,0},{0,1},{3,2},{2,3},{5,4},{4,5},{7,6},{6,7},{9,8},{8,9},{11,10... | collective-permute-start | bytes 245768 | tf_op jit(solution)/shard_map/ppermute | solution.py:866
  11.0 7.7 %collective-permute-start.2 = (f32[160,128]{1,0:T(8,128)S(1)}, f32[160,128]{1,0:T(8,128)S(1)}, u32[]{:S(2)}, u32[]{:S(2)}) collective-permute-start(f32[160,128]{1,0:T(8,128)S(1)} %get-tuple-element.47), channel_id=1, source_target_pairs={{15,0},{2,1},{1,2},{4,3},{3,4},{6,5},{5,6},{8,7},{7,8},{10,9},{9,1... | collective-permute-start | bytes 245768 | tf_op jit(solution)/shard_map/ppermute | solution.py:866
  15.3 4.0 %collective-permute-start.3 = (bf16[48,128]{1,0:T(8,128)(2,1)S(1)}, bf16[48,128]{1,0:T(8,128)(2,1)S(1)}, u32[]{:S(2)}, u32[]{:S(2)}) collective-permute-start(bf16[48,128]{1,0:T(8,128)(2,1)S(1)} %get-tuple-element.55), channel_id=1, source_target_pairs={{7,0},{10,1},{9,2},{12,3},{11,4},{14,5},{13,6},{0,7},{15,8},{2,9},... | collective-permute-start | bytes 36872 | tf_op jit(solution)/shard_map/ppermute | solution.py:866
  15.3 4.1 %collective-permute-start.4 = (bf16[48,128]{1,0:T(8,128)(2,1)S(1)}, bf16[48,128]{1,0:T(8,128)(2,1)S(1)}, u32[]{:S(2)}, u32[]{:S(2)}) collective-permute-start(bf16[48,128]{1,0:T(8,128)(2,1)S(1)} %get-tuple-element.56), channel_id=1, source_target_pairs={{9,0},{8,1},{11,2},{10,3},{13,4},{12,5},{15,6},{14,7},{1,8},{0,9},... | collective-permute-start | bytes 36872 | tf_op jit(solution)/shard_map/ppermute | solution.py:866
